TPU v7x, 32 devices: a whole 2x2x4 slice. The times are simulated.
32 devices in a mesh: blk: 8 (over z, y), tower: 4 (over x, core).
Axes of the slice: x: 2, y: 2, z: 4, core: 2. Of those that a mesh axis runs over, the one named last changes fastest.
Arguments:
- layer_input: bfloat16 [16384, 1152], P(('blk', 'tower')), may hold values from -8 to 8
- caption_ids: int32 [64, 64], P('blk'), may hold values from 0 to 31999, as said below
- positives: int32 [48], P('blk'), may hold values from 0 to 63, as said below
- ln_gain: float32 [2, 1152], replicated, may hold values from 0.1 to 1.9
- w_first: bfloat16 [2, 1152, 2176], P(None, None, 'blk'), may hold values from -0.1875 to 0.1875
- w_second: bfloat16 [2, 2176, 1152], P(None, 'blk'), may hold values from -0.125 to 0.125
- logit_scale: float32 [1], replicated, may hold values from 20 to 80
- logit_bias: float32 [1], replicated, may hold values from -6 to -2
Outputs:
- input_grad: float32 [16384, 1152], P(('blk', 'tower'))
Inputs may be any that keep to these rules, and one draw needn't show every extreme that they name: `caption_ids`: each caption's ids are nonzero for its first 32 or more positions and zero after; some caption has no zeros. `positives`: no two images have the same positive caption.
All inputs are finite; a program needn't handle non-finite values.
Results may differ from a plain program's by a relative error of at most 0.013.
Values may be sent and summed in bfloat16 or wider, within the bound.
No kernel may reach another device: no remote copies, remote signals or barrier semaphores. Data moves between devices by JAX's collectives and lax.ppermute only.
A program may use at most 128 MiB of HBM per device.

v0:
```python
import jax
import jax.numpy as jnp
from jax import lax
from jax.sharding import PartitionSpec as P

PATCHES = 256
TEXT_LEN = 64


norm_eps = 1e-06
loss_scale = 128.0
gelu_coeff = 0.7978845608028654


def broadcast(value, axis, source):
    kept = jnp.where(lax.axis_index(axis) == source, value, 0).astype(value.dtype)
    return lax.psum(kept, axis)


def gelu_pair(pre):
    inner = gelu_coeff * (pre + 0.044715 * pre * pre * pre)
    tanh_part = jnp.tanh(inner)
    value = 0.5 * pre * (1.0 + tanh_part)
    slope = 0.5 * (1.0 + tanh_part) + 0.5 * pre * (1.0 - tanh_part * tanh_part) * gelu_coeff * (
        1.0 + 3.0 * 0.044715 * pre * pre
    )
    return (value, slope)


def contract_last(left, right):
    return lax.dot_general(
        left, right, (((1,), (1,)), ((), ())), preferred_element_type=jnp.float32
    )


def contract_first(left, right):
    return lax.dot_general(
        left, right, (((0,), (0,)), ((), ())), preferred_element_type=jnp.float32
    )


def unit_rows(pooled):
    norm = jnp.sqrt(jnp.sum(pooled * pooled, axis=-1, keepdims=True) + norm_eps)
    return (pooled / norm, norm)


def unit_back(unit, norm, grad_emb):
    return (grad_emb - unit * jnp.sum(unit * grad_emb, axis=-1, keepdims=True)) / norm


def body(layer_input, caption_ids, positives, ln_gain, w_first, w_second, logit_scale, logit_bias):
    groups = lax.axis_size("tower")
    tower_index = lax.axis_index("tower")
    is_text = tower_index == groups - 1
    image_weight = jnp.where(is_text, 0.0, 1.0).astype(jnp.float32)
    row_count, width = layer_input.shape
    cap_count = caption_ids.shape[0]
    img_count = positives.shape[0] // (groups - 1)
    gain = jnp.where(is_text, ln_gain[1], ln_gain[0])
    first = jnp.where(is_text, w_first[1], w_first[0])
    second = jnp.where(is_text, w_second[1], w_second[0])
    values = layer_input.astype(jnp.float32)
    centered = values - jnp.mean(values, axis=-1, keepdims=True)
    variance = jnp.mean(centered * centered, axis=-1, keepdims=True)
    inv_std = lax.rsqrt(variance + norm_eps)
    standard = centered * inv_std
    normed = (standard * gain).astype(jnp.bfloat16)
    pre = jnp.dot(
        normed, lax.all_gather(first, "blk", axis=1, tiled=True), preferred_element_type=jnp.float32
    )
    value, slope = gelu_pair(pre)
    hidden = value.astype(jnp.bfloat16)
    columns = hidden
    block_out = values + jnp.dot(
        columns,
        lax.all_gather(second, "blk", axis=0, tiled=True),
        preferred_element_type=jnp.float32,
    )
    image_pool = jnp.mean(block_out.reshape(img_count, PATCHES, width), axis=1)
    mask = (caption_ids != 0).astype(jnp.float32)
    counts = jnp.sum(mask, axis=1, keepdims=True)
    text_pool = (
        jnp.sum(block_out.reshape(cap_count, TEXT_LEN, width) * mask[:, :, None], axis=1) / counts
    )
    image_unit, image_norm = unit_rows(image_pool)
    text_unit, text_norm = unit_rows(text_pool)
    image_emb = image_unit.astype(jnp.bfloat16)
    text_emb = text_unit.astype(jnp.bfloat16)
    span = broadcast(text_emb, "tower", groups - 1)
    slot = jnp.minimum(tower_index, groups - 2) * img_count
    own_positive = lax.dynamic_slice_in_dim(positives, slot, img_count, 0)
    scale = logit_scale[0]
    bias = logit_bias[0]
    every = lax.all_gather(span, "blk", axis=0, tiled=True)
    logits = scale * contract_last(image_emb, every) + bias
    caption_index = jnp.arange(every.shape[0], dtype=jnp.int32)
    onehot = (own_positive[:, None] == caption_index[None, :]).astype(jnp.float32)
    coef = (loss_scale * (jax.nn.sigmoid(logits) - onehot) * image_weight).astype(jnp.bfloat16)
    grad_image = scale * jnp.dot(coef, every, preferred_element_type=jnp.float32)
    span_grad = lax.psum_scatter(
        scale * contract_first(coef, image_emb), "blk", scatter_dimension=0, tiled=True
    )
    grad_text = lax.psum(span_grad.astype(jnp.bfloat16), "tower").astype(jnp.float32)
    image_gp = unit_back(image_unit, image_norm, grad_image)
    text_gp = unit_back(text_unit, text_norm, grad_text)
    image_rows = jnp.broadcast_to(
        image_gp[:, None, :] / PATCHES, (img_count, PATCHES, width)
    ).reshape(row_count, width)
    text_rows = (text_gp[:, None, :] * (mask / counts)[:, :, None]).reshape(row_count, width)
    grad_out = jnp.where(is_text, text_rows, image_rows)
    grad_rows = grad_out.astype(jnp.bfloat16)
    grad_hidden = contract_last(grad_rows, lax.all_gather(second, "blk", axis=0, tiled=True))
    grad_pre = (grad_hidden * slope).astype(jnp.bfloat16)
    columns = grad_pre
    grad_normed = contract_last(columns, lax.all_gather(first, "blk", axis=1, tiled=True))
    grad_std = grad_normed * gain
    first_mean = jnp.mean(grad_std, axis=-1, keepdims=True)
    second_mean = jnp.mean(grad_std * standard, axis=-1, keepdims=True)
    return grad_out + inv_std * (grad_std - first_mean - standard * second_mean)


def solution(mesh):
    placed = (
        P(("blk", "tower"), None),
        P("blk", None),
        P("blk"),
        P(),
        P(None, None, "blk"),
        P(None, "blk", None),
        P(),
        P(),
    )
    return jax.shard_map(
        body, mesh=mesh, in_specs=placed, out_specs=P(("blk", "tower"), None), check_vma=False
    )
```

profile of v0, /device:TPU:0, one launch (start us, length us, event | category | flops | bytes accessed | tf_op | source)
XLA Modules:
  0.0 303.5 jit_solution(2191321576698492670)
XLA Ops:
  6.6 2.3 slice_select_fusion.1
  9.0 0.9 slice_select_fusion
  11.5 0.6 dynamic-slice
  12.9 0.2 convert_reduce_fusion
  13.1 0.5 fusion.30
  13.6 82.1 %all-gather.5.cloned.1.call-done = bf16[1,1152,2176]{1,2,0:T(8,128)(2,1)} async-done(((bf16[1,1152,272]{1,2,0:T(8,128)(2,1)}), bf16[1,1152,2176]{1,2,0:T(8,128)(2,1)}) %all-gather.5.cloned.1.call-update) | async-done | bytes 5013520 | tf_op jit(solution)/shard_map/all_gather | solution.py:69
  95.8 7.6 %fusion.5 = f32[512,2176]{1,0:T(8,128)} fusion(bf16[1,1152,2176]{1,2,0:T(8,128)(2,1)} %all-gather.5.cloned.1.call-done, bf16[512,1152]{1,0:T(8,128)(2,1)S(1)} %copy-done, f32[1152]{0:T(1024)S(1)} %fusion.52, f32[512]{0:T(512)S(1)} %add_rsqrt_fusion, f32[512]{0:T(512)S(1)} %broadcast_multiply_fusion.2), kind=kOutput, calls=%fused_computation.8 | convolution fusion | flops 2569863168 | bytes 10658304 | tf_op jit(solution)/shard_map/dot_general | solution.py:68
  103.4 76.2 %all-gather.7.cloned.1.call-done = bf16[1,2176,1152]{2,1,0:T(8,128)(2,1)} async-done(((bf16[1,272,1152]{2,1,0:T(8,128)(2,1)}), bf16[1,2176,1152]{2,1,0:T(8,128)(2,1)}) %all-gather.7.cloned.1.call-update) | async-done | bytes 5013520 | tf_op jit(solution)/shard_map/all_gather | solution.py:76
  179.6 6.7 %multiply_reduce_fusion = (f32[8,1152]{1,0:T(8,128)S(1)}, f32[512,1152]{1,0:T(8,128)S(1)}) fusion(f32[8,64]{1,0:T(8,128)S(1)} %compare_convert_fusion, bf16[1,2176,1152]{2,1,0:T(8,128)(2,1)} %all-gather.7.cloned.1.call-done, f32[512,2176]{1,0:T(8,128)} %fusion.5, bf16[512,1152]{1,0:T(8,128)(2,1)S(1)} %copy-done), kind=kOutput, calls=%fused_computation.37 | convolution fusion | flops 2579291136 | bytes 13047808 | tf_op jit(solution)/shard_map/dot_general | solution.py:74
  186.3 0.1 bitcast_reduce_fusion
  186.6 0.2 multiply_reduce_fusion.1
  186.9 10.3 %psum.14 = bf16[8,1152]{1,0:T(8,128)(2,1)S(1)} all-reduce(bf16[8,1152]{1,0:T(8,128)(2,1)S(1)} %convert_select_fusion), channel_id=1, replica_groups=mesh['blk'=8,'tower'=4] {'tower'}, use_global_device_ids=true, to_apply=%region_7.8 | all-reduce | flops 9216 | bytes 36864 | tf_op jit(solution)/shard_map/psum | solution.py:17
  197.2 30.6 %all_gather.13 = bf16[64,1152]{1,0:T(8,128)(2,1)S(1)} all-gather(bf16[8,1152]{1,0:T(8,128)(2,1)S(1)} %psum.14), channel_id=1, replica_groups=mesh['blk'=8,'tower'=4] {'blk'}, dimensions={0}, use_global_device_ids=true | all-gather | bytes 165888 | tf_op jit(solution)/shard_map/all_gather | solution.py:94
  227.8 0.2 fusion.49
  228.0 0.3 multiply_reduce_fusion.2
  228.3 0.3 convolution_multiply_fusion.1
  228.5 38.8 %all-reduce.2 = bf16[64,1152]{1,0:T(8,128)(2,1)S(1)} all-reduce(f32[64,1152]{1,0:T(8,128)S(1)} %convolution_multiply_fusion.1), channel_id=4, replica_groups=mesh['blk'=8,'tower'=4] {'blk'}, use_global_device_ids=true, to_apply=%region_8.9.clone | all-reduce | flops 73728 | bytes 442368
  267.3 10.4 %psum.15 = bf16[8,1152]{1,0:T(8,128)(2,1)S(1)} all-reduce(bf16[8,1152]{1,0:T(8,128)(2,1)S(1)} %dynamic-slice_convert_fusion), channel_id=1, replica_groups=mesh['blk'=8,'tower'=4] {'tower'}, use_global_device_ids=true, to_apply=%region_9.10 | all-reduce | flops 9216 | bytes 36864 | tf_op jit(solution)/shard_map/psum | solution.py:103
  277.8 0.2 fusion.50
  278.1 0.6 copy-done.2
  278.8 1.3 fusion.31
  280.0 12.9 %fusion.66 = (f32[512]{0:T(512)}, f32[512]{0:T(512)}, f32[512,1152]{1,0:T(8,128)S(1)}) fusion(f32[512]{0:T(512)} %copy-done.6, f32[512]{0:T(512)} %copy-done.4, bf16[512,1152]{1,0:T(8,128)(2,1)S(1)} %copy-done, f32[1152]{0:T(1024)} %copy-done.7, bf16[1,1152,2176]{1,2,0:T(8,128)(2,1)} %all-gather.5.cloned.1.call-done, bf16[512,1152]{1,0:T(8,128)(2,1)} %fusion.31, ...), kind=kOutput, calls=%fused_computation.93 | convolution fusion | flops 5159123968 | bytes 19214848 | tf_op jit(solution)/shard_map/dot_general | solution.py:31
  292.9 0.7 broadcast_multiply_fusion
  293.6 3.0 fusion.29
  (38 shorter events, 0.9 us)
Async XLA Ops:
  6.5 2.4 copy-start.1
  6.5 89.2 %all-gather.5.cloned.1.call-start = ((), (), s32[]{:S(2)}) async-start(), calls=%async_computation | async-start | bytes 5640192 | tf_op jit(solution)/shard_map/all_gather | solution.py:69
  6.5 4.7 %copy-start.3 = (s32[8,64]{1,0:T(8,128)S(1)}, s32[8,64]{1,0:T(8,128)}, u32[]{:S(2)}) copy-start(s32[8,64]{1,0:T(8,128)} %param.9) | copy-start | bytes 6148
  6.5 5.0 %copy-start.9 = (u32[32]{0:T(128)S(1)}, u32[32]{0:T(128)}, u32[]{:S(2)}) copy-start(u32[32]{0:T(128)} %constant.49) | copy-start | bytes 388
  6.5 6.2 %copy-start.8 = (s32[6]{0:T(128)S(1)}, s32[6]{0:T(128)}, u32[]{:S(2)}) copy-start(s32[6]{0:T(128)} %param.10) | copy-start | bytes 76
  6.5 6.3 %copy-start.5 = (f32[2,1152]{1,0:T(2,128)S(1)}, f32[2,1152]{1,0:T(2,128)}, u32[]{:S(2)}) copy-start(f32[2,1152]{1,0:T(2,128)} %param.11) | copy-start | bytes 27652
  6.6 6.3 %copy-start = (bf16[512,1152]{1,0:T(8,128)(2,1)S(1)}, bf16[512,1152]{1,0:T(8,128)(2,1)}, u32[]{:S(2)}) copy-start(bf16[512,1152]{1,0:T(8,128)(2,1)} %param.8) | copy-start | bytes 3538948
  8.9 170.7 %all-gather.7.cloned.1.call-start = ((), (), s32[]{:S(2)}) async-start(), calls=%async_computation.1 | async-start | bytes 5640192 | tf_op jit(solution)/shard_map/all_gather | solution.py:76
  12.9 90.5 %copy-start.7 = (f32[1152]{0:T(1024)}, f32[1152]{0:T(1024)S(1)}, u32[]{:S(2)}) copy-start(f32[1152]{0:T(1024)S(1)} %fusion.52) | copy-start | bytes 13828
  13.1 90.2 %copy-start.4 = (f32[512]{0:T(512)}, f32[512]{0:T(512)S(1)}, u32[]{:S(2)}) copy-start(f32[512]{0:T(512)S(1)} %broadcast_multiply_fusion.2) | copy-start | bytes 6148
  13.6 89.8 %copy-start.6 = (f32[512]{0:T(512)}, f32[512]{0:T(512)S(1)}, u32[]{:S(2)}) copy-start(f32[512]{0:T(512)S(1)} %add_rsqrt_fusion) | copy-start | bytes 6148
  278.1 0.6 copy-start.2
Sparse Core Ops, SparseCore 0:
  9.5 86.1 all-gather.4
  97.9 81.6 all-gather.6
where the time goes:
time: 304 us; the launch traced here: 303 us
  waiting for transfers between devices  158 us (52%)
  blocking collectives  90.1 us (30%)
  matrix products  28 us (9%)
  between operations  15.5 us (5%)
  other arithmetic  10 us (3%)
    all_gather x1, waiting for transfers between devices, body(): lax.all_gather(first, 'blk', axis=1, tiled=True)  82.1 us
    all_gather x1, waiting for transfers between devices, body(): lax.all_gather(second, 'blk', axis=0, tiled=True)  76.2 us
    unnamed x1, blocking collectives  38.8 us
    all_gather x1, blocking collectives, body(): every = lax.all_gather(span, 'blk', axis=0, tiled=True)  30.6 us
    dot_general x2, matrix products, contract_last(): lax.dot_general(left, right, (((1,), (1,)), ((), ())), preferred_element_...  13.1 us
    psum x1, blocking collectives, body(): lax.psum(span_grad.astype(jnp.bfloat16), 'tower').astype(jnp.float32)  10.4 us
    psum x1, blocking collectives, broadcast(): return lax.psum(kept, axis)  10.3 us
    dot_general x1, matrix products, body(): jnp.dot(normed, lax.all_gather(first, 'blk', axis=1, tiled=True), preferr...  7.6 us
  transfers between devices with their start and end apart: 2, of which 2 were waited for; matrix products, arithmetic and copies ran while one was open for 3% of the time, Pallas kernels for 0%

commit v1 on v0

v1 whole, which is shorter than its diff:
```python
import functools

import jax
import jax.numpy as jnp
from jax import lax
from jax.experimental import pallas as pl
from jax.experimental.pallas import tpu as pltpu
from jax.sharding import PartitionSpec as P

PATCHES = 256
TEXT_LEN = 64

norm_eps = 1e-06
loss_scale = 128.0
gelu_coeff = 0.7978845608028654


def gelu_pair(pre):
    inner = gelu_coeff * (pre + 0.044715 * pre * pre * pre)
    tanh_part = jnp.tanh(inner)
    value = 0.5 * pre * (1.0 + tanh_part)
    slope = 0.5 * (1.0 + tanh_part) + 0.5 * pre * (1.0 - tanh_part * tanh_part) * gelu_coeff * (
        1.0 + 3.0 * 0.044715 * pre * pre
    )
    return (value, slope)


def contract_last(left, right):
    return lax.dot_general(
        left, right, (((1,), (1,)), ((), ())), preferred_element_type=jnp.float32
    )


def two_parts(value):
    high = value.astype(jnp.bfloat16)
    low = (value - high.astype(jnp.float32)).astype(jnp.bfloat16)
    return high, low


def ring_place(block):
    return block // 2 if block % 2 == 0 else 7 - block // 2


RING = sorted(range(8), key=ring_place)


def ring_gather(own, groups):
    def move(value, step):
        found = []
        for place in range(8):
            for t in range(groups):
                source = RING[place] * groups + t
                found.append((source, RING[(place + step) % 8] * groups + t))
        return lax.ppermute(value, ("blk", "tower"), found)

    pieces = [[None, None] for _ in range(8)]
    pieces[0] = own
    for k in range(1, 5):
        for step in (1, -1):
            for chunk in (0, 1):
                if k == 4 and chunk != (0 if step == 1 else 1):
                    continue
                held = pieces[(-step * (k - 1)) % 8][chunk]
                pieces[(-step * k) % 8][chunk] = move(held, step)
    return pieces


SMALL = 128
REST = 16


def groups_of(pieces):
    found = [([(0, 0), (0, 1)], [0])]
    for k in (1, 2, 3):
        found.append(([(8 - k, 0), (k, 0)], []))
        found.append(([(8 - k, 1), (k, 1)], [8 - k, k]))
    found.append(([(4, 0), (4, 1)], [4]))
    return [(parts, rest, [pieces[p][c] for p, c in parts]) for parts, rest in found]


def project(rest, normed, one, two):
    weights = [one[:SMALL], two[:SMALL]]
    if rest:
        weights += [ref[SMALL:] for ref in (one, two) if ref.shape[0] > SMALL]
    pre = contract_last(normed[...], jnp.concatenate(weights, axis=0))
    square = pre * pre
    tanh_part = jnp.tanh(pre * (gelu_coeff + (gelu_coeff * 0.044715) * square))
    return pre, square, tanh_part, 0.5 + 0.5 * tanh_part


def slope_of(pre, square, tanh_part, gate, mask):
    bend = (0.5 * gelu_coeff) + (0.5 * gelu_coeff * 3.0 * 0.044715) * square
    slope = gate + pre * (1.0 - tanh_part * tanh_part) * bend
    return (slope * mask[...]).astype(jnp.bfloat16)


def pool_of(member, pre, gate):
    hidden = (pre * gate).astype(jnp.bfloat16)
    return jnp.dot(member[...], hidden, preferred_element_type=jnp.float32)


def put_pool(held, block_of, parts, rest, pool):
    for k, (p, c) in enumerate(parts):
        held[block_of[p], :, c * SMALL : (c + 1) * SMALL] = pool[:, k * SMALL : (k + 1) * SMALL]
    for k, p in enumerate(rest):
        start = 2 * SMALL + k * REST
        held[block_of[p], :, 2 * SMALL :] = pool[:, start : start + REST]


def own_kernel(
    parts, rest, block_of, layer_input, share, member, mask, normed, one, two, slope_ref, held, value
):
    pre, square, tanh_part, gate = project(rest, normed, one, two)
    slope = slope_of(pre, square, tanh_part, gate, mask)
    slope_ref[:, : slope.shape[1]] = slope
    held[...] = jnp.zeros_like(held)
    put_pool(held, block_of, parts, rest, pool_of(member, pre, gate) * share[...])
    value[...] = jnp.dot(member[...], layer_input[...], preferred_element_type=jnp.float32)


def forward_kernel(
    parts, rest, block_of, before, share, member, mask, normed, one, two, slope_ref, held
):
    pre, square, tanh_part, gate = project(rest, normed, one, two)
    slope = slope_of(pre, square, tanh_part, gate, mask)
    slope_ref[:, : slope.shape[1]] = slope
    held[...] = before[...]
    put_pool(held, block_of, parts, rest, pool_of(member, pre, gate) * share[...])


def pool_kernel(parts, rest, block_of, before, share, member, normed, one, two, held):
    pre, _, _, gate = project(rest, normed, one, two)
    held[...] = before[...]
    put_pool(held, block_of, parts, rest, pool_of(member, pre, gate) * share[...])


def last_pool_kernel(rest, share, member, normed, one, two, pool_ref):
    pre, _, _, gate = project(rest, normed, one, two)
    pool_ref[...] = pool_of(member, pre, gate) * share[...]


def late_slope_kernel(rests, mask, normed, *refs):
    count = len(rests)
    weights, slopes = refs[: 2 * count], refs[2 * count + 1 :]
    for k, rest in enumerate(rests):
        slope = slope_of(*project(rest, normed, weights[2 * k], weights[2 * k + 1]), mask)
        slopes[k][:, : slope.shape[1]] = slope


def backward_kernel(
    plan, flags, block_of, grad_hidden, own_row, gain, mask, layer_input, *refs
):
    count = len(plan)
    slopes = refs[:count]
    weight_refs = refs[count : 3 * count]
    out = refs[3 * count]
    is_text = flags[0] == 1
    step = pl.program_id(0)
    tile = layer_input.shape[0]
    bands = [pl.ds(k * TEXT_LEN, TEXT_LEN) for k in range(tile // TEXT_LEN)]
    slots = [
        jnp.where(
            is_text,
            step * len(bands) + k,
            flags[1] + (step * len(bands) + k) * TEXT_LEN // PATCHES,
        )
        for k in range(len(bands))
    ]
    def pick(lines, slot):
        row = lax.broadcasted_iota(jnp.int32, lines.shape, 0)
        return jnp.sum(jnp.where(row == slot, lines, 0.0), axis=0, keepdims=True)

    def scaled(slope_ref, start, lines):
        found = []
        for band, slot in zip(bands, slots):
            slope = slope_ref[band, start : start + lines.shape[1]].astype(jnp.float32)
            found.append((pick(lines, slot) * slope).astype(jnp.bfloat16))
        return jnp.concatenate(found, axis=0)

    def multiply(left, parts):
        right = jnp.concatenate(parts, axis=0)
        return jnp.dot(left, right, preferred_element_type=jnp.float32)

    def main_part(g):
        parts, _ = plan[g]
        lines = [grad_hidden[block_of[p], :, c * SMALL : (c + 1) * SMALL] for p, c in parts]
        return scaled(slopes[g], 0, jnp.concatenate(lines, axis=1))

    def rest_part(g):
        _, rest = plan[g]
        lines = [grad_hidden[block_of[p], :, 2 * SMALL :] for p in rest]
        return scaled(slopes[g], 2 * SMALL, jnp.concatenate(lines, axis=1))

    rests = [rest_part(g) for g in range(count) if plan[g][1]]
    total = None
    for g in range(0, count, 2):
        left = jnp.concatenate([main_part(g), main_part(g + 1)], axis=1)
        product = multiply(left, [ref[:SMALL] for ref in weight_refs[2 * g : 2 * g + 4]])
        total = product if total is None else total + product
    tails = [ref[SMALL:] for ref in weight_refs if ref.shape[0] > SMALL]
    total = total + multiply(jnp.concatenate(rests, axis=1), tails)

    values = layer_input[...].astype(jnp.float32)
    centered = values - jnp.mean(values, axis=-1, keepdims=True)
    variance = jnp.mean(centered * centered, axis=-1, keepdims=True)
    inv_std = lax.rsqrt(variance + norm_eps)
    standard = centered * inv_std
    grad_std = total * gain[...]
    first_mean = jnp.mean(grad_std, axis=-1, keepdims=True)
    second_mean = jnp.mean(grad_std * standard, axis=-1, keepdims=True)
    result = inv_std * (grad_std - first_mean - standard * second_mean)
    for k, (band, slot) in enumerate(zip(bands, slots)):
        grad_out = pick(own_row[...], slot) * mask[band, :]
        out[band, :] = grad_out + result[k * TEXT_LEN : (k + 1) * TEXT_LEN]


def backward_call(flags, block_of, grad_hidden, own_row, mask, layer_input, gain, slopes, groups):
    row_count, width = layer_input.shape
    tile = 2 * TEXT_LEN
    whole = pl.BlockSpec(memory_space=pltpu.VMEM)
    scalar = pl.BlockSpec(memory_space=pltpu.SMEM)

    def by_rows(cols):
        return pl.BlockSpec((tile, cols), lambda i: (i, 0))

    plan = [(parts, rest) for parts, rest, _ in groups]
    weights = [w for _, _, pair in groups for w in pair]
    count = len(plan)
    units = sum(w.shape[0] for w in weights)
    return pl.pallas_call(
        functools.partial(backward_kernel, plan),
        grid=(row_count // tile,),
        in_specs=[scalar] * 2
        + [whole] * 3
        + [by_rows(1), by_rows(width)]
        + [by_rows(slope.shape[1]) for slope in slopes]
        + [whole] * (2 * count),
        out_specs=by_rows(width),
        out_shape=jax.ShapeDtypeStruct((row_count, width), jnp.float32),
        compiler_params=pltpu.CompilerParams(vmem_limit_bytes=60 * 1024 * 1024),
        cost_estimate=pl.CostEstimate(
            flops=2 * row_count * width * units, bytes_accessed=12_000_000, transcendentals=0
        ),
    )(
        flags,
        block_of,
        grad_hidden,
        own_row,
        gain.reshape(1, width),
        mask,
        layer_input,
        *slopes,
        *weights,
    )


def partial_kernel(flags, block_of, share, value_pool, mine, late, w_second, out, pools, rows):
    slots, shard = late.shape
    pools[...] = mine[...]
    pools[block_of[4]] = late[...]
    high, low = two_parts(pools[...].reshape(8 * slots, shard))
    second = w_second[flags[0]]
    both = jnp.dot(
        jnp.concatenate([high, low], axis=0), second, preferred_element_type=jnp.float32
    )
    rows[...] = both[: 8 * slots] + both[8 * slots :]
    own = pl.ds(pl.multiple_of(flags[2] * slots, slots), slots)
    rows[own, :] += value_pool[...] * share[...]
    pair = out.shape[1]
    for k in range(out.shape[0]):
        out[k] = rows[k * pair : (k + 1) * pair, :].astype(out.dtype)


def embed_kernel(groups, notes, back, *refs):
    out = refs[-1]

    def total(places):
        found = back[places[0]].astype(jnp.float32)
        for place in places[1:]:
            found = found + back[place].astype(jnp.float32)
        return found

    devices = range(back.shape[0])
    image = total([d for d in devices if d % groups < groups - 1])
    text = total([d for d in devices if d % groups == groups - 1])
    pooled = jnp.concatenate([image, text], axis=0)
    norm = jnp.sqrt(jnp.sum(pooled * pooled, axis=-1, keepdims=True) + norm_eps)
    emb = (pooled / norm).astype(jnp.bfloat16)
    high = norm.astype(jnp.bfloat16).astype(jnp.float32)
    lane = lax.broadcasted_iota(jnp.int32, notes.shape, 1)
    marks = jnp.where(lane == 0, high, jnp.where(lane == 1, norm - high, notes[...]))
    row = jnp.concatenate([emb, marks.astype(jnp.bfloat16)], axis=1)
    out[...] = jnp.broadcast_to(row[None], out.shape)


def loss_kernel(groups, flags, scalars, packed, w_second, grad_cols, own_row, rows_ref):
    is_text = flags[0] == 1
    scale, bias = scalars[0], scalars[1]
    count, total_width = packed.shape
    width = own_row.shape[1]
    half = count // 2
    row = lax.broadcasted_iota(jnp.int32, (half, count), 0)
    column = lax.broadcasted_iota(jnp.int32, (half, count), 1)
    place = 4 * (row // 2) + row % 2
    everything = packed[...]

    def chosen(offset):
        which = (column == place + offset).astype(jnp.bfloat16)
        return jnp.dot(which, everything, preferred_element_type=jnp.float32)

    image, text = chosen(0), chosen(2)
    image16 = image[:, :width].astype(jnp.bfloat16)
    text16 = text[:, :width].astype(jnp.bfloat16)
    logits = scale * contract_last(image16, text16) + bias
    positive = image[:, width + 2 : width + 3] * 64.0 + image[:, width + 3 : width + 4]
    row = lax.broadcasted_iota(jnp.int32, (half, half), 0)
    column = lax.broadcasted_iota(jnp.int32, (half, half), 1)
    onehot = (column.astype(jnp.float32) == positive).astype(jnp.float32)
    sigmoid = 1.0 / (1.0 + jnp.exp(-logits))
    real = row % (2 * groups) < 2 * (groups - 1)
    coef = jnp.where(real, loss_scale * (sigmoid - onehot), 0.0)
    left = jnp.where(is_text, coef.T, coef).astype(jnp.bfloat16)
    right = jnp.where(is_text, image16, text16)
    grad_emb = scale * jnp.dot(left, right, preferred_element_type=jnp.float32)
    own = jnp.where(is_text, text, image)
    unit = own[:, :width]
    norm = own[:, width : width + 1] + own[:, width + 1 : width + 2]
    rows = own[:, width + 4 : width + 5]
    grad_pooled = grad_emb - unit * jnp.sum(unit * grad_emb, axis=-1, keepdims=True)
    grad_row = grad_pooled / (norm * rows)
    rows_ref[...] = grad_row
    own_row[...] = rows_ref[pl.ds(pl.multiple_of(flags[2] * 8, 8), 8), :]
    second = w_second[flags[0]]
    columns = contract_last(grad_row.astype(jnp.bfloat16), second)
    for block in range(grad_cols.shape[0]):
        grad_cols[block] = columns[block * 8 : (block + 1) * 8]


def small_call(kernel, outs, operands, scalars, scratch=(), flops=0, moved=0, outside=0):
    single = not isinstance(outs, tuple)
    whole = pl.BlockSpec(memory_space=pltpu.VMEM)
    scalar = pl.BlockSpec(memory_space=pltpu.SMEM)
    return pl.pallas_call(
        kernel,
        in_specs=[scalar] * scalars
        + [whole] * (len(operands) - scalars - outside)
        + [pl.BlockSpec(memory_space=pl.ANY)] * outside,
        out_specs=whole if single else tuple(whole for _ in outs),
        out_shape=outs,
        scratch_shapes=scratch,
        compiler_params=pltpu.CompilerParams(vmem_limit_bytes=16 * 1024 * 1024),
        cost_estimate=pl.CostEstimate(flops=flops, bytes_accessed=moved, transcendentals=0),
    )(*operands)


def ring_body(
    layer_input, caption_ids, positives, ln_gain, w_first, w_second, logit_scale, logit_bias
):
    groups = lax.axis_size("tower")
    tower_index = lax.axis_index("tower")
    block_index = lax.axis_index("blk")
    is_text = tower_index == groups - 1
    row_count, width = layer_input.shape
    slots = caption_ids.shape[0]
    img_count = positives.shape[0] // (groups - 1)
    shard = w_first.shape[2]
    gain = jnp.where(is_text, ln_gain[1], ln_gain[0])
    own = [
        jnp.where(is_text, w_first[1, :, cut].T, w_first[0, :, cut].T)
        for cut in (slice(0, SMALL), slice(SMALL, shard))
    ]
    flags = jnp.stack([is_text.astype(jnp.int32), tower_index * img_count, block_index])
    flags = flags.astype(jnp.int32)
    place = jnp.where(block_index % 2 == 0, block_index // 2, 7 - block_index // 2)
    around = (place + jnp.arange(8, dtype=jnp.int32)) % 8
    block_of = jnp.where(around < 4, 2 * around, 2 * (7 - around) + 1).astype(jnp.int32)

    mask = (caption_ids != 0).astype(jnp.float32)
    counts = jnp.sum(mask, axis=1, keepdims=True)
    row = jnp.arange(row_count, dtype=jnp.int32)[None, :]
    slot = jnp.arange(slots, dtype=jnp.int32)[:, None]
    row_mask = jnp.where(is_text, mask.reshape(1, row_count), 1.0)
    slot_of = jnp.where(is_text, row // TEXT_LEN, tower_index * img_count + row // PATCHES)
    member16 = jnp.where(slot_of == slot, row_mask, 0.0).astype(jnp.bfloat16)
    share = jnp.where(is_text, 1.0 / counts, 1.0 / PATCHES)

    values = layer_input.astype(jnp.float32)
    centered = values - jnp.mean(values, axis=-1, keepdims=True)
    variance = jnp.mean(centered * centered, axis=-1, keepdims=True)
    normed = (centered * lax.rsqrt(variance + norm_eps) * gain).astype(jnp.bfloat16)
    row_mask = row_mask.reshape(row_count, 1)
    arrivals = groups_of(ring_gather(own, groups))
    plan = [(parts, rest) for parts, rest, _ in arrivals]
    share = share.astype(jnp.float32)
    cost = {"flops": int(4e9), "moved": int(16e6)}
    held_shape = jax.ShapeDtypeStruct((8, slots, shard), jnp.float32)
    slopes = []
    held = value_pool = last_pool = None
    for k, (parts, rest, (one, two)) in enumerate(arrivals):
        columns = 3 * SMALL if rest else 2 * SMALL
        slope_shape = jax.ShapeDtypeStruct((row_count, columns), jnp.bfloat16)
        shared = [share, member16]
        weights = [normed, one, two]
        if k == 0:
            slope, held, value_pool = small_call(
                functools.partial(own_kernel, parts, rest),
                (slope_shape, held_shape, jax.ShapeDtypeStruct((slots, width), jnp.float32)),
                [block_of, layer_input, *shared, row_mask, *weights],
                1,
                **cost,
            )
            slopes.append(slope)
        elif k < len(arrivals) - 2:
            slope, held = small_call(
                functools.partial(forward_kernel, parts, rest),
                (slope_shape, held_shape),
                [block_of, held, *shared, row_mask, *weights],
                1,
                **cost,
            )
            slopes.append(slope)
        elif k == len(arrivals) - 2:
            held = small_call(
                functools.partial(pool_kernel, parts, rest),
                held_shape,
                [block_of, held, *shared, *weights],
                1,
                **cost,
            )
        else:
            last_pool = small_call(
                functools.partial(last_pool_kernel, rest),
                jax.ShapeDtypeStruct((slots, shard), jnp.float32),
                [*shared, *weights],
                0,
                **cost,
            )

    devices = 8 * groups
    pair = slots // groups
    mine = lax.all_to_all(held, "blk", 0, 0)
    opposite = []
    for place in range(8):
        for t in range(groups):
            source = RING[place] * groups + t
            opposite.append((source, RING[(place + 4) % 8] * groups + t))
    late = lax.ppermute(last_pool, ("blk", "tower"), opposite)
    partial = small_call(
        partial_kernel,
        jax.ShapeDtypeStruct((devices, pair, width), jnp.bfloat16),
        [flags, block_of, share, value_pool, mine, late, w_second],
        2,
        (
            pltpu.VMEM((8, slots, shard), jnp.float32),
            pltpu.VMEM((8 * slots, width), jnp.float32),
        ),
    )
    back = lax.all_to_all(partial, ("blk", "tower"), 0, 0)
    slopes += small_call(
        functools.partial(late_slope_kernel, [rest for _, rest, _ in arrivals[-2:]]),
        (jax.ShapeDtypeStruct((row_count, 3 * SMALL), jnp.bfloat16),) * 2,
        [row_mask, normed] + [w for _, _, pair_of in arrivals[-2:] for w in pair_of] + [partial],
        0,
        flops=int(1e9),
        moved=int(4e6),
        outside=1,
    )

    start = jnp.minimum(tower_index, groups - 2) * img_count
    own_positive = lax.dynamic_slice_in_dim(positives, start, img_count, 0)
    own_counts = lax.dynamic_slice_in_dim(counts[:, 0], tower_index * pair, pair, 0)
    none = jnp.zeros((pair,), jnp.int32)
    notes = jnp.stack(
        [
            jnp.zeros((2 * pair,), jnp.float32),
            jnp.zeros((2 * pair,), jnp.float32),
            jnp.concatenate([own_positive // 64, none]).astype(jnp.float32),
            jnp.concatenate([own_positive % 64, none]).astype(jnp.float32),
            jnp.concatenate([jnp.full((pair,), PATCHES, jnp.float32), own_counts]),
        ],
        axis=1,
    )
    notes = jnp.pad(notes, ((0, 0), (0, 128 - notes.shape[1])))
    copies = small_call(
        functools.partial(embed_kernel, groups),
        jax.ShapeDtypeStruct((devices, 2 * pair, width + 128), jnp.bfloat16),
        [notes, back, *slopes[-2:]],
        0,
        outside=2,
    )
    packed = lax.all_to_all(copies, ("blk", "tower"), 0, 0)
    packed = packed.reshape(devices * 2 * pair, width + 128)
    grad_cols, own_row = small_call(
        functools.partial(loss_kernel, groups),
        (
            jax.ShapeDtypeStruct((8, slots, shard), jnp.float32),
            jax.ShapeDtypeStruct((slots, width), jnp.float32),
        ),
        [flags, jnp.concatenate([logit_scale, logit_bias]), packed, w_second],
        2,
        (pltpu.VMEM((devices * pair, width), jnp.float32),),
    )
    grad_hidden = lax.all_to_all(grad_cols, "blk", 0, 0)
    return backward_call(
        flags,
        block_of,
        grad_hidden,
        own_row,
        row_mask,
        layer_input,
        gain,
        slopes,
        arrivals,
    )


def general_body(layer_input, caption_ids, positives, ln_gain, w_first, w_second, logit_scale, logit_bias):
    groups = lax.axis_size("tower")
    blocks = lax.axis_size("blk")
    tower_index = lax.axis_index("tower")
    block_index = lax.axis_index("blk")
    is_text = tower_index == groups - 1
    row_count, width = layer_input.shape
    slots = caption_ids.shape[0]
    img_count = positives.shape[0] // (groups - 1)
    shard = w_first.shape[2]
    gain = jnp.where(is_text, ln_gain[1], ln_gain[0])
    first = jnp.where(is_text, w_first[1].T, w_first[0].T)
    second = jnp.where(is_text, w_second[1], w_second[0])

    mask = (caption_ids != 0).astype(jnp.float32)
    counts = jnp.sum(mask, axis=1, keepdims=True)
    row = jnp.arange(row_count, dtype=jnp.int32)[None, :]
    slot = jnp.arange(slots, dtype=jnp.int32)[:, None]
    row_mask = jnp.where(is_text, mask.reshape(1, row_count), 1.0)
    member = jnp.where(jnp.where(is_text, row // TEXT_LEN, row // PATCHES) == slot, row_mask, 0.0)
    share = jnp.where(is_text, 1.0 / counts, 1.0 / PATCHES)
    member16 = member.astype(jnp.bfloat16)

    values = layer_input.astype(jnp.float32)
    centered = values - jnp.mean(values, axis=-1, keepdims=True)
    variance = jnp.mean(centered * centered, axis=-1, keepdims=True)
    inv_std = lax.rsqrt(variance + norm_eps)
    standard = centered * inv_std
    normed = (standard * gain).astype(jnp.bfloat16)
    full = lax.all_gather(first, "blk", axis=0, tiled=True)
    value, slope = gelu_pair(contract_last(normed, full))
    hidden_pool = jnp.dot(member16, value.astype(jnp.bfloat16), preferred_element_type=jnp.float32)
    hidden_pool = hidden_pool * share
    value_pool = jnp.dot(member16, layer_input, preferred_element_type=jnp.float32) * share

    sent = hidden_pool.reshape(slots, blocks, shard).transpose(1, 0, 2)
    mine = lax.all_to_all(sent, "blk", 0, 0).reshape(blocks * slots, shard)
    high, low = two_parts(mine)
    partial = jnp.dot(high, second, preferred_element_type=jnp.float32) + jnp.dot(
        low, second, preferred_element_type=jnp.float32
    )
    back = lax.all_to_all(partial.reshape(blocks, slots, width), "blk", 0, 0)
    pooled = value_pool + jnp.sum(back, axis=0)

    norm = jnp.sqrt(jnp.sum(pooled * pooled, axis=-1, keepdims=True) + norm_eps)
    emb = (pooled / norm).astype(jnp.bfloat16)
    norm_high, norm_low = two_parts(norm)
    start = jnp.minimum(tower_index, groups - 2) * img_count
    own_positive = lax.dynamic_slice_in_dim(positives, start, img_count, 0)
    own_positive = jnp.pad(own_positive, (0, slots - img_count))[:, None]
    extra = jnp.concatenate(
        [
            norm_high,
            norm_low,
            (own_positive // 64).astype(jnp.bfloat16),
            (own_positive % 64).astype(jnp.bfloat16),
            jnp.where(is_text, counts, PATCHES).astype(jnp.bfloat16),
        ],
        axis=1,
    )
    extra = jnp.pad(extra, ((0, 0), (0, 128 - extra.shape[1])))
    packed = jnp.concatenate([emb, extra], axis=1)
    packed = lax.all_to_all(
        jnp.broadcast_to(packed[None], (groups * blocks, *packed.shape)), ("tower", "blk"), 0, 0
    ).reshape(groups * blocks * slots, packed.shape[1])
    every = packed[:, :width]
    notes = packed[:, width : width + 5].astype(jnp.float32)
    every_norm = notes[:, :1] + notes[:, 1:2]
    every_positive = (notes[:, 2:3] * 64.0 + notes[:, 3:4]).astype(jnp.int32)

    scale = logit_scale[0]
    bias = logit_bias[0]
    images = (groups - 1) * blocks * slots
    column = blocks * slots
    text_emb = every[images:]
    logits = scale * contract_last(every[:images], text_emb) + bias
    caption_index = jnp.arange(column, dtype=jnp.int32)[None, :]
    onehot = (every_positive[:images] == caption_index).astype(jnp.float32)
    real = (jnp.arange(images, dtype=jnp.int32) % slots < img_count)[:, None]
    coef = jnp.where(real, loss_scale * (jax.nn.sigmoid(logits) - onehot), 0.0).astype(jnp.bfloat16)
    own = lax.dynamic_slice_in_dim(every, tower_index * column, column, 0)
    own_norm = lax.dynamic_slice_in_dim(every_norm, tower_index * column, column, 0)
    own_coef = lax.dynamic_slice_in_dim(coef, jnp.minimum(tower_index, groups - 2) * column, column, 0)
    grad_image = jnp.dot(own_coef, text_emb, preferred_element_type=jnp.float32)
    grad_text = lax.dot_general(
        coef, every[:images], (((0,), (0,)), ((), ())), preferred_element_type=jnp.float32
    )
    grad_emb = scale * jnp.where(is_text, grad_text, grad_image)
    unit = own.astype(jnp.float32)
    grad_pooled = (grad_emb - unit * jnp.sum(unit * grad_emb, axis=-1, keepdims=True)) / own_norm
    own_rows = lax.dynamic_slice_in_dim(notes[:, 4:5], tower_index * column, column, 0)
    grad_row = grad_pooled / own_rows
    grad_cols = contract_last(grad_row.astype(jnp.bfloat16), second)
    grad_hidden = lax.all_to_all(grad_cols.reshape(blocks, slots, shard), "blk", 0, 0)
    own_row = lax.dynamic_slice_in_dim(grad_row, block_index * slots, slots, 0)
    def spread(rows):
        cols = rows.shape[1]
        image = jnp.broadcast_to(
            rows[:img_count, None, :], (img_count, PATCHES, cols)
        ).reshape(row_count, cols)
        text = (rows[:, None, :] * mask[:, :, None]).reshape(row_count, cols)
        return jnp.where(is_text, text, image)

    grad_hidden = grad_hidden.transpose(1, 0, 2).reshape(slots, blocks * shard)
    grad_out = spread(own_row)
    grad_pre = (spread(grad_hidden) * slope).astype(jnp.bfloat16)
    grad_normed = jnp.dot(grad_pre, full, preferred_element_type=jnp.float32)
    grad_std = grad_normed * gain
    first_mean = jnp.mean(grad_std, axis=-1, keepdims=True)
    second_mean = jnp.mean(grad_std * standard, axis=-1, keepdims=True)
    return grad_out + inv_std * (grad_std - first_mean - standard * second_mean)


def body(layer_input, *others):
    w_first = others[3]
    ring = (
        lax.axis_size("blk") == 8
        and lax.axis_size("tower") == 4
        and w_first.shape[2] == 272
        and others[0].shape[0] == 8
        and others[1].shape[0] == 6
    )
    return (ring_body if ring else general_body)(layer_input, *others)


def solution(mesh):
    placed = (
        P(("blk", "tower"), None),
        P("blk", None),
        P("blk"),
        P(),
        P(None, None, "blk"),
        P(None, "blk", None),
        P(),
        P(),
    )
    return jax.shard_map(
        body, mesh=mesh, in_specs=placed, out_specs=P(("blk", "tower"), None), check_vma=False
    )
```

time: 304 us -> 121 us (0.40)
  waiting for transfers between devices: 158 us -> 26.1 us
  blocking collectives: 90.1 us -> 10.2 us
  starting transfers between devices: 0.04 us -> 34.5 us
  Pallas kernels: 0 us -> 32.4 us
  matrix products: 28 us -> 0 us
  between operations: 15.5 us -> 1.63 us
  local copies, waits for them, and re-layouts: 1.43 us -> 9.72 us
  other arithmetic: 10 us -> 5.88 us
    all_gather x2 -> x0, waiting for transfers between devices: 158 us -> none  [the longest x1 82.1 us: body(): lax.all_gather(first, 'blk', axis=1, tiled=True)]
    unnamed x1 -> x0, blocking collectives: 38.8 us -> none
    pallas_call x0 -> x13, Pallas kernels: none -> 32.4 us  [the longest x12 23.4 us: small_call(): pl.pallas_call(kernel, in_specs=[scalar] * scalars + [whole] * (len(opera...]
    all_gather x1 -> x0, blocking collectives: 30.6 us -> none  [body(): every = lax.all_gather(span, 'blk', axis=0, tiled=True)]
    dot_general x6 -> x0, matrix products: 28 us -> none  [the longest x2 13.1 us: contract_last(): lax.dot_general(left, right, (((1,), (1,)), ((), ())), preferred_element_...]
    psum x2 -> x0, blocking collectives: 20.7 us -> none  [the longest x1 10.4 us: body(): lax.psum(span_grad.astype(jnp.bfloat16), 'tower').astype(jnp.float32)]
    ppermute x0 -> x15, starting transfers between devices: none -> 20.1 us  [the longest x14 15.3 us: move(): return lax.ppermute(value, ('blk', 'tower'), found)]
    all_to_all x0 -> x3, starting transfers between devices: none -> 14.4 us  [the longest x1 6.12 us: ring_body(): back = lax.all_to_all(partial, ('blk', 'tower'), 0, 0)]
  transfers between devices with their start and end apart: 2 -> 18, of which waited for: 2 -> 9; matrix products, arithmetic and copies ran while one was open for 3% -> 5% of each run, Pallas kernels for 0% -> 15%
where the time goes in v1:
time: 121 us; the launch traced here: 120 us
  starting transfers between devices  34.5 us (29%)
  Pallas kernels  32.4 us (27%)
  waiting for transfers between devices  26.1 us (22%)
  blocking collectives  10.2 us (8%)
  local copies, waits for them, and re-layouts  9.72 us (8%)
  other arithmetic  5.88 us (5%)
  between operations  1.63 us (1%)
    pallas_call x12, Pallas kernels, small_call(): pl.pallas_call(kernel, in_specs=[scalar] * scalars + [whole] * (len(opera...  23.4 us
    ppermute x14, starting transfers between devices, move(): return lax.ppermute(value, ('blk', 'tower'), found)  15.3 us
    ppermute x14, waiting for transfers between devices, move(): return lax.ppermute(value, ('blk', 'tower'), found)  11.7 us
    all_to_all x1, waiting for transfers between devices, ring_body(): packed = lax.all_to_all(copies, ('blk', 'tower'), 0, 0)  10.6 us
    all_to_all x1, blocking collectives, ring_body(): grad_hidden = lax.all_to_all(grad_cols, 'blk', 0, 0)  10.2 us
    pallas_call x1, Pallas kernels, backward_call(): pl.pallas_call(functools.partial(backward_kernel, plan), grid=(row_count...  8.99 us
    unnamed x66, local copies, waits for them, and re-layouts  8.84 us
    all_to_all x1, starting transfers between devices, ring_body(): back = lax.all_to_all(partial, ('blk', 'tower'), 0, 0)  6.12 us
  transfers between devices with their start and end apart: 18, of which 9 were waited for; matrix products, arithmetic and copies ran while one was open for 5% of the time, Pallas kernels for 15%

profile of v1, /device:TPU:0, one launch (start us, length us, event | category | flops | bytes accessed | tf_op | source)
XLA Modules:
  0.0 120.5 jit_solution(3602807732059291568)
XLA Ops:
  1.2 3.0 %collective-permute-start.1 = (bf16[128,1152]{1,0:T(8,128)(2,1)S(1)}, bf16[128,1152]{1,0:T(8,128)(2,1)}, u32[]{:S(2)}, u32[]{:S(2)}) collective-permute-start(bf16[128,1152]{1,0:T(8,128)(2,1)S(1)} %select_bitcast_fusion.1.one.refs_8_), channel_id=1, source_target_pairs={{0,4},{1,5},{2,6},{3,7},{8,0},{9,1},{10,2},{11,3},{16,8},{17,9},{1... | collective-permute-start | bytes 884744 | tf_op jit(solution)/shard_map/ppermute | solution.py:54
  5.5 2.0 %collective-permute-start.3 = (bf16[144,1152]{1,0:T(8,128)(2,1)S(1)}, bf16[144,1152]{1,0:T(8,128)(2,1)S(1)}, u32[]{:S(2)}, u32[]{:S(2)}) collective-permute-start(bf16[144,1152]{1,0:T(8,128)(2,1)S(1)} %select_bitcast_fusion.two.refs_9_), channel_id=1, source_target_pairs={{0,4},{1,5},{2,6},{3,7},{8,0},{9,1},{10,2},{11,3},{16,8},{17,9},{1... | collective-permute-start | bytes 995336 | tf_op jit(solution)/shard_map/ppermute | solution.py:54
  11.6 2.0 %shard_map.82 = (bf16[512,384]{1,0:T(8,128)(2,1)S(1)}, f32[8,8,272]{2,1,0:T(8,128)S(1)}, f32[8,1152]{1,0:T(8,128)S(1)}) custom-call(s32[8]{0:T(128)S(1)} %compare_select_fusion.2.block_of, bf16[512,1152]{1,0:T(8,128)(2,1)S(1)} %copy-done, f32[8,1]{1,0:T(8,128)S(1)} %copy.38.share, bf16[8,512]{1,0:T(8,128)(2,1)S(1)} %select_convert_fusion.member, ...), custom_call_target="tpu_custom_call" | custom-call | flops 4000000000 | bytes 16000000 | tf_op jit(solution)/shard_map/pallas_call | solution.py:343
  13.5 2.0 %collective-permute-start.5 = (bf16[128,1152]{1,0:T(8,128)(2,1)}, bf16[128,1152]{1,0:T(8,128)(2,1)S(1)}, u32[]{:S(2)}, u32[]{:S(2)}) collective-permute-start(bf16[128,1152]{1,0:T(8,128)(2,1)} %collective-permute-done.1.two.refs_11_), channel_id=1, source_target_pairs={{0,4},{1,5},{2,6},{3,7},{8,0},{9,1},{10,2},{11,3},{16,8},{17,9},{1... | collective-permute-start | bytes 884744 | tf_op jit(solution)/shard_map/ppermute | solution.py:54
  15.6 1.9 %shard_map.83 = (bf16[512,256]{1,0:T(8,128)(2,1)S(1)}, f32[8,8,272]{2,1,0:T(8,128)S(1)}) custom-call(s32[8]{0:T(128)S(1)} %compare_select_fusion.2.block_of, f32[8,8,272]{2,1,0:T(8,128)S(1)} %get-tuple-element.23.before, f32[8,1]{1,0:T(8,128)S(1)} %copy.38.share, bf16[8,512]{1,0:T(8,128)(2,1)S(1)} %select_convert_fusion.member, ...), custom_call_target="tpu_custom_call" | custom-call | flops 4000000000 | bytes 16000000 | tf_op jit(solution)/shard_map/pallas_call | solution.py:343
  19.2 2.0 %collective-permute-start.7 = (bf16[144,1152]{1,0:T(8,128)(2,1)S(1)}, bf16[144,1152]{1,0:T(8,128)(2,1)S(1)}, u32[]{:S(2)}, u32[]{:S(2)}) collective-permute-start(bf16[144,1152]{1,0:T(8,128)(2,1)S(1)} %collective-permute-done.3.two.refs_13_), channel_id=1, source_target_pairs={{0,4},{1,5},{2,6},{3,7},{8,0},{9,1},{10,2},{11,3},{16,8},{17,9},{1... | collective-permute-start | bytes 995336 | tf_op jit(solution)/shard_map/ppermute | solution.py:54
  21.4 1.9 %shard_map.84 = (bf16[512,384]{1,0:T(8,128)(2,1)S(1)}, f32[8,8,272]{2,1,0:T(8,128)S(1)}) custom-call(s32[8]{0:T(128)S(1)} %compare_select_fusion.2.block_of, f32[8,8,272]{2,1,0:T(8,128)S(1)} %get-tuple-element.24.before, f32[8,1]{1,0:T(8,128)S(1)} %copy.38.share, bf16[8,512]{1,0:T(8,128)(2,1)S(1)} %select_convert_fusion.member, ...), custom_call_target="tpu_custom_call" | custom-call | flops 4000000000 | bytes 16000000 | tf_op jit(solution)/shard_map/pallas_call | solution.py:343
  25.5 2.0 %collective-permute-start.9 = (bf16[128,1152]{1,0:T(8,128)(2,1)S(1)}, bf16[128,1152]{1,0:T(8,128)(2,1)S(1)}, u32[]{:S(2)}, u32[]{:S(2)}) collective-permute-start(bf16[128,1152]{1,0:T(8,128)(2,1)S(1)} %collective-permute-done.5.two.refs_15_), channel_id=1, source_target_pairs={{0,4},{1,5},{2,6},{3,7},{8,0},{9,1},{10,2},{11,3},{16,8},{17,9},{1... | collective-permute-start | bytes 884744 | tf_op jit(solution)/shard_map/ppermute | solution.py:54
  29.8 2.8 %collective-permute-done.7.two.refs_17_ = bf16[144,1152]{1,0:T(8,128)(2,1)S(1)} collective-permute-done((bf16[144,1152]{1,0:T(8,128)(2,1)S(1)}, bf16[144,1152]{1,0:T(8,128)(2,1)S(1)}, u32[]{:S(2)}, u32[]{:S(2)}) %collective-permute-start.7) | collective-permute-done | bytes 331808 | tf_op jit(solution)/shard_map/ppermute | solution.py:54
  32.7 2.0 %collective-permute-start.11 = (bf16[144,1152]{1,0:T(8,128)(2,1)S(1)}, bf16[144,1152]{1,0:T(8,128)(2,1)S(1)}, u32[]{:S(2)}, u32[]{:S(2)}) collective-permute-start(bf16[144,1152]{1,0:T(8,128)(2,1)S(1)} %collective-permute-done.7.two.refs_17_), channel_id=1, source_target_pairs={{0,4},{1,5},{2,6},{3,7},{8,0},{9,1},{10,2},{11,3},{16,8},{17,9},{1... | collective-permute-start | bytes 995336 | tf_op jit(solution)/shard_map/ppermute | solution.py:54
  34.8 1.9 %shard_map.86 = (bf16[512,384]{1,0:T(8,128)(2,1)S(1)}, f32[8,8,272]{2,1,0:T(8,128)S(1)}) custom-call(s32[8]{0:T(128)S(1)} %compare_select_fusion.2.block_of, f32[8,8,272]{2,1,0:T(8,128)S(1)} %get-tuple-element.26.before, f32[8,1]{1,0:T(8,128)S(1)} %copy.38.share, bf16[8,512]{1,0:T(8,128)(2,1)S(1)} %select_convert_fusion.member, ...), custom_call_target="tpu_custom_call" | custom-call | flops 4000000000 | bytes 16000000 | tf_op jit(solution)/shard_map/pallas_call | solution.py:343
  37.4 3.7 %collective-permute-done.8.one.refs_18_ = bf16[128,1152]{1,0:T(8,128)(2,1)} collective-permute-done((bf16[128,1152]{1,0:T(8,128)(2,1)S(1)}, bf16[128,1152]{1,0:T(8,128)(2,1)}, u32[]{:S(2)}, u32[]{:S(2)}) %collective-permute-start.8) | collective-permute-done | bytes 294944 | tf_op jit(solution)/shard_map/ppermute | solution.py:54
  41.2 1.9 %shard_map.87 = (bf16[512,256]{1,0:T(8,128)(2,1)S(1)}, f32[8,8,272]{2,1,0:T(8,128)S(1)}) custom-call(s32[8]{0:T(128)S(1)} %compare_select_fusion.2.block_of, f32[8,8,272]{2,1,0:T(8,128)S(1)} %get-tuple-element.27.before, f32[8,1]{1,0:T(8,128)S(1)} %copy.38.share, bf16[8,512]{1,0:T(8,128)(2,1)S(1)} %select_convert_fusion.member, ...), custom_call_target="tpu_custom_call" | custom-call | flops 4000000000 | bytes 16000000 | tf_op jit(solution)/shard_map/pallas_call | solution.py:343
  48.1 2.3 %shard_map.88 = f32[8,8,272]{2,1,0:T(8,128)} custom-call(s32[8]{0:T(128)S(1)} %compare_select_fusion.2.block_of, f32[8,8,272]{2,1,0:T(8,128)S(1)} %get-tuple-element.28.before, f32[8,1]{1,0:T(8,128)S(1)} %copy.38.share, bf16[8,512]{1,0:T(8,128)(2,1)S(1)} %select_convert_fusion.member, bf16[512,1152]{1,0:T(8,128)(2,1)S(1)} %fusion.4.normed, ...), custom_call_target="tpu_custom_call" | custom-call | flops 4000000000 | bytes 16000000 | tf_op jit(solution)/shard_map/pallas_call | solution.py:343
  51.2 4.9 %all-to-all-start = ((f32[8,8,272]{2,1,0:T(8,128)}), f32[8,8,272]{2,1,0:T(8,128)S(1)}, u32[]{:S(2)}, u32[]{:S(2)}) async-start(f32[8,8,272]{2,1,0:T(8,128)} %shard_map.88), calls=%async_computation | async-start | bytes 196608 | tf_op jit(solution)/shard_map/all_to_all | solution.py:441
  57.5 2.2 %shard_map.89 = f32[8,272]{1,0:T(8,128)S(1)} custom-call(f32[8,1]{1,0:T(8,128)S(1)} %copy.38.share, bf16[8,512]{1,0:T(8,128)(2,1)S(1)} %select_convert_fusion.member, bf16[512,1152]{1,0:T(8,128)(2,1)S(1)} %copy-done.7, bf16[128,1152]{1,0:T(8,128)(2,1)} %collective-permute-done.12.one.refs_2_.refs_22_, ...), custom_call_target="tpu_custom_call" | custom-call | flops 4000000000 | bytes 16000000 | tf_op jit(solution)/shard_map/pallas_call | solution.py:343
  59.7 4.8 %collective-permute-start.14 = (f32[8,272]{1,0:T(8,128)S(1)}, f32[8,272]{1,0:T(8,128)S(1)}, u32[]{:S(2)}, u32[]{:S(2)}) collective-permute-start(f32[8,272]{1,0:T(8,128)S(1)} %shard_map.89), channel_id=1, source_target_pairs={{0,28},{1,29},{2,30},{3,31},{8,20},{9,21},{10,22},{11,23},{16,12},... | collective-permute-start | bytes 26120 | tf_op jit(solution)/shard_map/ppermute | solution.py:447
  67.8 6.1 %all-to-all-start.1 = ((bf16[32,2,1152]{2,1,0:T(2,128)(2,1)}), bf16[32,2,1152]{2,1,0:T(2,128)(2,1)}, u32[]{:S(2)}, u32[]{:S(2)}) async-start(bf16[32,2,1152]{2,1,0:T(2,128)(2,1)} %shard_map.90.refs_4_), calls=%async_computation.1 | async-start | bytes 294912 | tf_op jit(solution)/shard_map/all_to_all | solution.py:458
  76.9 2.8 %shard_map.91 = (bf16[512,384]{1,0:T(8,128)(2,1)S(1)}, bf16[512,384]{1,0:T(8,128)(2,1)S(1)}) custom-call(f32[512,1]{1,0:T(8,128)S(1)} %select_n.177.mask, bf16[512,1152]{1,0:T(8,128)(2,1)S(1)} %copy-done.8, bf16[144,1152]{1,0:T(8,128)(2,1)S(1)} %copy-done.20, bf16[144,1152]{1,0:T(8,128)(2,1)S(1)} %copy-done.18, ...), custom_call_target="tpu_custom_call" | custom-call | flops 1000000000 | bytes 4000000 | tf_op jit(solution)/shard_map/pallas_call | solution.py:343
  79.8 2.5 %all-to-all-done.1.back = bf16[32,2,1152]{2,1,0:T(2,128)(2,1)} async-done(((bf16[32,2,1152]{2,1,0:T(2,128)(2,1)}), bf16[32,2,1152]{2,1,0:T(2,128)(2,1)}, u32[]{:S(2)}, u32[]{:S(2)}) %all-to-all-start.1) | async-done | bytes 147488 | tf_op jit(solution)/shard_map/all_to_all | solution.py:458
  84.1 3.4 %all-to-all-start.2 = ((bf16[32,4,1280]{2,1,0:T(4,128)(2,1)}), bf16[32,4,1280]{2,1,0:T(4,128)(2,1)S(1)}, u32[]{:S(2)}, u32[]{:S(2)}) async-start(bf16[32,4,1280]{2,1,0:T(4,128)(2,1)} %shard_map.92), calls=%async_computation.2 | async-start | bytes 655360 | tf_op jit(solution)/shard_map/all_to_all | solution.py:491
  88.9 10.6 %all-to-all-done.2 = bf16[32,4,1280]{2,1,0:T(4,128)(2,1)S(1)} async-done(((bf16[32,4,1280]{2,1,0:T(4,128)(2,1)}), bf16[32,4,1280]{2,1,0:T(4,128)(2,1)S(1)}, u32[]{:S(2)}, u32[]{:S(2)}) %all-to-all-start.2) | async-done | bytes 327712 | tf_op jit(solution)/shard_map/all_to_all | solution.py:491
  101.3 10.2 %all_to_all.20.grad_hidden = f32[8,8,272]{2,1,0:T(8,128)} all-to-all(f32[8,8,272]{2,1,0:T(8,128)S(1)} %get-tuple-element.31), channel_id=1, replica_groups=mesh['blk'=8,'tower'=4] {'blk'}, dimensions={0} | all-to-all | bytes 139264 | tf_op jit(solution)/shard_map/all_to_all | solution.py:503
  111.5 9.0 %shard_map.94 = f32[512,1152]{1,0:T(8,128)} custom-call(s32[3]{0:T(128)} %copy-done.30, s32[8]{0:T(128)} %copy-done.31, f32[8,8,272]{2,1,0:T(8,128)} %all_to_all.20.grad_hidden, f32[8,1152]{1,0:T(8,128)} %copy-done.29, f32[1,1152]{1,0:T(1,128)} %get-tuple-element.40.gain, f32[512,1]{1,0:T(8,128)} %copy-done.9, bf16[512,1152]{1,0:T(8,128)(2,1)} %layer_input.3, ...), custom_call_target="tpu_custom_call" | custom-call | flops 2566914048 | bytes 12000000 | tf_op jit(solution)/shard_map/pallas_call | solution.py:230
  (125 shorter events, 30.9 us)
Async XLA Ops:
  1.2 12.3 %collective-permute-start.1 = (bf16[128,1152]{1,0:T(8,128)(2,1)S(1)}, bf16[128,1152]{1,0:T(8,128)(2,1)}, u32[]{:S(2)}, u32[]{:S(2)}) collective-permute-start(bf16[128,1152]{1,0:T(8,128)(2,1)S(1)} %select_bitcast_fusion.1.one.refs_8_), channel_id=1, source_target_pairs={{0,4},{1,5},{2,6},{3,7},{8,0},{9,1},{10,2},{11,3},{16,8},{17,9},{1... | collective-permute-start | bytes 884744 | tf_op jit(solution)/shard_map/ppermute | solution.py:54
  4.2 11.3 %collective-permute-start = (bf16[128,1152]{1,0:T(8,128)(2,1)S(1)}, bf16[128,1152]{1,0:T(8,128)(2,1)}, u32[]{:S(2)}, u32[]{:S(2)}) collective-permute-start(bf16[128,1152]{1,0:T(8,128)(2,1)S(1)} %select_bitcast_fusion.1.one.refs_8_), channel_id=1, source_target_pairs={{0,8},{1,9},{2,10},{3,11},{8,16},{9,17},{10,18},{11,19},{16,24},{1... | collective-permute-start | bytes 884744 | tf_op jit(solution)/shard_map/ppermute | solution.py:54
  5.5 13.8 %collective-permute-start.3 = (bf16[144,1152]{1,0:T(8,128)(2,1)S(1)}, bf16[144,1152]{1,0:T(8,128)(2,1)S(1)}, u32[]{:S(2)}, u32[]{:S(2)}) collective-permute-start(bf16[144,1152]{1,0:T(8,128)(2,1)S(1)} %select_bitcast_fusion.two.refs_9_), channel_id=1, source_target_pairs={{0,4},{1,5},{2,6},{3,7},{8,0},{9,1},{10,2},{11,3},{16,8},{17,9},{1... | collective-permute-start | bytes 995336 | tf_op jit(solution)/shard_map/ppermute | solution.py:54
  7.4 13.8 %collective-permute-start.2 = (bf16[144,1152]{1,0:T(8,128)(2,1)S(1)}, bf16[144,1152]{1,0:T(8,128)(2,1)S(1)}, u32[]{:S(2)}, u32[]{:S(2)}) collective-permute-start(bf16[144,1152]{1,0:T(8,128)(2,1)S(1)} %select_bitcast_fusion.two.refs_9_), channel_id=1, source_target_pairs={{0,8},{1,9},{2,10},{3,11},{8,16},{9,17},{10,18},{11,19},{16,24},{1... | collective-permute-start | bytes 995336 | tf_op jit(solution)/shard_map/ppermute | solution.py:54
  8.5 65.5 %copy-start.9 = (f32[512,1]{1,0:T(8,128)}, f32[512,1]{1,0:T(8,128)S(1)}, u32[]{:S(2)}) copy-start(f32[512,1]{1,0:T(8,128)S(1)} %select_n.177.mask) | copy-start | bytes 6148
  8.6 57.6 %copy-start.31 = (s32[8]{0:T(128)}, s32[8]{0:T(128)S(1)}, u32[]{:S(2)}) copy-start(s32[8]{0:T(128)S(1)} %compare_select_fusion.2.block_of) | copy-start | bytes 100
  11.5 36.6 %copy-start.6 = (bf16[512,1152]{1,0:T(8,128)(2,1)}, bf16[512,1152]{1,0:T(8,128)(2,1)S(1)}, u32[]{:S(2)}) copy-start(bf16[512,1152]{1,0:T(8,128)(2,1)S(1)} %fusion.4.normed) | copy-start | bytes 3538948
  13.5 12.0 %collective-permute-start.5 = (bf16[128,1152]{1,0:T(8,128)(2,1)}, bf16[128,1152]{1,0:T(8,128)(2,1)S(1)}, u32[]{:S(2)}, u32[]{:S(2)}) collective-permute-start(bf16[128,1152]{1,0:T(8,128)(2,1)} %collective-permute-done.1.two.refs_11_), channel_id=1, source_target_pairs={{0,4},{1,5},{2,6},{3,7},{8,0},{9,1},{10,2},{11,3},{16,8},{17,9},{1... | collective-permute-start | bytes 884744 | tf_op jit(solution)/shard_map/ppermute | solution.py:54
  15.5 12.1 %collective-permute-start.4 = (bf16[128,1152]{1,0:T(8,128)(2,1)}, bf16[128,1152]{1,0:T(8,128)(2,1)S(1)}, u32[]{:S(2)}, u32[]{:S(2)}) collective-permute-start(bf16[128,1152]{1,0:T(8,128)(2,1)} %collective-permute-done.one.refs_10_), channel_id=1, source_target_pairs={{0,8},{1,9},{2,10},{3,11},{8,16},{9,17},{10,18},{11,19},{16,24},{1... | collective-permute-start | bytes 884744 | tf_op jit(solution)/shard_map/ppermute | solution.py:54
  19.2 13.4 %collective-permute-start.7 = (bf16[144,1152]{1,0:T(8,128)(2,1)S(1)}, bf16[144,1152]{1,0:T(8,128)(2,1)S(1)}, u32[]{:S(2)}, u32[]{:S(2)}) collective-permute-start(bf16[144,1152]{1,0:T(8,128)(2,1)S(1)} %collective-permute-done.3.two.refs_13_), channel_id=1, source_target_pairs={{0,4},{1,5},{2,6},{3,7},{8,0},{9,1},{10,2},{11,3},{16,8},{17,9},{1... | collective-permute-start | bytes 995336 | tf_op jit(solution)/shard_map/ppermute | solution.py:54
  21.3 13.4 %collective-permute-start.6 = (bf16[144,1152]{1,0:T(8,128)(2,1)S(1)}, bf16[144,1152]{1,0:T(8,128)(2,1)S(1)}, u32[]{:S(2)}, u32[]{:S(2)}) collective-permute-start(bf16[144,1152]{1,0:T(8,128)(2,1)S(1)} %collective-permute-done.2.one.refs_12_), channel_id=1, source_target_pairs={{0,8},{1,9},{2,10},{3,11},{8,16},{9,17},{10,18},{11,19},{16,24},{1... | collective-permute-start | bytes 995336 | tf_op jit(solution)/shard_map/ppermute | solution.py:54
  25.5 15.7 %collective-permute-start.9 = (bf16[128,1152]{1,0:T(8,128)(2,1)S(1)}, bf16[128,1152]{1,0:T(8,128)(2,1)S(1)}, u32[]{:S(2)}, u32[]{:S(2)}) collective-permute-start(bf16[128,1152]{1,0:T(8,128)(2,1)S(1)} %collective-permute-done.5.two.refs_15_), channel_id=1, source_target_pairs={{0,4},{1,5},{2,6},{3,7},{8,0},{9,1},{10,2},{11,3},{16,8},{17,9},{1... | collective-permute-start | bytes 884744 | tf_op jit(solution)/shard_map/ppermute | solution.py:54
  27.6 13.5 %collective-permute-start.8 = (bf16[128,1152]{1,0:T(8,128)(2,1)S(1)}, bf16[128,1152]{1,0:T(8,128)(2,1)}, u32[]{:S(2)}, u32[]{:S(2)}) collective-permute-start(bf16[128,1152]{1,0:T(8,128)(2,1)S(1)} %collective-permute-done.4.one.refs_14_), channel_id=1, source_target_pairs={{0,8},{1,9},{2,10},{3,11},{8,16},{9,17},{10,18},{11,19},{16,24},{1... | collective-permute-start | bytes 884744 | tf_op jit(solution)/shard_map/ppermute | solution.py:54
  32.7 12.6 %collective-permute-start.11 = (bf16[144,1152]{1,0:T(8,128)(2,1)S(1)}, bf16[144,1152]{1,0:T(8,128)(2,1)S(1)}, u32[]{:S(2)}, u32[]{:S(2)}) collective-permute-start(bf16[144,1152]{1,0:T(8,128)(2,1)S(1)} %collective-permute-done.7.two.refs_17_), channel_id=1, source_target_pairs={{0,4},{1,5},{2,6},{3,7},{8,0},{9,1},{10,2},{11,3},{16,8},{17,9},{1... | collective-permute-start | bytes 995336 | tf_op jit(solution)/shard_map/ppermute | solution.py:54
  34.7 13.4 %collective-permute-start.10 = (bf16[144,1152]{1,0:T(8,128)(2,1)S(1)}, bf16[144,1152]{1,0:T(8,128)(2,1)S(1)}, u32[]{:S(2)}, u32[]{:S(2)}) collective-permute-start(bf16[144,1152]{1,0:T(8,128)(2,1)S(1)} %collective-permute-done.6.one.refs_16_), channel_id=1, source_target_pairs={{0,8},{1,9},{2,10},{3,11},{8,16},{9,17},{10,18},{11,19},{16,24},{1... | collective-permute-start | bytes 995336 | tf_op jit(solution)/shard_map/ppermute | solution.py:54
  41.1 15.0 %collective-permute-start.12 = (bf16[128,1152]{1,0:T(8,128)(2,1)}, bf16[128,1152]{1,0:T(8,128)(2,1)}, u32[]{:S(2)}, u32[]{:S(2)}) collective-permute-start(bf16[128,1152]{1,0:T(8,128)(2,1)} %collective-permute-done.8.one.refs_18_), channel_id=1, source_target_pairs={{0,8},{1,9},{2,10},{3,11},{8,16},{9,17},{10,18},{11,19},{16,24},{1... | collective-permute-start | bytes 884744 | tf_op jit(solution)/shard_map/ppermute | solution.py:54
  45.3 10.9 %collective-permute-start.13 = (bf16[144,1152]{1,0:T(8,128)(2,1)S(1)}, bf16[144,1152]{1,0:T(8,128)(2,1)S(1)}, u32[]{:S(2)}, u32[]{:S(2)}) collective-permute-start(bf16[144,1152]{1,0:T(8,128)(2,1)S(1)} %collective-permute-done.11.two.refs_1_.refs_21_), channel_id=1, source_target_pairs={{0,4},{1,5},{2,6},{3,7},{8,0},{9,1},{10,2},{11,3},{16,8},{17,9},{1... | collective-permute-start | bytes 995336 | tf_op jit(solution)/shard_map/ppermute | solution.py:54
  51.2 13.6 %all-to-all-start = ((f32[8,8,272]{2,1,0:T(8,128)}), f32[8,8,272]{2,1,0:T(8,128)S(1)}, u32[]{:S(2)}, u32[]{:S(2)}) async-start(f32[8,8,272]{2,1,0:T(8,128)} %shard_map.88), calls=%async_computation | async-start | bytes 196608 | tf_op jit(solution)/shard_map/all_to_all | solution.py:441
  59.7 6.5 %collective-permute-start.14 = (f32[8,272]{1,0:T(8,128)S(1)}, f32[8,272]{1,0:T(8,128)S(1)}, u32[]{:S(2)}, u32[]{:S(2)}) collective-permute-start(f32[8,272]{1,0:T(8,128)S(1)} %shard_map.89), channel_id=1, source_target_pairs={{0,28},{1,29},{2,30},{3,31},{8,20},{9,21},{10,22},{11,23},{16,12},... | collective-permute-start | bytes 26120 | tf_op jit(solution)/shard_map/ppermute | solution.py:447
  64.6 35.1 %copy-start.30 = (s32[3]{0:T(128)}, s32[3]{0:T(128)S(1)}, u32[]{:S(2)}) copy-start(s32[3]{0:T(128)S(1)} %pad_add_fusion.flags) | copy-start | bytes 40
  67.8 14.5 %all-to-all-start.1 = ((bf16[32,2,1152]{2,1,0:T(2,128)(2,1)}), bf16[32,2,1152]{2,1,0:T(2,128)(2,1)}, u32[]{:S(2)}, u32[]{:S(2)}) async-start(bf16[32,2,1152]{2,1,0:T(2,128)(2,1)} %shard_map.90.refs_4_), calls=%async_computation.1 | async-start | bytes 294912 | tf_op jit(solution)/shard_map/all_to_all | solution.py:458
  79.8 31.7 %copy-start.2 = (bf16[512,384]{1,0:T(8,128)(2,1)}, bf16[512,384]{1,0:T(8,128)(2,1)S(1)}, u32[]{:S(2)}) copy-start(bf16[512,384]{1,0:T(8,128)(2,1)S(1)} %get-tuple-element.29.refs_0_.refs_6_) | copy-start | bytes 1179652
  79.8 31.7 %copy-start.3 = (bf16[512,384]{1,0:T(8,128)(2,1)}, bf16[512,384]{1,0:T(8,128)(2,1)S(1)}, u32[]{:S(2)}) copy-start(bf16[512,384]{1,0:T(8,128)(2,1)S(1)} %get-tuple-element.30.refs_1_.refs_7_) | copy-start | bytes 1179652
  84.1 15.4 %all-to-all-start.2 = ((bf16[32,4,1280]{2,1,0:T(4,128)(2,1)}), bf16[32,4,1280]{2,1,0:T(4,128)(2,1)S(1)}, u32[]{:S(2)}, u32[]{:S(2)}) async-start(bf16[32,4,1280]{2,1,0:T(4,128)(2,1)} %shard_map.92), calls=%async_computation.2 | async-start | bytes 655360 | tf_op jit(solution)/shard_map/all_to_all | solution.py:491
  (27 other events, 112.3 us)

commit v2 on v1

--- a/solution.py
+++ b/solution.py
@@ -128,23 +128,14 @@
     put_pool(held, block_of, parts, rest, pool_of(member, pre, gate) * share[...])
 
 
-def pool_kernel(parts, rest, block_of, before, share, member, normed, one, two, held):
-    pre, _, _, gate = project(rest, normed, one, two)
-    held[...] = before[...]
-    put_pool(held, block_of, parts, rest, pool_of(member, pre, gate) * share[...])
-
-
 def last_pool_kernel(rest, share, member, normed, one, two, pool_ref):
     pre, _, _, gate = project(rest, normed, one, two)
     pool_ref[...] = pool_of(member, pre, gate) * share[...]
 
 
-def late_slope_kernel(rests, mask, normed, *refs):
-    count = len(rests)
-    weights, slopes = refs[: 2 * count], refs[2 * count + 1 :]
-    for k, rest in enumerate(rests):
-        slope = slope_of(*project(rest, normed, weights[2 * k], weights[2 * k + 1]), mask)
-        slopes[k][:, : slope.shape[1]] = slope
+def late_slope_kernel(rest, mask, normed, one, two, after, slope_ref):
+    slope = slope_of(*project(rest, normed, one, two), mask)
+    slope_ref[:, : slope.shape[1]] = slope
 
 
 def backward_kernel(
@@ -410,7 +401,7 @@
                 **cost,
             )
             slopes.append(slope)
-        elif k < len(arrivals) - 2:
+        elif k < len(arrivals) - 1:
             slope, held = small_call(
                 functools.partial(forward_kernel, parts, rest),
                 (slope_shape, held_shape),
@@ -419,14 +410,6 @@
                 **cost,
             )
             slopes.append(slope)
-        elif k == len(arrivals) - 2:
-            held = small_call(
-                functools.partial(pool_kernel, parts, rest),
-                held_shape,
-                [block_of, held, *shared, *weights],
-                1,
-                **cost,
-            )
         else:
             last_pool = small_call(
                 functools.partial(last_pool_kernel, rest),
@@ -456,14 +439,17 @@
         ),
     )
     back = lax.all_to_all(partial, ("blk", "tower"), 0, 0)
-    slopes += small_call(
-        functools.partial(late_slope_kernel, [rest for _, rest, _ in arrivals[-2:]]),
-        (jax.ShapeDtypeStruct((row_count, 3 * SMALL), jnp.bfloat16),) * 2,
-        [row_mask, normed] + [w for _, _, pair_of in arrivals[-2:] for w in pair_of] + [partial],
-        0,
-        flops=int(1e9),
-        moved=int(4e6),
-        outside=1,
+    _, rest, (one, two) = arrivals[-1]
+    slopes.append(
+        small_call(
+            functools.partial(late_slope_kernel, rest),
+            jax.ShapeDtypeStruct((row_count, 3 * SMALL), jnp.bfloat16),
+            [row_mask, normed, one, two, partial],
+            0,
+            flops=int(1e9),
+            moved=int(4e6),
+            outside=1,
+        )
     )
 
     start = jnp.minimum(tower_index, groups - 2) * img_count
@@ -484,9 +470,9 @@
     copies = small_call(
         functools.partial(embed_kernel, groups),
         jax.ShapeDtypeStruct((devices, 2 * pair, width + 128), jnp.bfloat16),
-        [notes, back, *slopes[-2:]],
+        [notes, back, slopes[-1]],
         0,
-        outside=2,
+        outside=1,
     )
     packed = lax.all_to_all(copies, ("blk", "tower"), 0, 0)
     packed = packed.reshape(devices * 2 * pair, width + 128)

time: 121 us -> 119 us (0.983)
  local copies, waits for them, and re-layouts: 9.72 us -> 6.2 us
  waiting for transfers between devices: 26.1 us -> 28.6 us
    all_to_all x1, waiting for transfers between devices: 2.52 us -> 6.14 us  [ring_body(): back = lax.all_to_all(partial, ('blk', 'tower'), 0, 0)]
    unnamed x66 -> x48, local copies, waits for them, and re-layouts: 8.84 us -> 5.32 us
  transfers between devices with their start and end apart: 18 -> 18, of which waited for: 9 -> 9; matrix products, arithmetic and copies ran while one was open for 5% -> 5% of each run, Pallas kernels for 15% -> 16%
where the time goes in v2:
time: 119 us; the launch traced here: 118 us
  starting transfers between devices  33.5 us (28%)
  Pallas kernels  32.1 us (27%)
  waiting for transfers between devices  28.6 us (24%)
  blocking collectives  10.2 us (9%)
  local copies, waits for them, and re-layouts  6.2 us (5%)
  other arithmetic  5.89 us (5%)
  between operations  1.57 us (1%)
    pallas_call x12, Pallas kernels, small_call(): pl.pallas_call(kernel, in_specs=[scalar] * scalars + [whole] * (len(opera...  23.2 us
    ppermute x14, starting transfers between devices, move(): return lax.ppermute(value, ('blk', 'tower'), found)  15.3 us
    all_to_all x1, waiting for transfers between devices, ring_body(): packed = lax.all_to_all(copies, ('blk', 'tower'), 0, 0)  10.6 us
    ppermute x14, waiting for transfers between devices, move(): return lax.ppermute(value, ('blk', 'tower'), found)  10.5 us
    all_to_all x1, blocking collectives, ring_body(): grad_hidden = lax.all_to_all(grad_cols, 'blk', 0, 0)  10.2 us
    pallas_call x1, Pallas kernels, backward_call(): pl.pallas_call(functools.partial(backward_kernel, plan), grid=(row_count...  8.94 us
    all_to_all x1, waiting for transfers between devices, ring_body(): back = lax.all_to_all(partial, ('blk', 'tower'), 0, 0)  6.14 us
    all_to_all x1, starting transfers between devices, ring_body(): back = lax.all_to_all(partial, ('blk', 'tower'), 0, 0)  6 us
  transfers between devices with their start and end apart: 18, of which 9 were waited for; matrix products, arithmetic and copies ran while one was open for 5% of the time, Pallas kernels for 16%

profile of v2, /device:TPU:0, one launch (start us, length us, event | category | flops | bytes accessed | tf_op | source)
XLA Modules:
  0.0 118.0 jit_solution(12588615237742027689)
XLA Ops:
  1.2 3.0 %collective-permute-start.1 = (bf16[128,1152]{1,0:T(8,128)(2,1)S(1)}, bf16[128,1152]{1,0:T(8,128)(2,1)}, u32[]{:S(2)}, u32[]{:S(2)}) collective-permute-start(bf16[128,1152]{1,0:T(8,128)(2,1)S(1)} %select_bitcast_fusion.1.one.refs_8_), channel_id=1, source_target_pairs={{0,4},{1,5},{2,6},{3,7},{8,0},{9,1},{10,2},{11,3},{16,8},{17,9},{1... | collective-permute-start | bytes 884744 | tf_op jit(solution)/shard_map/ppermute | solution.py:54
  5.5 2.0 %collective-permute-start.3 = (bf16[144,1152]{1,0:T(8,128)(2,1)S(1)}, bf16[144,1152]{1,0:T(8,128)(2,1)}, u32[]{:S(2)}, u32[]{:S(2)}) collective-permute-start(bf16[144,1152]{1,0:T(8,128)(2,1)S(1)} %select_bitcast_fusion.two.refs_9_), channel_id=1, source_target_pairs={{0,4},{1,5},{2,6},{3,7},{8,0},{9,1},{10,2},{11,3},{16,8},{17,9},{1... | collective-permute-start | bytes 995336 | tf_op jit(solution)/shard_map/ppermute | solution.py:54
  11.6 2.0 %shard_map.82 = (bf16[512,384]{1,0:T(8,128)(2,1)S(1)}, f32[8,8,272]{2,1,0:T(8,128)S(1)}, f32[8,1152]{1,0:T(8,128)S(1)}) custom-call(s32[8]{0:T(128)S(1)} %compare_select_fusion.2.block_of, bf16[512,1152]{1,0:T(8,128)(2,1)S(1)} %copy-done, f32[8,1]{1,0:T(8,128)S(1)} %copy.39.share, bf16[8,512]{1,0:T(8,128)(2,1)S(1)} %select_convert_fusion.member, ...), custom_call_target="tpu_custom_call" | custom-call | flops 4000000000 | bytes 16000000 | tf_op jit(solution)/shard_map/pallas_call | solution.py:334
  14.3 1.9 %collective-permute-start.5 = (bf16[128,1152]{1,0:T(8,128)(2,1)}, bf16[128,1152]{1,0:T(8,128)(2,1)S(1)}, u32[]{:S(2)}, u32[]{:S(2)}) collective-permute-start(bf16[128,1152]{1,0:T(8,128)(2,1)} %collective-permute-done.1.two.refs_11_), channel_id=1, source_target_pairs={{0,4},{1,5},{2,6},{3,7},{8,0},{9,1},{10,2},{11,3},{16,8},{17,9},{1... | collective-permute-start | bytes 884744 | tf_op jit(solution)/shard_map/ppermute | solution.py:54
  16.3 1.9 %shard_map.83 = (bf16[512,256]{1,0:T(8,128)(2,1)S(1)}, f32[8,8,272]{2,1,0:T(8,128)S(1)}) custom-call(s32[8]{0:T(128)S(1)} %compare_select_fusion.2.block_of, f32[8,8,272]{2,1,0:T(8,128)S(1)} %get-tuple-element.23.before, f32[8,1]{1,0:T(8,128)S(1)} %copy.39.share, bf16[8,512]{1,0:T(8,128)(2,1)S(1)} %select_convert_fusion.member, ...), custom_call_target="tpu_custom_call" | custom-call | flops 4000000000 | bytes 16000000 | tf_op jit(solution)/shard_map/pallas_call | solution.py:334
  19.3 2.0 %collective-permute-start.7 = (bf16[144,1152]{1,0:T(8,128)(2,1)}, bf16[144,1152]{1,0:T(8,128)(2,1)S(1)}, u32[]{:S(2)}, u32[]{:S(2)}) collective-permute-start(bf16[144,1152]{1,0:T(8,128)(2,1)} %collective-permute-done.3.two.refs_13_), channel_id=1, source_target_pairs={{0,4},{1,5},{2,6},{3,7},{8,0},{9,1},{10,2},{11,3},{16,8},{17,9},{1... | collective-permute-start | bytes 995336 | tf_op jit(solution)/shard_map/ppermute | solution.py:54
  21.5 2.4 %shard_map.84 = (bf16[512,384]{1,0:T(8,128)(2,1)S(1)}, f32[8,8,272]{2,1,0:T(8,128)S(1)}) custom-call(s32[8]{0:T(128)S(1)} %compare_select_fusion.2.block_of, f32[8,8,272]{2,1,0:T(8,128)S(1)} %get-tuple-element.24.before, f32[8,1]{1,0:T(8,128)S(1)} %copy.39.share, bf16[8,512]{1,0:T(8,128)(2,1)S(1)} %select_convert_fusion.member, ...), custom_call_target="tpu_custom_call" | custom-call | flops 4000000000 | bytes 16000000 | tf_op jit(solution)/shard_map/pallas_call | solution.py:334
  25.5 2.0 %collective-permute-start.9 = (bf16[128,1152]{1,0:T(8,128)(2,1)S(1)}, bf16[128,1152]{1,0:T(8,128)(2,1)S(1)}, u32[]{:S(2)}, u32[]{:S(2)}) collective-permute-start(bf16[128,1152]{1,0:T(8,128)(2,1)S(1)} %collective-permute-done.5.two.refs_15_), channel_id=1, source_target_pairs={{0,4},{1,5},{2,6},{3,7},{8,0},{9,1},{10,2},{11,3},{16,8},{17,9},{1... | collective-permute-start | bytes 884744 | tf_op jit(solution)/shard_map/ppermute | solution.py:54
  29.8 2.8 %collective-permute-done.7.two.refs_17_ = bf16[144,1152]{1,0:T(8,128)(2,1)S(1)} collective-permute-done((bf16[144,1152]{1,0:T(8,128)(2,1)}, bf16[144,1152]{1,0:T(8,128)(2,1)S(1)}, u32[]{:S(2)}, u32[]{:S(2)}) %collective-permute-start.7) | collective-permute-done | bytes 331808 | tf_op jit(solution)/shard_map/ppermute | solution.py:54
  32.7 2.0 %collective-permute-start.11 = (bf16[144,1152]{1,0:T(8,128)(2,1)S(1)}, bf16[144,1152]{1,0:T(8,128)(2,1)}, u32[]{:S(2)}, u32[]{:S(2)}) collective-permute-start(bf16[144,1152]{1,0:T(8,128)(2,1)S(1)} %collective-permute-done.7.two.refs_17_), channel_id=1, source_target_pairs={{0,4},{1,5},{2,6},{3,7},{8,0},{9,1},{10,2},{11,3},{16,8},{17,9},{1... | collective-permute-start | bytes 995336 | tf_op jit(solution)/shard_map/ppermute | solution.py:54
  34.8 1.9 %shard_map.86 = (bf16[512,384]{1,0:T(8,128)(2,1)S(1)}, f32[8,8,272]{2,1,0:T(8,128)S(1)}) custom-call(s32[8]{0:T(128)S(1)} %compare_select_fusion.2.block_of, f32[8,8,272]{2,1,0:T(8,128)S(1)} %get-tuple-element.26.before, f32[8,1]{1,0:T(8,128)S(1)} %copy.39.share, bf16[8,512]{1,0:T(8,128)(2,1)S(1)} %select_convert_fusion.member, ...), custom_call_target="tpu_custom_call" | custom-call | flops 4000000000 | bytes 16000000 | tf_op jit(solution)/shard_map/pallas_call | solution.py:334
  37.4 3.7 %collective-permute-done.8.one.refs_18_ = bf16[128,1152]{1,0:T(8,128)(2,1)} collective-permute-done((bf16[128,1152]{1,0:T(8,128)(2,1)S(1)}, bf16[128,1152]{1,0:T(8,128)(2,1)}, u32[]{:S(2)}, u32[]{:S(2)}) %collective-permute-start.8) | collective-permute-done | bytes 294944 | tf_op jit(solution)/shard_map/ppermute | solution.py:54
  41.2 1.9 %shard_map.87 = (bf16[512,256]{1,0:T(8,128)(2,1)S(1)}, f32[8,8,272]{2,1,0:T(8,128)S(1)}) custom-call(s32[8]{0:T(128)S(1)} %compare_select_fusion.2.block_of, f32[8,8,272]{2,1,0:T(8,128)S(1)} %get-tuple-element.27.before, f32[8,1]{1,0:T(8,128)S(1)} %copy.39.share, bf16[8,512]{1,0:T(8,128)(2,1)S(1)} %select_convert_fusion.member, ...), custom_call_target="tpu_custom_call" | custom-call | flops 4000000000 | bytes 16000000 | tf_op jit(solution)/shard_map/pallas_call | solution.py:334
  48.1 3.1 %shard_map.88 = (bf16[512,384]{1,0:T(8,128)(2,1)S(1)}, f32[8,8,272]{2,1,0:T(8,128)}) custom-call(s32[8]{0:T(128)S(1)} %compare_select_fusion.2.block_of, f32[8,8,272]{2,1,0:T(8,128)S(1)} %get-tuple-element.28.before, f32[8,1]{1,0:T(8,128)S(1)} %copy.39.share, bf16[8,512]{1,0:T(8,128)(2,1)S(1)} %select_convert_fusion.member, f32[512,1]{1,0:T(8,128)S(1)} %select_n.177.mask, ...), custom_call_target="tpu_custom_call" | custom-call | flops 4000000000 | bytes 16000000 | tf_op jit(solution)/shard_map/pallas_call | solution.py:334
  52.0 4.9 %all-to-all-start = ((f32[8,8,272]{2,1,0:T(8,128)}), f32[8,8,272]{2,1,0:T(8,128)S(1)}, u32[]{:S(2)}, u32[]{:S(2)}) async-start(f32[8,8,272]{2,1,0:T(8,128)} %get-tuple-element.29), calls=%async_computation | async-start | bytes 196608 | tf_op jit(solution)/shard_map/all_to_all | solution.py:424
  56.9 2.2 %shard_map.89 = f32[8,272]{1,0:T(8,128)S(1)} custom-call(f32[8,1]{1,0:T(8,128)S(1)} %copy.39.share, bf16[8,512]{1,0:T(8,128)(2,1)S(1)} %select_convert_fusion.member, bf16[512,1152]{1,0:T(8,128)(2,1)S(1)} %fusion.4.normed, bf16[128,1152]{1,0:T(8,128)(2,1)} %collective-permute-done.12.one.refs_22_, bf16[144,1152]{1,0:T(8,128)(2,1)} %collective-permute-done.13.two.refs_23_), custom_call_target="tpu_custom_call" | custom-call | flops 4000000000 | bytes 16000000 | tf_op jit(solution)/shard_map/pallas_call | solution.py:334
  59.2 4.8 %collective-permute-start.14 = (f32[8,272]{1,0:T(8,128)S(1)}, f32[8,272]{1,0:T(8,128)S(1)}, u32[]{:S(2)}, u32[]{:S(2)}) collective-permute-start(f32[8,272]{1,0:T(8,128)S(1)} %shard_map.89), channel_id=1, source_target_pairs={{0,28},{1,29},{2,30},{3,31},{8,20},{9,21},{10,22},{11,23},{16,12},... | collective-permute-start | bytes 26120 | tf_op jit(solution)/shard_map/ppermute | solution.py:430
  67.2 6.0 %all-to-all-start.1 = ((bf16[32,2,1152]{2,1,0:T(2,128)(2,1)}), bf16[32,2,1152]{2,1,0:T(2,128)(2,1)S(1)}, u32[]{:S(2)}, u32[]{:S(2)}) async-start(bf16[32,2,1152]{2,1,0:T(2,128)(2,1)} %shard_map.90.after), calls=%async_computation.1 | async-start | bytes 294912 | tf_op jit(solution)/shard_map/all_to_all | solution.py:441
  73.3 2.2 %shard_map.91.refs_0_.refs_7_ = bf16[512,384]{1,0:T(8,128)(2,1)S(1)} custom-call(f32[512,1]{1,0:T(8,128)S(1)} %copy-done.6, bf16[512,1152]{1,0:T(8,128)(2,1)S(1)} %fusion.4.normed, bf16[128,1152]{1,0:T(8,128)(2,1)} %collective-permute-done.12.one.refs_22_, bf16[144,1152]{1,0:T(8,128)(2,1)} %collective-permute-done.13.two.refs_23_, ...), custom_call_target="tpu_custom_call" | custom-call | flops 1000000000 | bytes 4000000 | tf_op jit(solution)/shard_map/pallas_call | solution.py:334
  75.5 6.1 %all-to-all-done.1.back = bf16[32,2,1152]{2,1,0:T(2,128)(2,1)S(1)} async-done(((bf16[32,2,1152]{2,1,0:T(2,128)(2,1)}), bf16[32,2,1152]{2,1,0:T(2,128)(2,1)S(1)}, u32[]{:S(2)}, u32[]{:S(2)}) %all-to-all-start.1) | async-done | bytes 147488 | tf_op jit(solution)/shard_map/all_to_all | solution.py:441
  82.5 2.6 %all-to-all-start.2 = ((bf16[32,4,1280]{2,1,0:T(4,128)(2,1)}), bf16[32,4,1280]{2,1,0:T(4,128)(2,1)S(1)}, u32[]{:S(2)}, u32[]{:S(2)}) async-start(bf16[32,4,1280]{2,1,0:T(4,128)(2,1)} %shard_map.92), calls=%async_computation.2 | async-start | bytes 655360 | tf_op jit(solution)/shard_map/all_to_all | solution.py:477
  86.5 10.6 %all-to-all-done.2 = bf16[32,4,1280]{2,1,0:T(4,128)(2,1)S(1)} async-done(((bf16[32,4,1280]{2,1,0:T(4,128)(2,1)}), bf16[32,4,1280]{2,1,0:T(4,128)(2,1)S(1)}, u32[]{:S(2)}, u32[]{:S(2)}) %all-to-all-start.2) | async-done | bytes 327712 | tf_op jit(solution)/shard_map/all_to_all | solution.py:477
  98.9 10.2 %all_to_all.20.grad_hidden = f32[8,8,272]{2,1,0:T(8,128)} all-to-all(f32[8,8,272]{2,1,0:T(8,128)S(1)} %get-tuple-element.30), channel_id=1, replica_groups=mesh['blk'=8,'tower'=4] {'blk'}, dimensions={0} | all-to-all | bytes 139264 | tf_op jit(solution)/shard_map/all_to_all | solution.py:489
  109.1 8.9 %shard_map.94 = f32[512,1152]{1,0:T(8,128)} custom-call(s32[3]{0:T(128)} %copy-done.21, s32[8]{0:T(128)} %copy-done.22, f32[8,8,272]{2,1,0:T(8,128)} %all_to_all.20.grad_hidden, f32[8,1152]{1,0:T(8,128)} %copy-done.20, f32[1,1152]{1,0:T(1,128)} %get-tuple-element.40.gain, f32[512,1]{1,0:T(8,128)} %copy-done.5, bf16[512,1152]{1,0:T(8,128)(2,1)} %layer_input.3, ...), custom_call_target="tpu_custom_call" | custom-call | flops 2566914048 | bytes 12000000 | tf_op jit(solution)/shard_map/pallas_call | solution.py:221
  (107 shorter events, 25.3 us)
Async XLA Ops:
  0.0 10.5 %copy-start.23 = (f32[2,1152]{1,0:T(2,128)S(1)}, f32[2,1152]{1,0:T(2,128)}, u32[]{:S(2)}) copy-start(f32[2,1152]{1,0:T(2,128)} %param.11) | copy-start | bytes 27652
  1.2 13.1 %collective-permute-start.1 = (bf16[128,1152]{1,0:T(8,128)(2,1)S(1)}, bf16[128,1152]{1,0:T(8,128)(2,1)}, u32[]{:S(2)}, u32[]{:S(2)}) collective-permute-start(bf16[128,1152]{1,0:T(8,128)(2,1)S(1)} %select_bitcast_fusion.1.one.refs_8_), channel_id=1, source_target_pairs={{0,4},{1,5},{2,6},{3,7},{8,0},{9,1},{10,2},{11,3},{16,8},{17,9},{1... | collective-permute-start | bytes 884744 | tf_op jit(solution)/shard_map/ppermute | solution.py:54
  4.2 12.0 %collective-permute-start = (bf16[128,1152]{1,0:T(8,128)(2,1)S(1)}, bf16[128,1152]{1,0:T(8,128)(2,1)}, u32[]{:S(2)}, u32[]{:S(2)}) collective-permute-start(bf16[128,1152]{1,0:T(8,128)(2,1)S(1)} %select_bitcast_fusion.1.one.refs_8_), channel_id=1, source_target_pairs={{0,8},{1,9},{2,10},{3,11},{8,16},{9,17},{10,18},{11,19},{16,24},{1... | collective-permute-start | bytes 884744 | tf_op jit(solution)/shard_map/ppermute | solution.py:54
  5.5 13.9 %collective-permute-start.3 = (bf16[144,1152]{1,0:T(8,128)(2,1)S(1)}, bf16[144,1152]{1,0:T(8,128)(2,1)}, u32[]{:S(2)}, u32[]{:S(2)}) collective-permute-start(bf16[144,1152]{1,0:T(8,128)(2,1)S(1)} %select_bitcast_fusion.two.refs_9_), channel_id=1, source_target_pairs={{0,4},{1,5},{2,6},{3,7},{8,0},{9,1},{10,2},{11,3},{16,8},{17,9},{1... | collective-permute-start | bytes 995336 | tf_op jit(solution)/shard_map/ppermute | solution.py:54
  7.4 13.9 %collective-permute-start.2 = (bf16[144,1152]{1,0:T(8,128)(2,1)S(1)}, bf16[144,1152]{1,0:T(8,128)(2,1)}, u32[]{:S(2)}, u32[]{:S(2)}) collective-permute-start(bf16[144,1152]{1,0:T(8,128)(2,1)S(1)} %select_bitcast_fusion.two.refs_9_), channel_id=1, source_target_pairs={{0,8},{1,9},{2,10},{3,11},{8,16},{9,17},{10,18},{11,19},{16,24},{1... | collective-permute-start | bytes 995336 | tf_op jit(solution)/shard_map/ppermute | solution.py:54
  8.5 39.6 %copy-start.5 = (f32[512,1]{1,0:T(8,128)}, f32[512,1]{1,0:T(8,128)S(1)}, u32[]{:S(2)}) copy-start(f32[512,1]{1,0:T(8,128)S(1)} %select_n.177.mask) | copy-start | bytes 6148
  8.6 57.0 %copy-start.22 = (s32[8]{0:T(128)}, s32[8]{0:T(128)S(1)}, u32[]{:S(2)}) copy-start(s32[8]{0:T(128)S(1)} %compare_select_fusion.2.block_of) | copy-start | bytes 100
  14.3 11.3 %collective-permute-start.5 = (bf16[128,1152]{1,0:T(8,128)(2,1)}, bf16[128,1152]{1,0:T(8,128)(2,1)S(1)}, u32[]{:S(2)}, u32[]{:S(2)}) collective-permute-start(bf16[128,1152]{1,0:T(8,128)(2,1)} %collective-permute-done.1.two.refs_11_), channel_id=1, source_target_pairs={{0,4},{1,5},{2,6},{3,7},{8,0},{9,1},{10,2},{11,3},{16,8},{17,9},{1... | collective-permute-start | bytes 884744 | tf_op jit(solution)/shard_map/ppermute | solution.py:54
  16.2 11.4 %collective-permute-start.4 = (bf16[128,1152]{1,0:T(8,128)(2,1)}, bf16[128,1152]{1,0:T(8,128)(2,1)S(1)}, u32[]{:S(2)}, u32[]{:S(2)}) collective-permute-start(bf16[128,1152]{1,0:T(8,128)(2,1)} %collective-permute-done.one.refs_10_), channel_id=1, source_target_pairs={{0,8},{1,9},{2,10},{3,11},{8,16},{9,17},{10,18},{11,19},{16,24},{1... | collective-permute-start | bytes 884744 | tf_op jit(solution)/shard_map/ppermute | solution.py:54
  19.3 13.3 %collective-permute-start.7 = (bf16[144,1152]{1,0:T(8,128)(2,1)}, bf16[144,1152]{1,0:T(8,128)(2,1)S(1)}, u32[]{:S(2)}, u32[]{:S(2)}) collective-permute-start(bf16[144,1152]{1,0:T(8,128)(2,1)} %collective-permute-done.3.two.refs_13_), channel_id=1, source_target_pairs={{0,4},{1,5},{2,6},{3,7},{8,0},{9,1},{10,2},{11,3},{16,8},{17,9},{1... | collective-permute-start | bytes 995336 | tf_op jit(solution)/shard_map/ppermute | solution.py:54
  21.4 13.3 %collective-permute-start.6 = (bf16[144,1152]{1,0:T(8,128)(2,1)}, bf16[144,1152]{1,0:T(8,128)(2,1)S(1)}, u32[]{:S(2)}, u32[]{:S(2)}) collective-permute-start(bf16[144,1152]{1,0:T(8,128)(2,1)} %collective-permute-done.2.one.refs_12_), channel_id=1, source_target_pairs={{0,8},{1,9},{2,10},{3,11},{8,16},{9,17},{10,18},{11,19},{16,24},{1... | collective-permute-start | bytes 995336 | tf_op jit(solution)/shard_map/ppermute | solution.py:54
  25.5 15.7 %collective-permute-start.9 = (bf16[128,1152]{1,0:T(8,128)(2,1)S(1)}, bf16[128,1152]{1,0:T(8,128)(2,1)S(1)}, u32[]{:S(2)}, u32[]{:S(2)}) collective-permute-start(bf16[128,1152]{1,0:T(8,128)(2,1)S(1)} %collective-permute-done.5.two.refs_15_), channel_id=1, source_target_pairs={{0,4},{1,5},{2,6},{3,7},{8,0},{9,1},{10,2},{11,3},{16,8},{17,9},{1... | collective-permute-start | bytes 884744 | tf_op jit(solution)/shard_map/ppermute | solution.py:54
  27.6 13.5 %collective-permute-start.8 = (bf16[128,1152]{1,0:T(8,128)(2,1)S(1)}, bf16[128,1152]{1,0:T(8,128)(2,1)}, u32[]{:S(2)}, u32[]{:S(2)}) collective-permute-start(bf16[128,1152]{1,0:T(8,128)(2,1)S(1)} %collective-permute-done.4.one.refs_14_), channel_id=1, source_target_pairs={{0,8},{1,9},{2,10},{3,11},{8,16},{9,17},{10,18},{11,19},{16,24},{1... | collective-permute-start | bytes 884744 | tf_op jit(solution)/shard_map/ppermute | solution.py:54
  32.7 12.7 %collective-permute-start.11 = (bf16[144,1152]{1,0:T(8,128)(2,1)S(1)}, bf16[144,1152]{1,0:T(8,128)(2,1)}, u32[]{:S(2)}, u32[]{:S(2)}) collective-permute-start(bf16[144,1152]{1,0:T(8,128)(2,1)S(1)} %collective-permute-done.7.two.refs_17_), channel_id=1, source_target_pairs={{0,4},{1,5},{2,6},{3,7},{8,0},{9,1},{10,2},{11,3},{16,8},{17,9},{1... | collective-permute-start | bytes 995336 | tf_op jit(solution)/shard_map/ppermute | solution.py:54
  34.7 13.4 %collective-permute-start.10 = (bf16[144,1152]{1,0:T(8,128)(2,1)S(1)}, bf16[144,1152]{1,0:T(8,128)(2,1)S(1)}, u32[]{:S(2)}, u32[]{:S(2)}) collective-permute-start(bf16[144,1152]{1,0:T(8,128)(2,1)S(1)} %collective-permute-done.6.one.refs_16_), channel_id=1, source_target_pairs={{0,8},{1,9},{2,10},{3,11},{8,16},{9,17},{10,18},{11,19},{16,24},{1... | collective-permute-start | bytes 995336 | tf_op jit(solution)/shard_map/ppermute | solution.py:54
  41.1 15.8 %collective-permute-start.12 = (bf16[128,1152]{1,0:T(8,128)(2,1)}, bf16[128,1152]{1,0:T(8,128)(2,1)}, u32[]{:S(2)}, u32[]{:S(2)}) collective-permute-start(bf16[128,1152]{1,0:T(8,128)(2,1)} %collective-permute-done.8.one.refs_18_), channel_id=1, source_target_pairs={{0,8},{1,9},{2,10},{3,11},{8,16},{9,17},{10,18},{11,19},{16,24},{1... | collective-permute-start | bytes 884744 | tf_op jit(solution)/shard_map/ppermute | solution.py:54
  45.4 11.6 %collective-permute-start.13 = (bf16[144,1152]{1,0:T(8,128)(2,1)}, bf16[144,1152]{1,0:T(8,128)(2,1)}, u32[]{:S(2)}, u32[]{:S(2)}) collective-permute-start(bf16[144,1152]{1,0:T(8,128)(2,1)} %collective-permute-done.11.two.refs_21_), channel_id=1, source_target_pairs={{0,4},{1,5},{2,6},{3,7},{8,0},{9,1},{10,2},{11,3},{16,8},{17,9},{1... | collective-permute-start | bytes 995336 | tf_op jit(solution)/shard_map/ppermute | solution.py:54
  52.0 12.3 %all-to-all-start = ((f32[8,8,272]{2,1,0:T(8,128)}), f32[8,8,272]{2,1,0:T(8,128)S(1)}, u32[]{:S(2)}, u32[]{:S(2)}) async-start(f32[8,8,272]{2,1,0:T(8,128)} %get-tuple-element.29), calls=%async_computation | async-start | bytes 196608 | tf_op jit(solution)/shard_map/all_to_all | solution.py:424
  56.9 16.4 %copy-start.6 = (f32[512,1]{1,0:T(8,128)S(1)}, f32[512,1]{1,0:T(8,128)}, u32[]{:S(2)}) copy-start(f32[512,1]{1,0:T(8,128)} %copy-done.5) | copy-start | bytes 6148
  59.2 6.5 %collective-permute-start.14 = (f32[8,272]{1,0:T(8,128)S(1)}, f32[8,272]{1,0:T(8,128)S(1)}, u32[]{:S(2)}, u32[]{:S(2)}) collective-permute-start(f32[8,272]{1,0:T(8,128)S(1)} %shard_map.89), channel_id=1, source_target_pairs={{0,28},{1,29},{2,30},{3,31},{8,20},{9,21},{10,22},{11,23},{16,12},... | collective-permute-start | bytes 26120 | tf_op jit(solution)/shard_map/ppermute | solution.py:430
  64.0 33.2 %copy-start.21 = (s32[3]{0:T(128)}, s32[3]{0:T(128)S(1)}, u32[]{:S(2)}) copy-start(s32[3]{0:T(128)S(1)} %pad_add_fusion.flags) | copy-start | bytes 40
  67.2 14.4 %all-to-all-start.1 = ((bf16[32,2,1152]{2,1,0:T(2,128)(2,1)}), bf16[32,2,1152]{2,1,0:T(2,128)(2,1)S(1)}, u32[]{:S(2)}, u32[]{:S(2)}) async-start(bf16[32,2,1152]{2,1,0:T(2,128)(2,1)} %shard_map.90.after), calls=%async_computation.1 | async-start | bytes 294912 | tf_op jit(solution)/shard_map/all_to_all | solution.py:441
  75.5 33.5 %copy-start.2 = (bf16[512,384]{1,0:T(8,128)(2,1)}, bf16[512,384]{1,0:T(8,128)(2,1)S(1)}, u32[]{:S(2)}) copy-start(bf16[512,384]{1,0:T(8,128)(2,1)S(1)} %shard_map.91.refs_0_.refs_7_) | copy-start | bytes 1179652
  82.5 14.6 %all-to-all-start.2 = ((bf16[32,4,1280]{2,1,0:T(4,128)(2,1)}), bf16[32,4,1280]{2,1,0:T(4,128)(2,1)S(1)}, u32[]{:S(2)}, u32[]{:S(2)}) async-start(bf16[32,4,1280]{2,1,0:T(4,128)(2,1)} %shard_map.92), calls=%async_computation.2 | async-start | bytes 655360 | tf_op jit(solution)/shard_map/all_to_all | solution.py:477
  (18 other events, 66.1 us)

commit v3 on v2

--- a/solution.py
+++ b/solution.py
@@ -207,7 +207,7 @@
 
 def backward_call(flags, block_of, grad_hidden, own_row, mask, layer_input, gain, slopes, groups):
     row_count, width = layer_input.shape
-    tile = 2 * TEXT_LEN
+    tile = 4 * TEXT_LEN
     whole = pl.BlockSpec(memory_space=pltpu.VMEM)
     scalar = pl.BlockSpec(memory_space=pltpu.SMEM)
 

time: 119 us -> 119 us (level)
  no operation moved by 1% of the time
where the time goes in v3:
time: 119 us; the launch traced here: 118 us
  starting transfers between devices  33.7 us (28%)
  Pallas kernels  32.1 us (27%)
  waiting for transfers between devices  28.4 us (24%)
  blocking collectives  10.2 us (9%)
  local copies, waits for them, and re-layouts  6.2 us (5%)
  other arithmetic  5.89 us (5%)
  between operations  1.73 us (1%)
    pallas_call x12, Pallas kernels, small_call(): pl.pallas_call(kernel, in_specs=[scalar] * scalars + [whole] * (len(opera...  23.1 us
    ppermute x14, starting transfers between devices, move(): return lax.ppermute(value, ('blk', 'tower'), found)  15.3 us
    ppermute x14, waiting for transfers between devices, move(): return lax.ppermute(value, ('blk', 'tower'), found)  10.5 us
    all_to_all x1, waiting for transfers between devices, ring_body(): packed = lax.all_to_all(copies, ('blk', 'tower'), 0, 0)  10.4 us
    all_to_all x1, blocking collectives, ring_body(): grad_hidden = lax.all_to_all(grad_cols, 'blk', 0, 0)  10.2 us
    pallas_call x1, Pallas kernels, backward_call(): pl.pallas_call(functools.partial(backward_kernel, plan), grid=(row_count...  8.92 us
    all_to_all x1, waiting for transfers between devices, ring_body(): back = lax.all_to_all(partial, ('blk', 'tower'), 0, 0)  6.14 us
    all_to_all x1, starting transfers between devices, ring_body(): back = lax.all_to_all(partial, ('blk', 'tower'), 0, 0)  6 us
  transfers between devices with their start and end apart: 18, of which 9 were waited for; matrix products, arithmetic and copies ran while one was open for 5% of the time, Pallas kernels for 16%

profile of v3, /device:TPU:0, one launch (start us, length us, event | category | flops | bytes accessed | tf_op | source)
XLA Modules:
  0.0 118.1 jit_solution(13286620182384979171)
XLA Ops:
  1.2 3.0 %collective-permute-start.1 = (bf16[128,1152]{1,0:T(8,128)(2,1)S(1)}, bf16[128,1152]{1,0:T(8,128)(2,1)}, u32[]{:S(2)}, u32[]{:S(2)}) collective-permute-start(bf16[128,1152]{1,0:T(8,128)(2,1)S(1)} %select_bitcast_fusion.1.one.refs_8_), channel_id=1, source_target_pairs={{0,4},{1,5},{2,6},{3,7},{8,0},{9,1},{10,2},{11,3},{16,8},{17,9},{1... | collective-permute-start | bytes 884744 | tf_op jit(solution)/shard_map/ppermute | solution.py:54
  5.5 2.0 %collective-permute-start.3 = (bf16[144,1152]{1,0:T(8,128)(2,1)S(1)}, bf16[144,1152]{1,0:T(8,128)(2,1)}, u32[]{:S(2)}, u32[]{:S(2)}) collective-permute-start(bf16[144,1152]{1,0:T(8,128)(2,1)S(1)} %select_bitcast_fusion.two.refs_9_), channel_id=1, source_target_pairs={{0,4},{1,5},{2,6},{3,7},{8,0},{9,1},{10,2},{11,3},{16,8},{17,9},{1... | collective-permute-start | bytes 995336 | tf_op jit(solution)/shard_map/ppermute | solution.py:54
  11.6 2.0 %shard_map.82 = (bf16[512,384]{1,0:T(8,128)(2,1)S(1)}, f32[8,8,272]{2,1,0:T(8,128)S(1)}, f32[8,1152]{1,0:T(8,128)S(1)}) custom-call(s32[8]{0:T(128)S(1)} %compare_select_fusion.2.block_of, bf16[512,1152]{1,0:T(8,128)(2,1)S(1)} %copy-done, f32[8,1]{1,0:T(8,128)S(1)} %copy.39.share, bf16[8,512]{1,0:T(8,128)(2,1)S(1)} %select_convert_fusion.member, ...), custom_call_target="tpu_custom_call" | custom-call | flops 4000000000 | bytes 16000000 | tf_op jit(solution)/shard_map/pallas_call | solution.py:334
  14.3 1.9 %collective-permute-start.5 = (bf16[128,1152]{1,0:T(8,128)(2,1)}, bf16[128,1152]{1,0:T(8,128)(2,1)S(1)}, u32[]{:S(2)}, u32[]{:S(2)}) collective-permute-start(bf16[128,1152]{1,0:T(8,128)(2,1)} %collective-permute-done.1.two.refs_11_), channel_id=1, source_target_pairs={{0,4},{1,5},{2,6},{3,7},{8,0},{9,1},{10,2},{11,3},{16,8},{17,9},{1... | collective-permute-start | bytes 884744 | tf_op jit(solution)/shard_map/ppermute | solution.py:54
  16.3 1.9 %shard_map.83 = (bf16[512,256]{1,0:T(8,128)(2,1)S(1)}, f32[8,8,272]{2,1,0:T(8,128)S(1)}) custom-call(s32[8]{0:T(128)S(1)} %compare_select_fusion.2.block_of, f32[8,8,272]{2,1,0:T(8,128)S(1)} %get-tuple-element.23.before, f32[8,1]{1,0:T(8,128)S(1)} %copy.39.share, bf16[8,512]{1,0:T(8,128)(2,1)S(1)} %select_convert_fusion.member, ...), custom_call_target="tpu_custom_call" | custom-call | flops 4000000000 | bytes 16000000 | tf_op jit(solution)/shard_map/pallas_call | solution.py:334
  19.3 2.0 %collective-permute-start.7 = (bf16[144,1152]{1,0:T(8,128)(2,1)}, bf16[144,1152]{1,0:T(8,128)(2,1)S(1)}, u32[]{:S(2)}, u32[]{:S(2)}) collective-permute-start(bf16[144,1152]{1,0:T(8,128)(2,1)} %collective-permute-done.3.two.refs_13_), channel_id=1, source_target_pairs={{0,4},{1,5},{2,6},{3,7},{8,0},{9,1},{10,2},{11,3},{16,8},{17,9},{1... | collective-permute-start | bytes 995336 | tf_op jit(solution)/shard_map/ppermute | solution.py:54
  21.5 2.4 %shard_map.84 = (bf16[512,384]{1,0:T(8,128)(2,1)S(1)}, f32[8,8,272]{2,1,0:T(8,128)S(1)}) custom-call(s32[8]{0:T(128)S(1)} %compare_select_fusion.2.block_of, f32[8,8,272]{2,1,0:T(8,128)S(1)} %get-tuple-element.24.before, f32[8,1]{1,0:T(8,128)S(1)} %copy.39.share, bf16[8,512]{1,0:T(8,128)(2,1)S(1)} %select_convert_fusion.member, ...), custom_call_target="tpu_custom_call" | custom-call | flops 4000000000 | bytes 16000000 | tf_op jit(solution)/shard_map/pallas_call | solution.py:334
  25.5 2.0 %collective-permute-start.9 = (bf16[128,1152]{1,0:T(8,128)(2,1)S(1)}, bf16[128,1152]{1,0:T(8,128)(2,1)S(1)}, u32[]{:S(2)}, u32[]{:S(2)}) collective-permute-start(bf16[128,1152]{1,0:T(8,128)(2,1)S(1)} %collective-permute-done.5.two.refs_15_), channel_id=1, source_target_pairs={{0,4},{1,5},{2,6},{3,7},{8,0},{9,1},{10,2},{11,3},{16,8},{17,9},{1... | collective-permute-start | bytes 884744 | tf_op jit(solution)/shard_map/ppermute | solution.py:54
  29.8 2.9 %collective-permute-done.7.two.refs_17_ = bf16[144,1152]{1,0:T(8,128)(2,1)S(1)} collective-permute-done((bf16[144,1152]{1,0:T(8,128)(2,1)}, bf16[144,1152]{1,0:T(8,128)(2,1)S(1)}, u32[]{:S(2)}, u32[]{:S(2)}) %collective-permute-start.7) | collective-permute-done | bytes 331808 | tf_op jit(solution)/shard_map/ppermute | solution.py:54
  32.7 2.0 %collective-permute-start.11 = (bf16[144,1152]{1,0:T(8,128)(2,1)S(1)}, bf16[144,1152]{1,0:T(8,128)(2,1)}, u32[]{:S(2)}, u32[]{:S(2)}) collective-permute-start(bf16[144,1152]{1,0:T(8,128)(2,1)S(1)} %collective-permute-done.7.two.refs_17_), channel_id=1, source_target_pairs={{0,4},{1,5},{2,6},{3,7},{8,0},{9,1},{10,2},{11,3},{16,8},{17,9},{1... | collective-permute-start | bytes 995336 | tf_op jit(solution)/shard_map/ppermute | solution.py:54
  34.8 1.9 %shard_map.86 = (bf16[512,384]{1,0:T(8,128)(2,1)S(1)}, f32[8,8,272]{2,1,0:T(8,128)S(1)}) custom-call(s32[8]{0:T(128)S(1)} %compare_select_fusion.2.block_of, f32[8,8,272]{2,1,0:T(8,128)S(1)} %get-tuple-element.26.before, f32[8,1]{1,0:T(8,128)S(1)} %copy.39.share, bf16[8,512]{1,0:T(8,128)(2,1)S(1)} %select_convert_fusion.member, ...), custom_call_target="tpu_custom_call" | custom-call | flops 4000000000 | bytes 16000000 | tf_op jit(solution)/shard_map/pallas_call | solution.py:334
  37.4 3.7 %collective-permute-done.8.one.refs_18_ = bf16[128,1152]{1,0:T(8,128)(2,1)} collective-permute-done((bf16[128,1152]{1,0:T(8,128)(2,1)S(1)}, bf16[128,1152]{1,0:T(8,128)(2,1)}, u32[]{:S(2)}, u32[]{:S(2)}) %collective-permute-start.8) | collective-permute-done | bytes 294944 | tf_op jit(solution)/shard_map/ppermute | solution.py:54
  41.2 1.9 %shard_map.87 = (bf16[512,256]{1,0:T(8,128)(2,1)S(1)}, f32[8,8,272]{2,1,0:T(8,128)S(1)}) custom-call(s32[8]{0:T(128)S(1)} %compare_select_fusion.2.block_of, f32[8,8,272]{2,1,0:T(8,128)S(1)} %get-tuple-element.27.before, f32[8,1]{1,0:T(8,128)S(1)} %copy.39.share, bf16[8,512]{1,0:T(8,128)(2,1)S(1)} %select_convert_fusion.member, ...), custom_call_target="tpu_custom_call" | custom-call | flops 4000000000 | bytes 16000000 | tf_op jit(solution)/shard_map/pallas_call | solution.py:334
  48.1 3.1 %shard_map.88 = (bf16[512,384]{1,0:T(8,128)(2,1)S(1)}, f32[8,8,272]{2,1,0:T(8,128)}) custom-call(s32[8]{0:T(128)S(1)} %compare_select_fusion.2.block_of, f32[8,8,272]{2,1,0:T(8,128)S(1)} %get-tuple-element.28.before, f32[8,1]{1,0:T(8,128)S(1)} %copy.39.share, bf16[8,512]{1,0:T(8,128)(2,1)S(1)} %select_convert_fusion.member, f32[512,1]{1,0:T(8,128)S(1)} %select_n.177.mask, ...), custom_call_target="tpu_custom_call" | custom-call | flops 4000000000 | bytes 16000000 | tf_op jit(solution)/shard_map/pallas_call | solution.py:334
  52.0 4.9 %all-to-all-start = ((f32[8,8,272]{2,1,0:T(8,128)}), f32[8,8,272]{2,1,0:T(8,128)S(1)}, u32[]{:S(2)}, u32[]{:S(2)}) async-start(f32[8,8,272]{2,1,0:T(8,128)} %get-tuple-element.29), calls=%async_computation | async-start | bytes 196608 | tf_op jit(solution)/shard_map/all_to_all | solution.py:424
  56.9 2.2 %shard_map.89 = f32[8,272]{1,0:T(8,128)S(1)} custom-call(f32[8,1]{1,0:T(8,128)S(1)} %copy.39.share, bf16[8,512]{1,0:T(8,128)(2,1)S(1)} %select_convert_fusion.member, bf16[512,1152]{1,0:T(8,128)(2,1)S(1)} %fusion.4.normed, bf16[128,1152]{1,0:T(8,128)(2,1)} %collective-permute-done.12.one.refs_22_, bf16[144,1152]{1,0:T(8,128)(2,1)} %collective-permute-done.13.two.refs_23_), custom_call_target="tpu_custom_call" | custom-call | flops 4000000000 | bytes 16000000 | tf_op jit(solution)/shard_map/pallas_call | solution.py:334
  59.2 4.8 %collective-permute-start.14 = (f32[8,272]{1,0:T(8,128)S(1)}, f32[8,272]{1,0:T(8,128)S(1)}, u32[]{:S(2)}, u32[]{:S(2)}) collective-permute-start(f32[8,272]{1,0:T(8,128)S(1)} %shard_map.89), channel_id=1, source_target_pairs={{0,28},{1,29},{2,30},{3,31},{8,20},{9,21},{10,22},{11,23},{16,12},... | collective-permute-start | bytes 26120 | tf_op jit(solution)/shard_map/ppermute | solution.py:430
  67.2 6.0 %all-to-all-start.1 = ((bf16[32,2,1152]{2,1,0:T(2,128)(2,1)}), bf16[32,2,1152]{2,1,0:T(2,128)(2,1)S(1)}, u32[]{:S(2)}, u32[]{:S(2)}) async-start(bf16[32,2,1152]{2,1,0:T(2,128)(2,1)} %shard_map.90.after), calls=%async_computation.1 | async-start | bytes 294912 | tf_op jit(solution)/shard_map/all_to_all | solution.py:441
  73.3 2.2 %shard_map.91.refs_0_.refs_7_ = bf16[512,384]{1,0:T(8,128)(2,1)S(1)} custom-call(f32[512,1]{1,0:T(8,128)S(1)} %copy-done.6, bf16[512,1152]{1,0:T(8,128)(2,1)S(1)} %fusion.4.normed, bf16[128,1152]{1,0:T(8,128)(2,1)} %collective-permute-done.12.one.refs_22_, bf16[144,1152]{1,0:T(8,128)(2,1)} %collective-permute-done.13.two.refs_23_, ...), custom_call_target="tpu_custom_call" | custom-call | flops 1000000000 | bytes 4000000 | tf_op jit(solution)/shard_map/pallas_call | solution.py:334
  75.5 6.1 %all-to-all-done.1.back = bf16[32,2,1152]{2,1,0:T(2,128)(2,1)S(1)} async-done(((bf16[32,2,1152]{2,1,0:T(2,128)(2,1)}), bf16[32,2,1152]{2,1,0:T(2,128)(2,1)S(1)}, u32[]{:S(2)}, u32[]{:S(2)}) %all-to-all-start.1) | async-done | bytes 147488 | tf_op jit(solution)/shard_map/all_to_all | solution.py:441
  82.5 2.8 %all-to-all-start.2 = ((bf16[32,4,1280]{2,1,0:T(4,128)(2,1)}), bf16[32,4,1280]{2,1,0:T(4,128)(2,1)S(1)}, u32[]{:S(2)}, u32[]{:S(2)}) async-start(bf16[32,4,1280]{2,1,0:T(4,128)(2,1)} %shard_map.92), calls=%async_computation.2 | async-start | bytes 655360 | tf_op jit(solution)/shard_map/all_to_all | solution.py:477
  86.7 10.4 %all-to-all-done.2 = bf16[32,4,1280]{2,1,0:T(4,128)(2,1)S(1)} async-done(((bf16[32,4,1280]{2,1,0:T(4,128)(2,1)}), bf16[32,4,1280]{2,1,0:T(4,128)(2,1)S(1)}, u32[]{:S(2)}, u32[]{:S(2)}) %all-to-all-start.2) | async-done | bytes 327712 | tf_op jit(solution)/shard_map/all_to_all | solution.py:477
  98.9 10.2 %all_to_all.20.grad_hidden = f32[8,8,272]{2,1,0:T(8,128)} all-to-all(f32[8,8,272]{2,1,0:T(8,128)S(1)} %get-tuple-element.30), channel_id=1, replica_groups=mesh['blk'=8,'tower'=4] {'blk'}, dimensions={0} | all-to-all | bytes 139264 | tf_op jit(solution)/shard_map/all_to_all | solution.py:489
  109.1 8.9 %shard_map.94 = f32[512,1152]{1,0:T(8,128)} custom-call(s32[3]{0:T(128)} %copy-done.21, s32[8]{0:T(128)} %copy-done.22, f32[8,8,272]{2,1,0:T(8,128)} %all_to_all.20.grad_hidden, f32[8,1152]{1,0:T(8,128)} %copy-done.20, f32[1,1152]{1,0:T(1,128)} %get-tuple-element.40.gain, f32[512,1]{1,0:T(8,128)} %copy-done.5, bf16[512,1152]{1,0:T(8,128)(2,1)} %layer_input.3, ...), custom_call_target="tpu_custom_call" | custom-call | flops 2566914048 | bytes 12000000 | tf_op jit(solution)/shard_map/pallas_call | solution.py:221
  (107 shorter events, 25.2 us)
Async XLA Ops:
  0.0 10.5 %copy-start.23 = (f32[2,1152]{1,0:T(2,128)S(1)}, f32[2,1152]{1,0:T(2,128)}, u32[]{:S(2)}) copy-start(f32[2,1152]{1,0:T(2,128)} %param.11) | copy-start | bytes 27652
  1.2 13.1 %collective-permute-start.1 = (bf16[128,1152]{1,0:T(8,128)(2,1)S(1)}, bf16[128,1152]{1,0:T(8,128)(2,1)}, u32[]{:S(2)}, u32[]{:S(2)}) collective-permute-start(bf16[128,1152]{1,0:T(8,128)(2,1)S(1)} %select_bitcast_fusion.1.one.refs_8_), channel_id=1, source_target_pairs={{0,4},{1,5},{2,6},{3,7},{8,0},{9,1},{10,2},{11,3},{16,8},{17,9},{1... | collective-permute-start | bytes 884744 | tf_op jit(solution)/shard_map/ppermute | solution.py:54
  4.2 12.0 %collective-permute-start = (bf16[128,1152]{1,0:T(8,128)(2,1)S(1)}, bf16[128,1152]{1,0:T(8,128)(2,1)}, u32[]{:S(2)}, u32[]{:S(2)}) collective-permute-start(bf16[128,1152]{1,0:T(8,128)(2,1)S(1)} %select_bitcast_fusion.1.one.refs_8_), channel_id=1, source_target_pairs={{0,8},{1,9},{2,10},{3,11},{8,16},{9,17},{10,18},{11,19},{16,24},{1... | collective-permute-start | bytes 884744 | tf_op jit(solution)/shard_map/ppermute | solution.py:54
  5.5 13.9 %collective-permute-start.3 = (bf16[144,1152]{1,0:T(8,128)(2,1)S(1)}, bf16[144,1152]{1,0:T(8,128)(2,1)}, u32[]{:S(2)}, u32[]{:S(2)}) collective-permute-start(bf16[144,1152]{1,0:T(8,128)(2,1)S(1)} %select_bitcast_fusion.two.refs_9_), channel_id=1, source_target_pairs={{0,4},{1,5},{2,6},{3,7},{8,0},{9,1},{10,2},{11,3},{16,8},{17,9},{1... | collective-permute-start | bytes 995336 | tf_op jit(solution)/shard_map/ppermute | solution.py:54
  7.4 13.9 %collective-permute-start.2 = (bf16[144,1152]{1,0:T(8,128)(2,1)S(1)}, bf16[144,1152]{1,0:T(8,128)(2,1)}, u32[]{:S(2)}, u32[]{:S(2)}) collective-permute-start(bf16[144,1152]{1,0:T(8,128)(2,1)S(1)} %select_bitcast_fusion.two.refs_9_), channel_id=1, source_target_pairs={{0,8},{1,9},{2,10},{3,11},{8,16},{9,17},{10,18},{11,19},{16,24},{1... | collective-permute-start | bytes 995336 | tf_op jit(solution)/shard_map/ppermute | solution.py:54
  8.5 39.6 %copy-start.5 = (f32[512,1]{1,0:T(8,128)}, f32[512,1]{1,0:T(8,128)S(1)}, u32[]{:S(2)}) copy-start(f32[512,1]{1,0:T(8,128)S(1)} %select_n.177.mask) | copy-start | bytes 6148
  8.6 57.0 %copy-start.22 = (s32[8]{0:T(128)}, s32[8]{0:T(128)S(1)}, u32[]{:S(2)}) copy-start(s32[8]{0:T(128)S(1)} %compare_select_fusion.2.block_of) | copy-start | bytes 100
  14.3 11.3 %collective-permute-start.5 = (bf16[128,1152]{1,0:T(8,128)(2,1)}, bf16[128,1152]{1,0:T(8,128)(2,1)S(1)}, u32[]{:S(2)}, u32[]{:S(2)}) collective-permute-start(bf16[128,1152]{1,0:T(8,128)(2,1)} %collective-permute-done.1.two.refs_11_), channel_id=1, source_target_pairs={{0,4},{1,5},{2,6},{3,7},{8,0},{9,1},{10,2},{11,3},{16,8},{17,9},{1... | collective-permute-start | bytes 884744 | tf_op jit(solution)/shard_map/ppermute | solution.py:54
  16.2 11.4 %collective-permute-start.4 = (bf16[128,1152]{1,0:T(8,128)(2,1)}, bf16[128,1152]{1,0:T(8,128)(2,1)S(1)}, u32[]{:S(2)}, u32[]{:S(2)}) collective-permute-start(bf16[128,1152]{1,0:T(8,128)(2,1)} %collective-permute-done.one.refs_10_), channel_id=1, source_target_pairs={{0,8},{1,9},{2,10},{3,11},{8,16},{9,17},{10,18},{11,19},{16,24},{1... | collective-permute-start | bytes 884744 | tf_op jit(solution)/shard_map/ppermute | solution.py:54
  19.3 13.3 %collective-permute-start.7 = (bf16[144,1152]{1,0:T(8,128)(2,1)}, bf16[144,1152]{1,0:T(8,128)(2,1)S(1)}, u32[]{:S(2)}, u32[]{:S(2)}) collective-permute-start(bf16[144,1152]{1,0:T(8,128)(2,1)} %collective-permute-done.3.two.refs_13_), channel_id=1, source_target_pairs={{0,4},{1,5},{2,6},{3,7},{8,0},{9,1},{10,2},{11,3},{16,8},{17,9},{1... | collective-permute-start | bytes 995336 | tf_op jit(solution)/shard_map/ppermute | solution.py:54
  21.4 13.3 %collective-permute-start.6 = (bf16[144,1152]{1,0:T(8,128)(2,1)}, bf16[144,1152]{1,0:T(8,128)(2,1)S(1)}, u32[]{:S(2)}, u32[]{:S(2)}) collective-permute-start(bf16[144,1152]{1,0:T(8,128)(2,1)} %collective-permute-done.2.one.refs_12_), channel_id=1, source_target_pairs={{0,8},{1,9},{2,10},{3,11},{8,16},{9,17},{10,18},{11,19},{16,24},{1... | collective-permute-start | bytes 995336 | tf_op jit(solution)/shard_map/ppermute | solution.py:54
  25.5 15.7 %collective-permute-start.9 = (bf16[128,1152]{1,0:T(8,128)(2,1)S(1)}, bf16[128,1152]{1,0:T(8,128)(2,1)S(1)}, u32[]{:S(2)}, u32[]{:S(2)}) collective-permute-start(bf16[128,1152]{1,0:T(8,128)(2,1)S(1)} %collective-permute-done.5.two.refs_15_), channel_id=1, source_target_pairs={{0,4},{1,5},{2,6},{3,7},{8,0},{9,1},{10,2},{11,3},{16,8},{17,9},{1... | collective-permute-start | bytes 884744 | tf_op jit(solution)/shard_map/ppermute | solution.py:54
  27.6 13.5 %collective-permute-start.8 = (bf16[128,1152]{1,0:T(8,128)(2,1)S(1)}, bf16[128,1152]{1,0:T(8,128)(2,1)}, u32[]{:S(2)}, u32[]{:S(2)}) collective-permute-start(bf16[128,1152]{1,0:T(8,128)(2,1)S(1)} %collective-permute-done.4.one.refs_14_), channel_id=1, source_target_pairs={{0,8},{1,9},{2,10},{3,11},{8,16},{9,17},{10,18},{11,19},{16,24},{1... | collective-permute-start | bytes 884744 | tf_op jit(solution)/shard_map/ppermute | solution.py:54
  32.7 12.7 %collective-permute-start.11 = (bf16[144,1152]{1,0:T(8,128)(2,1)S(1)}, bf16[144,1152]{1,0:T(8,128)(2,1)}, u32[]{:S(2)}, u32[]{:S(2)}) collective-permute-start(bf16[144,1152]{1,0:T(8,128)(2,1)S(1)} %collective-permute-done.7.two.refs_17_), channel_id=1, source_target_pairs={{0,4},{1,5},{2,6},{3,7},{8,0},{9,1},{10,2},{11,3},{16,8},{17,9},{1... | collective-permute-start | bytes 995336 | tf_op jit(solution)/shard_map/ppermute | solution.py:54
  34.7 13.4 %collective-permute-start.10 = (bf16[144,1152]{1,0:T(8,128)(2,1)S(1)}, bf16[144,1152]{1,0:T(8,128)(2,1)S(1)}, u32[]{:S(2)}, u32[]{:S(2)}) collective-permute-start(bf16[144,1152]{1,0:T(8,128)(2,1)S(1)} %collective-permute-done.6.one.refs_16_), channel_id=1, source_target_pairs={{0,8},{1,9},{2,10},{3,11},{8,16},{9,17},{10,18},{11,19},{16,24},{1... | collective-permute-start | bytes 995336 | tf_op jit(solution)/shard_map/ppermute | solution.py:54
  41.1 15.8 %collective-permute-start.12 = (bf16[128,1152]{1,0:T(8,128)(2,1)}, bf16[128,1152]{1,0:T(8,128)(2,1)}, u32[]{:S(2)}, u32[]{:S(2)}) collective-permute-start(bf16[128,1152]{1,0:T(8,128)(2,1)} %collective-permute-done.8.one.refs_18_), channel_id=1, source_target_pairs={{0,8},{1,9},{2,10},{3,11},{8,16},{9,17},{10,18},{11,19},{16,24},{1... | collective-permute-start | bytes 884744 | tf_op jit(solution)/shard_map/ppermute | solution.py:54
  45.4 11.6 %collective-permute-start.13 = (bf16[144,1152]{1,0:T(8,128)(2,1)}, bf16[144,1152]{1,0:T(8,128)(2,1)}, u32[]{:S(2)}, u32[]{:S(2)}) collective-permute-start(bf16[144,1152]{1,0:T(8,128)(2,1)} %collective-permute-done.11.two.refs_21_), channel_id=1, source_target_pairs={{0,4},{1,5},{2,6},{3,7},{8,0},{9,1},{10,2},{11,3},{16,8},{17,9},{1... | collective-permute-start | bytes 995336 | tf_op jit(solution)/shard_map/ppermute | solution.py:54
  52.0 12.3 %all-to-all-start = ((f32[8,8,272]{2,1,0:T(8,128)}), f32[8,8,272]{2,1,0:T(8,128)S(1)}, u32[]{:S(2)}, u32[]{:S(2)}) async-start(f32[8,8,272]{2,1,0:T(8,128)} %get-tuple-element.29), calls=%async_computation | async-start | bytes 196608 | tf_op jit(solution)/shard_map/all_to_all | solution.py:424
  56.9 16.4 %copy-start.6 = (f32[512,1]{1,0:T(8,128)S(1)}, f32[512,1]{1,0:T(8,128)}, u32[]{:S(2)}) copy-start(f32[512,1]{1,0:T(8,128)} %copy-done.5) | copy-start | bytes 6148
  59.2 6.5 %collective-permute-start.14 = (f32[8,272]{1,0:T(8,128)S(1)}, f32[8,272]{1,0:T(8,128)S(1)}, u32[]{:S(2)}, u32[]{:S(2)}) collective-permute-start(f32[8,272]{1,0:T(8,128)S(1)} %shard_map.89), channel_id=1, source_target_pairs={{0,28},{1,29},{2,30},{3,31},{8,20},{9,21},{10,22},{11,23},{16,12},... | collective-permute-start | bytes 26120 | tf_op jit(solution)/shard_map/ppermute | solution.py:430
  64.0 33.2 %copy-start.21 = (s32[3]{0:T(128)}, s32[3]{0:T(128)S(1)}, u32[]{:S(2)}) copy-start(s32[3]{0:T(128)S(1)} %pad_add_fusion.flags) | copy-start | bytes 40
  67.2 14.4 %all-to-all-start.1 = ((bf16[32,2,1152]{2,1,0:T(2,128)(2,1)}), bf16[32,2,1152]{2,1,0:T(2,128)(2,1)S(1)}, u32[]{:S(2)}, u32[]{:S(2)}) async-start(bf16[32,2,1152]{2,1,0:T(2,128)(2,1)} %shard_map.90.after), calls=%async_computation.1 | async-start | bytes 294912 | tf_op jit(solution)/shard_map/all_to_all | solution.py:441
  75.5 33.5 %copy-start.2 = (bf16[512,384]{1,0:T(8,128)(2,1)}, bf16[512,384]{1,0:T(8,128)(2,1)S(1)}, u32[]{:S(2)}) copy-start(bf16[512,384]{1,0:T(8,128)(2,1)S(1)} %shard_map.91.refs_0_.refs_7_) | copy-start | bytes 1179652
  82.5 14.6 %all-to-all-start.2 = ((bf16[32,4,1280]{2,1,0:T(4,128)(2,1)}), bf16[32,4,1280]{2,1,0:T(4,128)(2,1)S(1)}, u32[]{:S(2)}, u32[]{:S(2)}) async-start(bf16[32,4,1280]{2,1,0:T(4,128)(2,1)} %shard_map.92), calls=%async_computation.2 | async-start | bytes 655360 | tf_op jit(solution)/shard_map/all_to_all | solution.py:477
  (18 other events, 66.1 us)

commit v4 on v2

--- a/solution.py
+++ b/solution.py
@@ -126,6 +126,19 @@
     slope_ref[:, : slope.shape[1]] = slope
     held[...] = before[...]
     put_pool(held, block_of, parts, rest, pool_of(member, pre, gate) * share[...])
+
+
+def edge_kernel(
+    rest, share, member, mask, normed, one, two, slope_ref, low_pool, high_pool
+):
+    pre, square, tanh_part, gate = project(rest, normed, one, two)
+    slope = slope_of(pre, square, tanh_part, gate, mask)
+    slope_ref[:, : slope.shape[1]] = slope
+    pool = pool_of(member, pre, gate) * share[...]
+    for k, ref in enumerate((low_pool, high_pool)):
+        start = 2 * SMALL + k * REST
+        ref[:, :SMALL] = pool[:, k * SMALL : (k + 1) * SMALL]
+        ref[:, SMALL:] = pool[:, start : start + REST]
 
 
 def last_pool_kernel(rest, share, member, normed, one, two, pool_ref):
@@ -245,10 +258,14 @@
     )
 
 
-def partial_kernel(flags, block_of, share, value_pool, mine, late, w_second, out, pools, rows):
+def partial_kernel(
+    flags, block_of, share, value_pool, mine, late, from_3, from_5, w_second, out, pools, rows
+):
     slots, shard = late.shape
     pools[...] = mine[...]
     pools[block_of[4]] = late[...]
+    pools[block_of[3], :, SMALL:] = from_3[...]
+    pools[block_of[5], :, SMALL:] = from_5[...]
     high, low = two_parts(pools[...].reshape(8 * slots, shard))
     second = w_second[flags[0]]
     both = jnp.dot(
@@ -401,12 +418,22 @@
                 **cost,
             )
             slopes.append(slope)
-        elif k < len(arrivals) - 1:
+        elif k < len(arrivals) - 2:
             slope, held = small_call(
                 functools.partial(forward_kernel, parts, rest),
                 (slope_shape, held_shape),
                 [block_of, held, *shared, row_mask, *weights],
                 1,
+                **cost,
+            )
+            slopes.append(slope)
+        elif k == len(arrivals) - 2:
+            edge_shape = jax.ShapeDtypeStruct((slots, SMALL + REST), jnp.float32)
+            slope, *edge_pools = small_call(
+                functools.partial(edge_kernel, rest),
+                (slope_shape, edge_shape, edge_shape),
+                [*shared, row_mask, *weights],
+                0,
                 **cost,
             )
             slopes.append(slope)
@@ -422,16 +449,21 @@
     devices = 8 * groups
     pair = slots // groups
     mine = lax.all_to_all(held, "blk", 0, 0)
-    opposite = []
-    for place in range(8):
-        for t in range(groups):
-            source = RING[place] * groups + t
-            opposite.append((source, RING[(place + 4) % 8] * groups + t))
-    late = lax.ppermute(last_pool, ("blk", "tower"), opposite)
+
+    def along_ring(value, step):
+        routes = []
+        for place in range(8):
+            for t in range(groups):
+                source = RING[place] * groups + t
+                routes.append((source, RING[(place + step) % 8] * groups + t))
+        return lax.ppermute(value, ("blk", "tower"), routes)
+
+    edges = [along_ring(pool, step) for pool, step in zip(edge_pools, (5, 3))]
+    late = along_ring(last_pool, 4)
     partial = small_call(
         partial_kernel,
         jax.ShapeDtypeStruct((devices, pair, width), jnp.bfloat16),
-        [flags, block_of, share, value_pool, mine, late, w_second],
+        [flags, block_of, share, value_pool, mine, late, *edges, w_second],
         2,
         (
             pltpu.VMEM((8, slots, shard), jnp.float32),

time: 119 us -> 119 us (level)
  waiting for transfers between devices: 28.6 us -> 24.5 us
  starting transfers between devices: 33.5 us -> 36.3 us
  local copies, waits for them, and re-layouts: 6.2 us -> 8.67 us
  Pallas kernels: 32.1 us -> 29.9 us
    ppermute x14, waiting for transfers between devices: 10.5 us -> 6.64 us  [move(): return lax.ppermute(value, ('blk', 'tower'), found)]
    ppermute x1 -> x3, starting transfers between devices: 4.77 us -> 8.06 us  [along_ring(): return lax.ppermute(value, ('blk', 'tower'), routes)]
    pallas_call x12, Pallas kernels: 23.2 us -> 21 us  [small_call(): pl.pallas_call(kernel, in_specs=[scalar] * scalars + [whole] * (len(opera...]
    unnamed x48 -> x74, local copies, waits for them, and re-layouts: 5.32 us -> 7.27 us
  transfers between devices with their start and end apart: 18 -> 20, of which waited for: 9 -> 8; matrix products, arithmetic and copies ran while one was open for 5% -> 6% of each run, Pallas kernels for 16% -> 14%
where the time goes in v4:
time: 119 us; the launch traced here: 118 us
  starting transfers between devices  36.3 us (31%)
  Pallas kernels  29.9 us (25%)
  waiting for transfers between devices  24.5 us (21%)
  blocking collectives  10.2 us (9%)
  local copies, waits for them, and re-layouts  8.67 us (7%)
  other arithmetic  6.94 us (6%)
  between operations  1.61 us (1%)
    pallas_call x12, Pallas kernels, small_call(): pl.pallas_call(kernel, in_specs=[scalar] * scalars + [whole] * (len(opera...  21 us
    ppermute x14, starting transfers between devices, move(): return lax.ppermute(value, ('blk', 'tower'), found)  15.4 us
    all_to_all x1, waiting for transfers between devices, ring_body(): packed = lax.all_to_all(copies, ('blk', 'tower'), 0, 0)  10.6 us
    all_to_all x1, blocking collectives, ring_body(): grad_hidden = lax.all_to_all(grad_cols, 'blk', 0, 0)  10.2 us
    pallas_call x1, Pallas kernels, backward_call(): pl.pallas_call(functools.partial(backward_kernel, plan), grid=(row_count...  8.94 us
    ppermute x3, starting transfers between devices, along_ring(): return lax.ppermute(value, ('blk', 'tower'), routes)  8.06 us
    unnamed x74, local copies, waits for them, and re-layouts  7.27 us
    ppermute x14, waiting for transfers between devices, move(): return lax.ppermute(value, ('blk', 'tower'), found)  6.64 us
  transfers between devices with their start and end apart: 20, of which 8 were waited for; matrix products, arithmetic and copies ran while one was open for 6% of the time, Pallas kernels for 14%

profile of v4, /device:TPU:0, one launch (start us, length us, event | category | flops | bytes accessed | tf_op | source)
XLA Modules:
  0.0 118.1 jit_solution(18171882985334266596)
XLA Ops:
  1.2 3.0 %collective-permute-start.1 = (bf16[128,1152]{1,0:T(8,128)(2,1)S(1)}, bf16[128,1152]{1,0:T(8,128)(2,1)}, u32[]{:S(2)}, u32[]{:S(2)}) collective-permute-start(bf16[128,1152]{1,0:T(8,128)(2,1)S(1)} %select_bitcast_fusion.1.one.refs_8_), channel_id=1, source_target_pairs={{0,4},{1,5},{2,6},{3,7},{8,0},{9,1},{10,2},{11,3},{16,8},{17,9},{1... | collective-permute-start | bytes 884744 | tf_op jit(solution)/shard_map/ppermute | solution.py:54
  5.5 2.0 %collective-permute-start.3 = (bf16[144,1152]{1,0:T(8,128)(2,1)S(1)}, bf16[144,1152]{1,0:T(8,128)(2,1)}, u32[]{:S(2)}, u32[]{:S(2)}) collective-permute-start(bf16[144,1152]{1,0:T(8,128)(2,1)S(1)} %select_bitcast_fusion.two.refs_9_), channel_id=1, source_target_pairs={{0,4},{1,5},{2,6},{3,7},{8,0},{9,1},{10,2},{11,3},{16,8},{17,9},{1... | collective-permute-start | bytes 995336 | tf_op jit(solution)/shard_map/ppermute | solution.py:54
  13.1 2.0 %shard_map.82 = (bf16[512,384]{1,0:T(8,128)(2,1)S(1)}, f32[8,8,272]{2,1,0:T(8,128)S(1)}, f32[8,1152]{1,0:T(8,128)S(1)}) custom-call(s32[8]{0:T(128)S(1)} %compare_select_fusion.2.block_of, bf16[512,1152]{1,0:T(8,128)(2,1)S(1)} %copy-done, f32[8,1]{1,0:T(8,128)S(1)} %copy.39.share, bf16[8,512]{1,0:T(8,128)(2,1)S(1)} %select_convert_fusion.member, ...), custom_call_target="tpu_custom_call" | custom-call | flops 4000000000 | bytes 16000000 | tf_op jit(solution)/shard_map/pallas_call | solution.py:351
  15.8 1.9 %collective-permute-start.5 = (bf16[128,1152]{1,0:T(8,128)(2,1)}, bf16[128,1152]{1,0:T(8,128)(2,1)S(1)}, u32[]{:S(2)}, u32[]{:S(2)}) collective-permute-start(bf16[128,1152]{1,0:T(8,128)(2,1)} %collective-permute-done.1.two.refs_11_), channel_id=1, source_target_pairs={{0,4},{1,5},{2,6},{3,7},{8,0},{9,1},{10,2},{11,3},{16,8},{17,9},{1... | collective-permute-start | bytes 884744 | tf_op jit(solution)/shard_map/ppermute | solution.py:54
  17.9 1.9 %shard_map.83 = (bf16[512,256]{1,0:T(8,128)(2,1)S(1)}, f32[8,8,272]{2,1,0:T(8,128)S(1)}) custom-call(s32[8]{0:T(128)S(1)} %compare_select_fusion.2.block_of, f32[8,8,272]{2,1,0:T(8,128)S(1)} %get-tuple-element.24.before, f32[8,1]{1,0:T(8,128)S(1)} %copy.39.share, bf16[8,512]{1,0:T(8,128)(2,1)S(1)} %select_convert_fusion.member, ...), custom_call_target="tpu_custom_call" | custom-call | flops 4000000000 | bytes 16000000 | tf_op jit(solution)/shard_map/pallas_call | solution.py:351
  20.5 1.9 %collective-permute-start.7 = (bf16[144,1152]{1,0:T(8,128)(2,1)}, bf16[144,1152]{1,0:T(8,128)(2,1)S(1)}, u32[]{:S(2)}, u32[]{:S(2)}) collective-permute-start(bf16[144,1152]{1,0:T(8,128)(2,1)} %collective-permute-done.3.two.refs_13_), channel_id=1, source_target_pairs={{0,4},{1,5},{2,6},{3,7},{8,0},{9,1},{10,2},{11,3},{16,8},{17,9},{1... | collective-permute-start | bytes 995336 | tf_op jit(solution)/shard_map/ppermute | solution.py:54
  22.6 2.4 %shard_map.84 = (bf16[512,384]{1,0:T(8,128)(2,1)S(1)}, f32[8,8,272]{2,1,0:T(8,128)S(1)}) custom-call(s32[8]{0:T(128)S(1)} %compare_select_fusion.2.block_of, f32[8,8,272]{2,1,0:T(8,128)S(1)} %get-tuple-element.25.before, f32[8,1]{1,0:T(8,128)S(1)} %copy.39.share, bf16[8,512]{1,0:T(8,128)(2,1)S(1)} %select_convert_fusion.member, ...), custom_call_target="tpu_custom_call" | custom-call | flops 4000000000 | bytes 16000000 | tf_op jit(solution)/shard_map/pallas_call | solution.py:351
  26.0 1.9 %collective-permute-start.9 = (bf16[128,1152]{1,0:T(8,128)(2,1)S(1)}, bf16[128,1152]{1,0:T(8,128)(2,1)S(1)}, u32[]{:S(2)}, u32[]{:S(2)}) collective-permute-start(bf16[128,1152]{1,0:T(8,128)(2,1)S(1)} %collective-permute-done.5.two.refs_15_), channel_id=1, source_target_pairs={{0,4},{1,5},{2,6},{3,7},{8,0},{9,1},{10,2},{11,3},{16,8},{17,9},{1... | collective-permute-start | bytes 884744 | tf_op jit(solution)/shard_map/ppermute | solution.py:54
  30.8 2.3 %collective-permute-done.7.two.refs_17_ = bf16[144,1152]{1,0:T(8,128)(2,1)S(1)} collective-permute-done((bf16[144,1152]{1,0:T(8,128)(2,1)}, bf16[144,1152]{1,0:T(8,128)(2,1)S(1)}, u32[]{:S(2)}, u32[]{:S(2)}) %collective-permute-start.7) | collective-permute-done | bytes 331808 | tf_op jit(solution)/shard_map/ppermute | solution.py:54
  33.1 1.9 %collective-permute-start.11 = (bf16[144,1152]{1,0:T(8,128)(2,1)S(1)}, bf16[144,1152]{1,0:T(8,128)(2,1)}, u32[]{:S(2)}, u32[]{:S(2)}) collective-permute-start(bf16[144,1152]{1,0:T(8,128)(2,1)S(1)} %collective-permute-done.7.two.refs_17_), channel_id=1, source_target_pairs={{0,4},{1,5},{2,6},{3,7},{8,0},{9,1},{10,2},{11,3},{16,8},{17,9},{1... | collective-permute-start | bytes 995336 | tf_op jit(solution)/shard_map/ppermute | solution.py:54
  39.4 1.9 %collective-permute-done.8.one.refs_18_ = bf16[128,1152]{1,0:T(8,128)(2,1)S(1)} collective-permute-done((bf16[128,1152]{1,0:T(8,128)(2,1)S(1)}, bf16[128,1152]{1,0:T(8,128)(2,1)S(1)}, u32[]{:S(2)}, u32[]{:S(2)}) %collective-permute-start.8) | collective-permute-done | bytes 294944 | tf_op jit(solution)/shard_map/ppermute | solution.py:54
  41.3 2.0 %shard_map.87 = (bf16[512,256]{1,0:T(8,128)(2,1)S(1)}, f32[8,8,272]{2,1,0:T(8,128)}) custom-call(s32[8]{0:T(128)S(1)} %copy-done.31, f32[8,8,272]{2,1,0:T(8,128)S(1)} %get-tuple-element.28.before, f32[8,1]{1,0:T(8,128)S(1)} %copy.39.share, bf16[8,512]{1,0:T(8,128)(2,1)S(1)} %select_convert_fusion.member, f32[512,1]{1,0:T(8,128)S(1)} %select_n.177.mask, ...), custom_call_target="tpu_custom_call" | custom-call | flops 4000000000 | bytes 16000000 | tf_op jit(solution)/shard_map/pallas_call | solution.py:351
  43.4 4.9 %all-to-all-start = ((f32[8,8,272]{2,1,0:T(8,128)}), f32[8,8,272]{2,1,0:T(8,128)S(1)}, u32[]{:S(2)}, u32[]{:S(2)}) async-start(f32[8,8,272]{2,1,0:T(8,128)} %get-tuple-element.29), calls=%async_computation | async-start | bytes 196608 | tf_op jit(solution)/shard_map/all_to_all | solution.py:451
  48.3 2.0 %collective-permute-start.10 = (bf16[128,1152]{1,0:T(8,128)(2,1)S(1)}, bf16[128,1152]{1,0:T(8,128)(2,1)S(1)}, u32[]{:S(2)}, u32[]{:S(2)}) collective-permute-start(bf16[128,1152]{1,0:T(8,128)(2,1)S(1)} %collective-permute-done.8.one.refs_18_), channel_id=1, source_target_pairs={{0,8},{1,9},{2,10},{3,11},{8,16},{9,17},{10,18},{11,19},{16,24},{1... | collective-permute-start | bytes 884744 | tf_op jit(solution)/shard_map/ppermute | solution.py:54
  50.4 3.1 %shard_map.89 = (bf16[512,384]{1,0:T(8,128)(2,1)S(1)}, f32[8,144]{1,0:T(8,128)}, f32[8,144]{1,0:T(8,128)}) custom-call(f32[8,1]{1,0:T(8,128)S(1)} %copy.39.share, bf16[8,512]{1,0:T(8,128)(2,1)S(1)} %select_convert_fusion.member, f32[512,1]{1,0:T(8,128)S(1)} %select_n.177.mask, bf16[512,1152]{1,0:T(8,128)(2,1)S(1)} %fusion.4.normed, ...), custom_call_target="tpu_custom_call" | custom-call | flops 4000000000 | bytes 16000000 | tf_op jit(solution)/shard_map/pallas_call | solution.py:351
  53.4 3.8 %collective-permute-start.15 = (f32[8,144]{1,0:T(8,128)}, f32[8,144]{1,0:T(8,128)S(1)}, u32[]{:S(2)}, u32[]{:S(2)}) collective-permute-start(f32[8,144]{1,0:T(8,128)} %get-tuple-element.30), channel_id=1, source_target_pairs={{0,20},{1,21},{2,22},{3,23},{8,12},{9,13},{10,14},{11,15},{16,4},{... | collective-permute-start | bytes 13832 | tf_op jit(solution)/shard_map/ppermute | solution.py:459
  59.1 4.1 %collective-permute-start.13 = (f32[8,272]{1,0:T(8,128)S(1)}, f32[8,272]{1,0:T(8,128)S(1)}, u32[]{:S(2)}, u32[]{:S(2)}) collective-permute-start(f32[8,272]{1,0:T(8,128)S(1)} %shard_map.88), channel_id=1, source_target_pairs={{0,28},{1,29},{2,30},{3,31},{8,20},{9,21},{10,22},{11,23},{16,12},... | collective-permute-start | bytes 26120 | tf_op jit(solution)/shard_map/ppermute | solution.py:459
  63.7 1.9 %collective-permute-done.13.late = f32[8,272]{1,0:T(8,128)S(1)} collective-permute-done((f32[8,272]{1,0:T(8,128)S(1)}, f32[8,272]{1,0:T(8,128)S(1)}, u32[]{:S(2)}, u32[]{:S(2)}) %collective-permute-start.13) | collective-permute-done | bytes 8736 | tf_op jit(solution)/shard_map/ppermute | solution.py:459
  68.0 5.3 %all-to-all-start.1 = ((bf16[32,2,1152]{2,1,0:T(2,128)(2,1)}), bf16[32,2,1152]{2,1,0:T(2,128)(2,1)S(1)}, u32[]{:S(2)}, u32[]{:S(2)}) async-start(bf16[32,2,1152]{2,1,0:T(2,128)(2,1)} %shard_map.90.after), calls=%async_computation.1 | async-start | bytes 294912 | tf_op jit(solution)/shard_map/all_to_all | solution.py:473
  76.5 5.3 %all-to-all-done.1.back = bf16[32,2,1152]{2,1,0:T(2,128)(2,1)S(1)} async-done(((bf16[32,2,1152]{2,1,0:T(2,128)(2,1)}), bf16[32,2,1152]{2,1,0:T(2,128)(2,1)S(1)}, u32[]{:S(2)}, u32[]{:S(2)}) %all-to-all-start.1) | async-done | bytes 147488 | tf_op jit(solution)/shard_map/all_to_all | solution.py:473
  82.6 2.6 %all-to-all-start.2 = ((bf16[32,4,1280]{2,1,0:T(4,128)(2,1)}), bf16[32,4,1280]{2,1,0:T(4,128)(2,1)S(1)}, u32[]{:S(2)}, u32[]{:S(2)}) async-start(bf16[32,4,1280]{2,1,0:T(4,128)(2,1)} %shard_map.92), calls=%async_computation.2 | async-start | bytes 655360 | tf_op jit(solution)/shard_map/all_to_all | solution.py:509
  86.6 10.6 %all-to-all-done.2 = bf16[32,4,1280]{2,1,0:T(4,128)(2,1)S(1)} async-done(((bf16[32,4,1280]{2,1,0:T(4,128)(2,1)}), bf16[32,4,1280]{2,1,0:T(4,128)(2,1)S(1)}, u32[]{:S(2)}, u32[]{:S(2)}) %all-to-all-start.2) | async-done | bytes 327712 | tf_op jit(solution)/shard_map/all_to_all | solution.py:509
  98.9 10.2 %all_to_all.20.grad_hidden = f32[8,8,272]{2,1,0:T(8,128)} all-to-all(f32[8,8,272]{2,1,0:T(8,128)S(1)} %get-tuple-element.32), channel_id=1, replica_groups=mesh['blk'=8,'tower'=4] {'blk'}, dimensions={0} | all-to-all | bytes 139264 | tf_op jit(solution)/shard_map/all_to_all | solution.py:521
  109.1 8.9 %shard_map.94 = f32[512,1152]{1,0:T(8,128)} custom-call(s32[3]{0:T(128)} %copy-done.28, s32[8]{0:T(128)} %copy-done.29, f32[8,8,272]{2,1,0:T(8,128)} %all_to_all.20.grad_hidden, f32[8,1152]{1,0:T(8,128)} %copy-done.25, f32[1,1152]{1,0:T(1,128)} %get-tuple-element.42.gain, f32[512,1]{1,0:T(8,128)} %copy-done.5, bf16[512,1152]{1,0:T(8,128)(2,1)} %layer_input.3, ...), custom_call_target="tpu_custom_call" | custom-call | flops 2566914048 | bytes 12000000 | tf_op jit(solution)/shard_map/pallas_call | solution.py:234
  (137 shorter events, 28.6 us)
Async XLA Ops:
  1.2 14.6 %collective-permute-start.1 = (bf16[128,1152]{1,0:T(8,128)(2,1)S(1)}, bf16[128,1152]{1,0:T(8,128)(2,1)}, u32[]{:S(2)}, u32[]{:S(2)}) collective-permute-start(bf16[128,1152]{1,0:T(8,128)(2,1)S(1)} %select_bitcast_fusion.1.one.refs_8_), channel_id=1, source_target_pairs={{0,4},{1,5},{2,6},{3,7},{8,0},{9,1},{10,2},{11,3},{16,8},{17,9},{1... | collective-permute-start | bytes 884744 | tf_op jit(solution)/shard_map/ppermute | solution.py:54
  4.2 13.5 %collective-permute-start = (bf16[128,1152]{1,0:T(8,128)(2,1)S(1)}, bf16[128,1152]{1,0:T(8,128)(2,1)}, u32[]{:S(2)}, u32[]{:S(2)}) collective-permute-start(bf16[128,1152]{1,0:T(8,128)(2,1)S(1)} %select_bitcast_fusion.1.one.refs_8_), channel_id=1, source_target_pairs={{0,8},{1,9},{2,10},{3,11},{8,16},{9,17},{10,18},{11,19},{16,24},{1... | collective-permute-start | bytes 884744 | tf_op jit(solution)/shard_map/ppermute | solution.py:54
  5.5 15.1 %collective-permute-start.3 = (bf16[144,1152]{1,0:T(8,128)(2,1)S(1)}, bf16[144,1152]{1,0:T(8,128)(2,1)}, u32[]{:S(2)}, u32[]{:S(2)}) collective-permute-start(bf16[144,1152]{1,0:T(8,128)(2,1)S(1)} %select_bitcast_fusion.two.refs_9_), channel_id=1, source_target_pairs={{0,4},{1,5},{2,6},{3,7},{8,0},{9,1},{10,2},{11,3},{16,8},{17,9},{1... | collective-permute-start | bytes 995336 | tf_op jit(solution)/shard_map/ppermute | solution.py:54
  7.4 15.0 %collective-permute-start.2 = (bf16[144,1152]{1,0:T(8,128)(2,1)S(1)}, bf16[144,1152]{1,0:T(8,128)(2,1)}, u32[]{:S(2)}, u32[]{:S(2)}) collective-permute-start(bf16[144,1152]{1,0:T(8,128)(2,1)S(1)} %select_bitcast_fusion.two.refs_9_), channel_id=1, source_target_pairs={{0,8},{1,9},{2,10},{3,11},{8,16},{9,17},{10,18},{11,19},{16,24},{1... | collective-permute-start | bytes 995336 | tf_op jit(solution)/shard_map/ppermute | solution.py:54
  8.5 41.8 %copy-start.5 = (f32[512,1]{1,0:T(8,128)}, f32[512,1]{1,0:T(8,128)S(1)}, u32[]{:S(2)}) copy-start(f32[512,1]{1,0:T(8,128)S(1)} %select_n.177.mask) | copy-start | bytes 6148
  15.8 10.2 %collective-permute-start.5 = (bf16[128,1152]{1,0:T(8,128)(2,1)}, bf16[128,1152]{1,0:T(8,128)(2,1)S(1)}, u32[]{:S(2)}, u32[]{:S(2)}) collective-permute-start(bf16[128,1152]{1,0:T(8,128)(2,1)} %collective-permute-done.1.two.refs_11_), channel_id=1, source_target_pairs={{0,4},{1,5},{2,6},{3,7},{8,0},{9,1},{10,2},{11,3},{16,8},{17,9},{1... | collective-permute-start | bytes 884744 | tf_op jit(solution)/shard_map/ppermute | solution.py:54
  17.7 10.2 %collective-permute-start.4 = (bf16[128,1152]{1,0:T(8,128)(2,1)}, bf16[128,1152]{1,0:T(8,128)(2,1)S(1)}, u32[]{:S(2)}, u32[]{:S(2)}) collective-permute-start(bf16[128,1152]{1,0:T(8,128)(2,1)} %collective-permute-done.one.refs_10_), channel_id=1, source_target_pairs={{0,8},{1,9},{2,10},{3,11},{8,16},{9,17},{10,18},{11,19},{16,24},{1... | collective-permute-start | bytes 884744 | tf_op jit(solution)/shard_map/ppermute | solution.py:54
  20.5 12.6 %collective-permute-start.7 = (bf16[144,1152]{1,0:T(8,128)(2,1)}, bf16[144,1152]{1,0:T(8,128)(2,1)S(1)}, u32[]{:S(2)}, u32[]{:S(2)}) collective-permute-start(bf16[144,1152]{1,0:T(8,128)(2,1)} %collective-permute-done.3.two.refs_13_), channel_id=1, source_target_pairs={{0,4},{1,5},{2,6},{3,7},{8,0},{9,1},{10,2},{11,3},{16,8},{17,9},{1... | collective-permute-start | bytes 995336 | tf_op jit(solution)/shard_map/ppermute | solution.py:54
  22.4 12.6 %collective-permute-start.6 = (bf16[144,1152]{1,0:T(8,128)(2,1)}, bf16[144,1152]{1,0:T(8,128)(2,1)S(1)}, u32[]{:S(2)}, u32[]{:S(2)}) collective-permute-start(bf16[144,1152]{1,0:T(8,128)(2,1)} %collective-permute-done.2.one.refs_12_), channel_id=1, source_target_pairs={{0,8},{1,9},{2,10},{3,11},{8,16},{9,17},{10,18},{11,19},{16,24},{1... | collective-permute-start | bytes 995336 | tf_op jit(solution)/shard_map/ppermute | solution.py:54
  26.0 13.4 %collective-permute-start.9 = (bf16[128,1152]{1,0:T(8,128)(2,1)S(1)}, bf16[128,1152]{1,0:T(8,128)(2,1)S(1)}, u32[]{:S(2)}, u32[]{:S(2)}) collective-permute-start(bf16[128,1152]{1,0:T(8,128)(2,1)S(1)} %collective-permute-done.5.two.refs_15_), channel_id=1, source_target_pairs={{0,4},{1,5},{2,6},{3,7},{8,0},{9,1},{10,2},{11,3},{16,8},{17,9},{1... | collective-permute-start | bytes 884744 | tf_op jit(solution)/shard_map/ppermute | solution.py:54
  27.9 13.4 %collective-permute-start.8 = (bf16[128,1152]{1,0:T(8,128)(2,1)S(1)}, bf16[128,1152]{1,0:T(8,128)(2,1)S(1)}, u32[]{:S(2)}, u32[]{:S(2)}) collective-permute-start(bf16[128,1152]{1,0:T(8,128)(2,1)S(1)} %collective-permute-done.4.one.refs_14_), channel_id=1, source_target_pairs={{0,8},{1,9},{2,10},{3,11},{8,16},{9,17},{10,18},{11,19},{16,24},{1... | collective-permute-start | bytes 884744 | tf_op jit(solution)/shard_map/ppermute | solution.py:54
  33.1 17.2 %collective-permute-start.11 = (bf16[144,1152]{1,0:T(8,128)(2,1)S(1)}, bf16[144,1152]{1,0:T(8,128)(2,1)}, u32[]{:S(2)}, u32[]{:S(2)}) collective-permute-start(bf16[144,1152]{1,0:T(8,128)(2,1)S(1)} %collective-permute-done.7.two.refs_17_), channel_id=1, source_target_pairs={{0,4},{1,5},{2,6},{3,7},{8,0},{9,1},{10,2},{11,3},{16,8},{17,9},{1... | collective-permute-start | bytes 995336 | tf_op jit(solution)/shard_map/ppermute | solution.py:54
  35.0 15.3 %collective-permute-start.14 = (bf16[144,1152]{1,0:T(8,128)(2,1)S(1)}, bf16[144,1152]{1,0:T(8,128)(2,1)S(1)}, u32[]{:S(2)}, u32[]{:S(2)}) collective-permute-start(bf16[144,1152]{1,0:T(8,128)(2,1)S(1)} %collective-permute-done.6.one.refs_16_), channel_id=1, source_target_pairs={{0,8},{1,9},{2,10},{3,11},{8,16},{9,17},{10,18},{11,19},{16,24},{1... | collective-permute-start | bytes 995336 | tf_op jit(solution)/shard_map/ppermute | solution.py:54
  43.4 20.3 %all-to-all-start = ((f32[8,8,272]{2,1,0:T(8,128)}), f32[8,8,272]{2,1,0:T(8,128)S(1)}, u32[]{:S(2)}, u32[]{:S(2)}) async-start(f32[8,8,272]{2,1,0:T(8,128)} %get-tuple-element.29), calls=%async_computation | async-start | bytes 196608 | tf_op jit(solution)/shard_map/all_to_all | solution.py:451
  48.3 9.1 %collective-permute-start.10 = (bf16[128,1152]{1,0:T(8,128)(2,1)S(1)}, bf16[128,1152]{1,0:T(8,128)(2,1)S(1)}, u32[]{:S(2)}, u32[]{:S(2)}) collective-permute-start(bf16[128,1152]{1,0:T(8,128)(2,1)S(1)} %collective-permute-done.8.one.refs_18_), channel_id=1, source_target_pairs={{0,8},{1,9},{2,10},{3,11},{8,16},{9,17},{10,18},{11,19},{16,24},{1... | collective-permute-start | bytes 884744 | tf_op jit(solution)/shard_map/ppermute | solution.py:54
  50.3 7.7 %collective-permute-start.12 = (bf16[144,1152]{1,0:T(8,128)(2,1)}, bf16[144,1152]{1,0:T(8,128)(2,1)S(1)}, u32[]{:S(2)}, u32[]{:S(2)}) collective-permute-start(bf16[144,1152]{1,0:T(8,128)(2,1)} %collective-permute-done.11.two.refs_21_), channel_id=1, source_target_pairs={{0,4},{1,5},{2,6},{3,7},{8,0},{9,1},{10,2},{11,3},{16,8},{17,9},{1... | collective-permute-start | bytes 995336 | tf_op jit(solution)/shard_map/ppermute | solution.py:54
  53.4 10.2 %collective-permute-start.15 = (f32[8,144]{1,0:T(8,128)}, f32[8,144]{1,0:T(8,128)S(1)}, u32[]{:S(2)}, u32[]{:S(2)}) collective-permute-start(f32[8,144]{1,0:T(8,128)} %get-tuple-element.30), channel_id=1, source_target_pairs={{0,20},{1,21},{2,22},{3,23},{8,12},{9,13},{10,14},{11,15},{16,4},{... | collective-permute-start | bytes 13832 | tf_op jit(solution)/shard_map/ppermute | solution.py:459
  57.3 16.1 %copy-start.6 = (f32[512,1]{1,0:T(8,128)S(1)}, f32[512,1]{1,0:T(8,128)}, u32[]{:S(2)}) copy-start(f32[512,1]{1,0:T(8,128)} %copy-done.5) | copy-start | bytes 6148
  57.3 6.4 %collective-permute-start.16 = (f32[8,144]{1,0:T(8,128)}, f32[8,144]{1,0:T(8,128)S(1)}, u32[]{:S(2)}, u32[]{:S(2)}) collective-permute-start(f32[8,144]{1,0:T(8,128)} %get-tuple-element.31), channel_id=1, source_target_pairs={{0,24},{1,25},{2,26},{3,27},{8,28},{9,29},{10,30},{11,31},{16,20},... | collective-permute-start | bytes 13832 | tf_op jit(solution)/shard_map/ppermute | solution.py:459
  59.1 6.5 %collective-permute-start.13 = (f32[8,272]{1,0:T(8,128)S(1)}, f32[8,272]{1,0:T(8,128)S(1)}, u32[]{:S(2)}, u32[]{:S(2)}) collective-permute-start(f32[8,272]{1,0:T(8,128)S(1)} %shard_map.88), channel_id=1, source_target_pairs={{0,28},{1,29},{2,30},{3,31},{8,20},{9,21},{10,22},{11,23},{16,12},... | collective-permute-start | bytes 26120 | tf_op jit(solution)/shard_map/ppermute | solution.py:459
  63.3 34.0 %copy-start.28 = (s32[3]{0:T(128)}, s32[3]{0:T(128)S(1)}, u32[]{:S(2)}) copy-start(s32[3]{0:T(128)S(1)} %pad_add_fusion.flags) | copy-start | bytes 40
  68.0 13.8 %all-to-all-start.1 = ((bf16[32,2,1152]{2,1,0:T(2,128)(2,1)}), bf16[32,2,1152]{2,1,0:T(2,128)(2,1)S(1)}, u32[]{:S(2)}, u32[]{:S(2)}) async-start(bf16[32,2,1152]{2,1,0:T(2,128)(2,1)} %shard_map.90.after), calls=%async_computation.1 | async-start | bytes 294912 | tf_op jit(solution)/shard_map/all_to_all | solution.py:473
  76.5 32.7 %copy-start.2 = (bf16[512,384]{1,0:T(8,128)(2,1)}, bf16[512,384]{1,0:T(8,128)(2,1)S(1)}, u32[]{:S(2)}) copy-start(bf16[512,384]{1,0:T(8,128)(2,1)S(1)} %shard_map.91.refs_0_.refs_7_) | copy-start | bytes 1179652
  82.6 14.6 %all-to-all-start.2 = ((bf16[32,4,1280]{2,1,0:T(4,128)(2,1)}), bf16[32,4,1280]{2,1,0:T(4,128)(2,1)S(1)}, u32[]{:S(2)}, u32[]{:S(2)}) async-start(bf16[32,4,1280]{2,1,0:T(4,128)(2,1)} %shard_map.92), calls=%async_computation.2 | async-start | bytes 655360 | tf_op jit(solution)/shard_map/all_to_all | solution.py:509
  (33 other events, 163.8 us)

commit v5 on v2

--- a/solution.py
+++ b/solution.py
@@ -182,14 +182,11 @@
         lines = [grad_hidden[block_of[p], :, 2 * SMALL :] for p in rest]
         return scaled(slopes[g], 2 * SMALL, jnp.concatenate(lines, axis=1))
 
-    rests = [rest_part(g) for g in range(count) if plan[g][1]]
-    total = None
-    for g in range(0, count, 2):
-        left = jnp.concatenate([main_part(g), main_part(g + 1)], axis=1)
-        product = multiply(left, [ref[:SMALL] for ref in weight_refs[2 * g : 2 * g + 4]])
-        total = product if total is None else total + product
-    tails = [ref[SMALL:] for ref in weight_refs if ref.shape[0] > SMALL]
-    total = total + multiply(jnp.concatenate(rests, axis=1), tails)
+    left = [main_part(g) for g in range(count)]
+    left += [rest_part(g) for g in range(count) if plan[g][1]]
+    parts = [ref[:SMALL] for ref in weight_refs]
+    parts += [ref[SMALL:] for ref in weight_refs if ref.shape[0] > SMALL]
+    total = multiply(jnp.concatenate(left, axis=1), parts)
 
     values = layer_input[...].astype(jnp.float32)
     centered = values - jnp.mean(values, axis=-1, keepdims=True)

time: 119 us -> 119 us (level)
  no operation moved by 1% of the time
where the time goes in v5:
time: 119 us; the launch traced here: 118 us
  starting transfers between devices  33.5 us (28%)
  Pallas kernels  32.2 us (27%)
  waiting for transfers between devices  28.6 us (24%)
  blocking collectives  10.2 us (9%)
  local copies, waits for them, and re-layouts  6.2 us (5%)
  other arithmetic  5.89 us (5%)
  between operations  1.57 us (1%)
    pallas_call x12, Pallas kernels, small_call(): pl.pallas_call(kernel, in_specs=[scalar] * scalars + [whole] * (len(opera...  23.2 us
    ppermute x14, starting transfers between devices, move(): return lax.ppermute(value, ('blk', 'tower'), found)  15.3 us
    all_to_all x1, waiting for transfers between devices, ring_body(): packed = lax.all_to_all(copies, ('blk', 'tower'), 0, 0)  10.6 us
    ppermute x14, waiting for transfers between devices, move(): return lax.ppermute(value, ('blk', 'tower'), found)  10.5 us
    all_to_all x1, blocking collectives, ring_body(): grad_hidden = lax.all_to_all(grad_cols, 'blk', 0, 0)  10.2 us
    pallas_call x1, Pallas kernels, backward_call(): pl.pallas_call(functools.partial(backward_kernel, plan), grid=(row_count...  9.08 us
    all_to_all x1, waiting for transfers between devices, ring_body(): back = lax.all_to_all(partial, ('blk', 'tower'), 0, 0)  6.14 us
    all_to_all x1, starting transfers between devices, ring_body(): back = lax.all_to_all(partial, ('blk', 'tower'), 0, 0)  6 us
  transfers between devices with their start and end apart: 18, of which 9 were waited for; matrix products, arithmetic and copies ran while one was open for 5% of the time, Pallas kernels for 16%

profile of v5, /device:TPU:0, one launch (start us, length us, event | category | flops | bytes accessed | tf_op | source)
XLA Modules:
  0.0 118.1 jit_solution(9049068101312122166)
XLA Ops:
  1.2 3.0 %collective-permute-start.1 = (bf16[128,1152]{1,0:T(8,128)(2,1)S(1)}, bf16[128,1152]{1,0:T(8,128)(2,1)}, u32[]{:S(2)}, u32[]{:S(2)}) collective-permute-start(bf16[128,1152]{1,0:T(8,128)(2,1)S(1)} %select_bitcast_fusion.1.one.refs_8_), channel_id=1, source_target_pairs={{0,4},{1,5},{2,6},{3,7},{8,0},{9,1},{10,2},{11,3},{16,8},{17,9},{1... | collective-permute-start | bytes 884744 | tf_op jit(solution)/shard_map/ppermute | solution.py:54
  5.5 2.0 %collective-permute-start.3 = (bf16[144,1152]{1,0:T(8,128)(2,1)S(1)}, bf16[144,1152]{1,0:T(8,128)(2,1)}, u32[]{:S(2)}, u32[]{:S(2)}) collective-permute-start(bf16[144,1152]{1,0:T(8,128)(2,1)S(1)} %select_bitcast_fusion.two.refs_9_), channel_id=1, source_target_pairs={{0,4},{1,5},{2,6},{3,7},{8,0},{9,1},{10,2},{11,3},{16,8},{17,9},{1... | collective-permute-start | bytes 995336 | tf_op jit(solution)/shard_map/ppermute | solution.py:54
  11.6 2.0 %shard_map.82 = (bf16[512,384]{1,0:T(8,128)(2,1)S(1)}, f32[8,8,272]{2,1,0:T(8,128)S(1)}, f32[8,1152]{1,0:T(8,128)S(1)}) custom-call(s32[8]{0:T(128)S(1)} %compare_select_fusion.2.block_of, bf16[512,1152]{1,0:T(8,128)(2,1)S(1)} %copy-done, f32[8,1]{1,0:T(8,128)S(1)} %copy.39.share, bf16[8,512]{1,0:T(8,128)(2,1)S(1)} %select_convert_fusion.member, ...), custom_call_target="tpu_custom_call" | custom-call | flops 4000000000 | bytes 16000000 | tf_op jit(solution)/shard_map/pallas_call | solution.py:331
  14.3 1.9 %collective-permute-start.5 = (bf16[128,1152]{1,0:T(8,128)(2,1)}, bf16[128,1152]{1,0:T(8,128)(2,1)S(1)}, u32[]{:S(2)}, u32[]{:S(2)}) collective-permute-start(bf16[128,1152]{1,0:T(8,128)(2,1)} %collective-permute-done.1.two.refs_11_), channel_id=1, source_target_pairs={{0,4},{1,5},{2,6},{3,7},{8,0},{9,1},{10,2},{11,3},{16,8},{17,9},{1... | collective-permute-start | bytes 884744 | tf_op jit(solution)/shard_map/ppermute | solution.py:54
  16.3 1.9 %shard_map.83 = (bf16[512,256]{1,0:T(8,128)(2,1)S(1)}, f32[8,8,272]{2,1,0:T(8,128)S(1)}) custom-call(s32[8]{0:T(128)S(1)} %compare_select_fusion.2.block_of, f32[8,8,272]{2,1,0:T(8,128)S(1)} %get-tuple-element.23.before, f32[8,1]{1,0:T(8,128)S(1)} %copy.39.share, bf16[8,512]{1,0:T(8,128)(2,1)S(1)} %select_convert_fusion.member, ...), custom_call_target="tpu_custom_call" | custom-call | flops 4000000000 | bytes 16000000 | tf_op jit(solution)/shard_map/pallas_call | solution.py:331
  19.3 2.0 %collective-permute-start.7 = (bf16[144,1152]{1,0:T(8,128)(2,1)}, bf16[144,1152]{1,0:T(8,128)(2,1)S(1)}, u32[]{:S(2)}, u32[]{:S(2)}) collective-permute-start(bf16[144,1152]{1,0:T(8,128)(2,1)} %collective-permute-done.3.two.refs_13_), channel_id=1, source_target_pairs={{0,4},{1,5},{2,6},{3,7},{8,0},{9,1},{10,2},{11,3},{16,8},{17,9},{1... | collective-permute-start | bytes 995336 | tf_op jit(solution)/shard_map/ppermute | solution.py:54
  21.5 2.4 %shard_map.84 = (bf16[512,384]{1,0:T(8,128)(2,1)S(1)}, f32[8,8,272]{2,1,0:T(8,128)S(1)}) custom-call(s32[8]{0:T(128)S(1)} %compare_select_fusion.2.block_of, f32[8,8,272]{2,1,0:T(8,128)S(1)} %get-tuple-element.24.before, f32[8,1]{1,0:T(8,128)S(1)} %copy.39.share, bf16[8,512]{1,0:T(8,128)(2,1)S(1)} %select_convert_fusion.member, ...), custom_call_target="tpu_custom_call" | custom-call | flops 4000000000 | bytes 16000000 | tf_op jit(solution)/shard_map/pallas_call | solution.py:331
  25.5 2.0 %collective-permute-start.9 = (bf16[128,1152]{1,0:T(8,128)(2,1)S(1)}, bf16[128,1152]{1,0:T(8,128)(2,1)S(1)}, u32[]{:S(2)}, u32[]{:S(2)}) collective-permute-start(bf16[128,1152]{1,0:T(8,128)(2,1)S(1)} %collective-permute-done.5.two.refs_15_), channel_id=1, source_target_pairs={{0,4},{1,5},{2,6},{3,7},{8,0},{9,1},{10,2},{11,3},{16,8},{17,9},{1... | collective-permute-start | bytes 884744 | tf_op jit(solution)/shard_map/ppermute | solution.py:54
  29.8 2.8 %collective-permute-done.7.two.refs_17_ = bf16[144,1152]{1,0:T(8,128)(2,1)S(1)} collective-permute-done((bf16[144,1152]{1,0:T(8,128)(2,1)}, bf16[144,1152]{1,0:T(8,128)(2,1)S(1)}, u32[]{:S(2)}, u32[]{:S(2)}) %collective-permute-start.7) | collective-permute-done | bytes 331808 | tf_op jit(solution)/shard_map/ppermute | solution.py:54
  32.7 2.0 %collective-permute-start.11 = (bf16[144,1152]{1,0:T(8,128)(2,1)S(1)}, bf16[144,1152]{1,0:T(8,128)(2,1)}, u32[]{:S(2)}, u32[]{:S(2)}) collective-permute-start(bf16[144,1152]{1,0:T(8,128)(2,1)S(1)} %collective-permute-done.7.two.refs_17_), channel_id=1, source_target_pairs={{0,4},{1,5},{2,6},{3,7},{8,0},{9,1},{10,2},{11,3},{16,8},{17,9},{1... | collective-permute-start | bytes 995336 | tf_op jit(solution)/shard_map/ppermute | solution.py:54
  34.8 1.9 %shard_map.86 = (bf16[512,384]{1,0:T(8,128)(2,1)S(1)}, f32[8,8,272]{2,1,0:T(8,128)S(1)}) custom-call(s32[8]{0:T(128)S(1)} %compare_select_fusion.2.block_of, f32[8,8,272]{2,1,0:T(8,128)S(1)} %get-tuple-element.26.before, f32[8,1]{1,0:T(8,128)S(1)} %copy.39.share, bf16[8,512]{1,0:T(8,128)(2,1)S(1)} %select_convert_fusion.member, ...), custom_call_target="tpu_custom_call" | custom-call | flops 4000000000 | bytes 16000000 | tf_op jit(solution)/shard_map/pallas_call | solution.py:331
  37.4 3.7 %collective-permute-done.8.one.refs_18_ = bf16[128,1152]{1,0:T(8,128)(2,1)} collective-permute-done((bf16[128,1152]{1,0:T(8,128)(2,1)S(1)}, bf16[128,1152]{1,0:T(8,128)(2,1)}, u32[]{:S(2)}, u32[]{:S(2)}) %collective-permute-start.8) | collective-permute-done | bytes 294944 | tf_op jit(solution)/shard_map/ppermute | solution.py:54
  41.2 1.9 %shard_map.87 = (bf16[512,256]{1,0:T(8,128)(2,1)S(1)}, f32[8,8,272]{2,1,0:T(8,128)S(1)}) custom-call(s32[8]{0:T(128)S(1)} %compare_select_fusion.2.block_of, f32[8,8,272]{2,1,0:T(8,128)S(1)} %get-tuple-element.27.before, f32[8,1]{1,0:T(8,128)S(1)} %copy.39.share, bf16[8,512]{1,0:T(8,128)(2,1)S(1)} %select_convert_fusion.member, ...), custom_call_target="tpu_custom_call" | custom-call | flops 4000000000 | bytes 16000000 | tf_op jit(solution)/shard_map/pallas_call | solution.py:331
  48.1 3.1 %shard_map.88 = (bf16[512,384]{1,0:T(8,128)(2,1)S(1)}, f32[8,8,272]{2,1,0:T(8,128)}) custom-call(s32[8]{0:T(128)S(1)} %compare_select_fusion.2.block_of, f32[8,8,272]{2,1,0:T(8,128)S(1)} %get-tuple-element.28.before, f32[8,1]{1,0:T(8,128)S(1)} %copy.39.share, bf16[8,512]{1,0:T(8,128)(2,1)S(1)} %select_convert_fusion.member, f32[512,1]{1,0:T(8,128)S(1)} %select_n.177.mask, ...), custom_call_target="tpu_custom_call" | custom-call | flops 4000000000 | bytes 16000000 | tf_op jit(solution)/shard_map/pallas_call | solution.py:331
  52.0 4.9 %all-to-all-start = ((f32[8,8,272]{2,1,0:T(8,128)}), f32[8,8,272]{2,1,0:T(8,128)S(1)}, u32[]{:S(2)}, u32[]{:S(2)}) async-start(f32[8,8,272]{2,1,0:T(8,128)} %get-tuple-element.29), calls=%async_computation | async-start | bytes 196608 | tf_op jit(solution)/shard_map/all_to_all | solution.py:421
  56.9 2.2 %shard_map.89 = f32[8,272]{1,0:T(8,128)S(1)} custom-call(f32[8,1]{1,0:T(8,128)S(1)} %copy.39.share, bf16[8,512]{1,0:T(8,128)(2,1)S(1)} %select_convert_fusion.member, bf16[512,1152]{1,0:T(8,128)(2,1)S(1)} %fusion.4.normed, bf16[128,1152]{1,0:T(8,128)(2,1)} %collective-permute-done.12.one.refs_22_, bf16[144,1152]{1,0:T(8,128)(2,1)} %collective-permute-done.13.two.refs_23_), custom_call_target="tpu_custom_call" | custom-call | flops 4000000000 | bytes 16000000 | tf_op jit(solution)/shard_map/pallas_call | solution.py:331
  59.2 4.8 %collective-permute-start.14 = (f32[8,272]{1,0:T(8,128)S(1)}, f32[8,272]{1,0:T(8,128)S(1)}, u32[]{:S(2)}, u32[]{:S(2)}) collective-permute-start(f32[8,272]{1,0:T(8,128)S(1)} %shard_map.89), channel_id=1, source_target_pairs={{0,28},{1,29},{2,30},{3,31},{8,20},{9,21},{10,22},{11,23},{16,12},... | collective-permute-start | bytes 26120 | tf_op jit(solution)/shard_map/ppermute | solution.py:427
  67.2 6.0 %all-to-all-start.1 = ((bf16[32,2,1152]{2,1,0:T(2,128)(2,1)}), bf16[32,2,1152]{2,1,0:T(2,128)(2,1)S(1)}, u32[]{:S(2)}, u32[]{:S(2)}) async-start(bf16[32,2,1152]{2,1,0:T(2,128)(2,1)} %shard_map.90.after), calls=%async_computation.1 | async-start | bytes 294912 | tf_op jit(solution)/shard_map/all_to_all | solution.py:438
  73.3 2.2 %shard_map.91.refs_0_.refs_7_ = bf16[512,384]{1,0:T(8,128)(2,1)S(1)} custom-call(f32[512,1]{1,0:T(8,128)S(1)} %copy-done.6, bf16[512,1152]{1,0:T(8,128)(2,1)S(1)} %fusion.4.normed, bf16[128,1152]{1,0:T(8,128)(2,1)} %collective-permute-done.12.one.refs_22_, bf16[144,1152]{1,0:T(8,128)(2,1)} %collective-permute-done.13.two.refs_23_, ...), custom_call_target="tpu_custom_call" | custom-call | flops 1000000000 | bytes 4000000 | tf_op jit(solution)/shard_map/pallas_call | solution.py:331
  75.5 6.1 %all-to-all-done.1.back = bf16[32,2,1152]{2,1,0:T(2,128)(2,1)S(1)} async-done(((bf16[32,2,1152]{2,1,0:T(2,128)(2,1)}), bf16[32,2,1152]{2,1,0:T(2,128)(2,1)S(1)}, u32[]{:S(2)}, u32[]{:S(2)}) %all-to-all-start.1) | async-done | bytes 147488 | tf_op jit(solution)/shard_map/all_to_all | solution.py:438
  82.5 2.6 %all-to-all-start.2 = ((bf16[32,4,1280]{2,1,0:T(4,128)(2,1)}), bf16[32,4,1280]{2,1,0:T(4,128)(2,1)S(1)}, u32[]{:S(2)}, u32[]{:S(2)}) async-start(bf16[32,4,1280]{2,1,0:T(4,128)(2,1)} %shard_map.92), calls=%async_computation.2 | async-start | bytes 655360 | tf_op jit(solution)/shard_map/all_to_all | solution.py:474
  86.5 10.6 %all-to-all-done.2 = bf16[32,4,1280]{2,1,0:T(4,128)(2,1)S(1)} async-done(((bf16[32,4,1280]{2,1,0:T(4,128)(2,1)}), bf16[32,4,1280]{2,1,0:T(4,128)(2,1)S(1)}, u32[]{:S(2)}, u32[]{:S(2)}) %all-to-all-start.2) | async-done | bytes 327712 | tf_op jit(solution)/shard_map/all_to_all | solution.py:474
  98.9 10.2 %all_to_all.20.grad_hidden = f32[8,8,272]{2,1,0:T(8,128)} all-to-all(f32[8,8,272]{2,1,0:T(8,128)S(1)} %get-tuple-element.30), channel_id=1, replica_groups=mesh['blk'=8,'tower'=4] {'blk'}, dimensions={0} | all-to-all | bytes 139264 | tf_op jit(solution)/shard_map/all_to_all | solution.py:486
  109.1 9.1 %shard_map.94 = f32[512,1152]{1,0:T(8,128)} custom-call(s32[3]{0:T(128)} %copy-done.21, s32[8]{0:T(128)} %copy-done.22, f32[8,8,272]{2,1,0:T(8,128)} %all_to_all.20.grad_hidden, f32[8,1152]{1,0:T(8,128)} %copy-done.20, f32[1,1152]{1,0:T(1,128)} %get-tuple-element.40.gain, f32[512,1]{1,0:T(8,128)} %copy-done.5, bf16[512,1152]{1,0:T(8,128)(2,1)} %layer_input.3, ...), custom_call_target="tpu_custom_call" | custom-call | flops 2566914048 | bytes 12000000 | tf_op jit(solution)/shard_map/pallas_call | solution.py:218
  (107 shorter events, 25.3 us)
Async XLA Ops:
  0.0 10.5 %copy-start.23 = (f32[2,1152]{1,0:T(2,128)S(1)}, f32[2,1152]{1,0:T(2,128)}, u32[]{:S(2)}) copy-start(f32[2,1152]{1,0:T(2,128)} %param.11) | copy-start | bytes 27652
  1.2 13.1 %collective-permute-start.1 = (bf16[128,1152]{1,0:T(8,128)(2,1)S(1)}, bf16[128,1152]{1,0:T(8,128)(2,1)}, u32[]{:S(2)}, u32[]{:S(2)}) collective-permute-start(bf16[128,1152]{1,0:T(8,128)(2,1)S(1)} %select_bitcast_fusion.1.one.refs_8_), channel_id=1, source_target_pairs={{0,4},{1,5},{2,6},{3,7},{8,0},{9,1},{10,2},{11,3},{16,8},{17,9},{1... | collective-permute-start | bytes 884744 | tf_op jit(solution)/shard_map/ppermute | solution.py:54
  4.2 12.0 %collective-permute-start = (bf16[128,1152]{1,0:T(8,128)(2,1)S(1)}, bf16[128,1152]{1,0:T(8,128)(2,1)}, u32[]{:S(2)}, u32[]{:S(2)}) collective-permute-start(bf16[128,1152]{1,0:T(8,128)(2,1)S(1)} %select_bitcast_fusion.1.one.refs_8_), channel_id=1, source_target_pairs={{0,8},{1,9},{2,10},{3,11},{8,16},{9,17},{10,18},{11,19},{16,24},{1... | collective-permute-start | bytes 884744 | tf_op jit(solution)/shard_map/ppermute | solution.py:54
  5.5 13.9 %collective-permute-start.3 = (bf16[144,1152]{1,0:T(8,128)(2,1)S(1)}, bf16[144,1152]{1,0:T(8,128)(2,1)}, u32[]{:S(2)}, u32[]{:S(2)}) collective-permute-start(bf16[144,1152]{1,0:T(8,128)(2,1)S(1)} %select_bitcast_fusion.two.refs_9_), channel_id=1, source_target_pairs={{0,4},{1,5},{2,6},{3,7},{8,0},{9,1},{10,2},{11,3},{16,8},{17,9},{1... | collective-permute-start | bytes 995336 | tf_op jit(solution)/shard_map/ppermute | solution.py:54
  7.4 13.9 %collective-permute-start.2 = (bf16[144,1152]{1,0:T(8,128)(2,1)S(1)}, bf16[144,1152]{1,0:T(8,128)(2,1)}, u32[]{:S(2)}, u32[]{:S(2)}) collective-permute-start(bf16[144,1152]{1,0:T(8,128)(2,1)S(1)} %select_bitcast_fusion.two.refs_9_), channel_id=1, source_target_pairs={{0,8},{1,9},{2,10},{3,11},{8,16},{9,17},{10,18},{11,19},{16,24},{1... | collective-permute-start | bytes 995336 | tf_op jit(solution)/shard_map/ppermute | solution.py:54
  8.5 39.6 %copy-start.5 = (f32[512,1]{1,0:T(8,128)}, f32[512,1]{1,0:T(8,128)S(1)}, u32[]{:S(2)}) copy-start(f32[512,1]{1,0:T(8,128)S(1)} %select_n.177.mask) | copy-start | bytes 6148
  8.6 57.0 %copy-start.22 = (s32[8]{0:T(128)}, s32[8]{0:T(128)S(1)}, u32[]{:S(2)}) copy-start(s32[8]{0:T(128)S(1)} %compare_select_fusion.2.block_of) | copy-start | bytes 100
  14.3 11.3 %collective-permute-start.5 = (bf16[128,1152]{1,0:T(8,128)(2,1)}, bf16[128,1152]{1,0:T(8,128)(2,1)S(1)}, u32[]{:S(2)}, u32[]{:S(2)}) collective-permute-start(bf16[128,1152]{1,0:T(8,128)(2,1)} %collective-permute-done.1.two.refs_11_), channel_id=1, source_target_pairs={{0,4},{1,5},{2,6},{3,7},{8,0},{9,1},{10,2},{11,3},{16,8},{17,9},{1... | collective-permute-start | bytes 884744 | tf_op jit(solution)/shard_map/ppermute | solution.py:54
  16.2 11.4 %collective-permute-start.4 = (bf16[128,1152]{1,0:T(8,128)(2,1)}, bf16[128,1152]{1,0:T(8,128)(2,1)S(1)}, u32[]{:S(2)}, u32[]{:S(2)}) collective-permute-start(bf16[128,1152]{1,0:T(8,128)(2,1)} %collective-permute-done.one.refs_10_), channel_id=1, source_target_pairs={{0,8},{1,9},{2,10},{3,11},{8,16},{9,17},{10,18},{11,19},{16,24},{1... | collective-permute-start | bytes 884744 | tf_op jit(solution)/shard_map/ppermute | solution.py:54
  19.3 13.3 %collective-permute-start.7 = (bf16[144,1152]{1,0:T(8,128)(2,1)}, bf16[144,1152]{1,0:T(8,128)(2,1)S(1)}, u32[]{:S(2)}, u32[]{:S(2)}) collective-permute-start(bf16[144,1152]{1,0:T(8,128)(2,1)} %collective-permute-done.3.two.refs_13_), channel_id=1, source_target_pairs={{0,4},{1,5},{2,6},{3,7},{8,0},{9,1},{10,2},{11,3},{16,8},{17,9},{1... | collective-permute-start | bytes 995336 | tf_op jit(solution)/shard_map/ppermute | solution.py:54
  21.4 13.3 %collective-permute-start.6 = (bf16[144,1152]{1,0:T(8,128)(2,1)}, bf16[144,1152]{1,0:T(8,128)(2,1)S(1)}, u32[]{:S(2)}, u32[]{:S(2)}) collective-permute-start(bf16[144,1152]{1,0:T(8,128)(2,1)} %collective-permute-done.2.one.refs_12_), channel_id=1, source_target_pairs={{0,8},{1,9},{2,10},{3,11},{8,16},{9,17},{10,18},{11,19},{16,24},{1... | collective-permute-start | bytes 995336 | tf_op jit(solution)/shard_map/ppermute | solution.py:54
  25.5 15.7 %collective-permute-start.9 = (bf16[128,1152]{1,0:T(8,128)(2,1)S(1)}, bf16[128,1152]{1,0:T(8,128)(2,1)S(1)}, u32[]{:S(2)}, u32[]{:S(2)}) collective-permute-start(bf16[128,1152]{1,0:T(8,128)(2,1)S(1)} %collective-permute-done.5.two.refs_15_), channel_id=1, source_target_pairs={{0,4},{1,5},{2,6},{3,7},{8,0},{9,1},{10,2},{11,3},{16,8},{17,9},{1... | collective-permute-start | bytes 884744 | tf_op jit(solution)/shard_map/ppermute | solution.py:54
  27.6 13.5 %collective-permute-start.8 = (bf16[128,1152]{1,0:T(8,128)(2,1)S(1)}, bf16[128,1152]{1,0:T(8,128)(2,1)}, u32[]{:S(2)}, u32[]{:S(2)}) collective-permute-start(bf16[128,1152]{1,0:T(8,128)(2,1)S(1)} %collective-permute-done.4.one.refs_14_), channel_id=1, source_target_pairs={{0,8},{1,9},{2,10},{3,11},{8,16},{9,17},{10,18},{11,19},{16,24},{1... | collective-permute-start | bytes 884744 | tf_op jit(solution)/shard_map/ppermute | solution.py:54
  32.7 12.7 %collective-permute-start.11 = (bf16[144,1152]{1,0:T(8,128)(2,1)S(1)}, bf16[144,1152]{1,0:T(8,128)(2,1)}, u32[]{:S(2)}, u32[]{:S(2)}) collective-permute-start(bf16[144,1152]{1,0:T(8,128)(2,1)S(1)} %collective-permute-done.7.two.refs_17_), channel_id=1, source_target_pairs={{0,4},{1,5},{2,6},{3,7},{8,0},{9,1},{10,2},{11,3},{16,8},{17,9},{1... | collective-permute-start | bytes 995336 | tf_op jit(solution)/shard_map/ppermute | solution.py:54
  34.7 13.4 %collective-permute-start.10 = (bf16[144,1152]{1,0:T(8,128)(2,1)S(1)}, bf16[144,1152]{1,0:T(8,128)(2,1)S(1)}, u32[]{:S(2)}, u32[]{:S(2)}) collective-permute-start(bf16[144,1152]{1,0:T(8,128)(2,1)S(1)} %collective-permute-done.6.one.refs_16_), channel_id=1, source_target_pairs={{0,8},{1,9},{2,10},{3,11},{8,16},{9,17},{10,18},{11,19},{16,24},{1... | collective-permute-start | bytes 995336 | tf_op jit(solution)/shard_map/ppermute | solution.py:54
  41.1 15.8 %collective-permute-start.12 = (bf16[128,1152]{1,0:T(8,128)(2,1)}, bf16[128,1152]{1,0:T(8,128)(2,1)}, u32[]{:S(2)}, u32[]{:S(2)}) collective-permute-start(bf16[128,1152]{1,0:T(8,128)(2,1)} %collective-permute-done.8.one.refs_18_), channel_id=1, source_target_pairs={{0,8},{1,9},{2,10},{3,11},{8,16},{9,17},{10,18},{11,19},{16,24},{1... | collective-permute-start | bytes 884744 | tf_op jit(solution)/shard_map/ppermute | solution.py:54
  45.4 11.6 %collective-permute-start.13 = (bf16[144,1152]{1,0:T(8,128)(2,1)}, bf16[144,1152]{1,0:T(8,128)(2,1)}, u32[]{:S(2)}, u32[]{:S(2)}) collective-permute-start(bf16[144,1152]{1,0:T(8,128)(2,1)} %collective-permute-done.11.two.refs_21_), channel_id=1, source_target_pairs={{0,4},{1,5},{2,6},{3,7},{8,0},{9,1},{10,2},{11,3},{16,8},{17,9},{1... | collective-permute-start | bytes 995336 | tf_op jit(solution)/shard_map/ppermute | solution.py:54
  52.0 12.3 %all-to-all-start = ((f32[8,8,272]{2,1,0:T(8,128)}), f32[8,8,272]{2,1,0:T(8,128)S(1)}, u32[]{:S(2)}, u32[]{:S(2)}) async-start(f32[8,8,272]{2,1,0:T(8,128)} %get-tuple-element.29), calls=%async_computation | async-start | bytes 196608 | tf_op jit(solution)/shard_map/all_to_all | solution.py:421
  56.9 16.4 %copy-start.6 = (f32[512,1]{1,0:T(8,128)S(1)}, f32[512,1]{1,0:T(8,128)}, u32[]{:S(2)}) copy-start(f32[512,1]{1,0:T(8,128)} %copy-done.5) | copy-start | bytes 6148
  59.2 6.5 %collective-permute-start.14 = (f32[8,272]{1,0:T(8,128)S(1)}, f32[8,272]{1,0:T(8,128)S(1)}, u32[]{:S(2)}, u32[]{:S(2)}) collective-permute-start(f32[8,272]{1,0:T(8,128)S(1)} %shard_map.89), channel_id=1, source_target_pairs={{0,28},{1,29},{2,30},{3,31},{8,20},{9,21},{10,22},{11,23},{16,12},... | collective-permute-start | bytes 26120 | tf_op jit(solution)/shard_map/ppermute | solution.py:427
  64.0 33.2 %copy-start.21 = (s32[3]{0:T(128)}, s32[3]{0:T(128)S(1)}, u32[]{:S(2)}) copy-start(s32[3]{0:T(128)S(1)} %pad_add_fusion.flags) | copy-start | bytes 40
  67.2 14.4 %all-to-all-start.1 = ((bf16[32,2,1152]{2,1,0:T(2,128)(2,1)}), bf16[32,2,1152]{2,1,0:T(2,128)(2,1)S(1)}, u32[]{:S(2)}, u32[]{:S(2)}) async-start(bf16[32,2,1152]{2,1,0:T(2,128)(2,1)} %shard_map.90.after), calls=%async_computation.1 | async-start | bytes 294912 | tf_op jit(solution)/shard_map/all_to_all | solution.py:438
  75.5 33.5 %copy-start.2 = (bf16[512,384]{1,0:T(8,128)(2,1)}, bf16[512,384]{1,0:T(8,128)(2,1)S(1)}, u32[]{:S(2)}) copy-start(bf16[512,384]{1,0:T(8,128)(2,1)S(1)} %shard_map.91.refs_0_.refs_7_) | copy-start | bytes 1179652
  82.5 14.6 %all-to-all-start.2 = ((bf16[32,4,1280]{2,1,0:T(4,128)(2,1)}), bf16[32,4,1280]{2,1,0:T(4,128)(2,1)S(1)}, u32[]{:S(2)}, u32[]{:S(2)}) async-start(bf16[32,4,1280]{2,1,0:T(4,128)(2,1)} %shard_map.92), calls=%async_computation.2 | async-start | bytes 655360 | tf_op jit(solution)/shard_map/all_to_all | solution.py:474
  (18 other events, 66.1 us)

commit v6 on v2

--- a/solution.py
+++ b/solution.py
@@ -357,7 +357,7 @@
     shard = w_first.shape[2]
     gain = jnp.where(is_text, ln_gain[1], ln_gain[0])
     own = [
-        jnp.where(is_text, w_first[1, :, cut].T, w_first[0, :, cut].T)
+        lax.dynamic_index_in_dim(w_first[:, :, cut], is_text.astype(jnp.int32), 0, False).T
         for cut in (slice(0, SMALL), slice(SMALL, shard))
     ]
     flags = jnp.stack([is_text.astype(jnp.int32), tower_index * img_count, block_index])

time: 119 us -> 119 us (level)
  other arithmetic: 5.89 us -> 2.2 us
  waiting for transfers between devices: 28.6 us -> 30.9 us
  local copies, waits for them, and re-layouts: 6.2 us -> 7.52 us
    ppermute x14, waiting for transfers between devices: 10.5 us -> 12.9 us  [move(): return lax.ppermute(value, ('blk', 'tower'), found)]
    select_n x2 -> x0, other arithmetic: 2.3 us -> none  [ring_body(): jnp.where(is_text, w_first[1, :, cut].T, w_first[0, :, cut].T)]
    slice x0 -> x3, local copies, waits for them, and re-layouts: none -> 1.25 us  [ring_body(): w_first[:, :, cut]]
    unnamed x48 -> x52, local copies, waits for them, and re-layouts: 5.32 us -> 5.33 us
  transfers between devices with their start and end apart: 18 -> 18, of which waited for: 9 -> 10; matrix products, arithmetic and copies ran while one was open for 5% -> 3% of each run, Pallas kernels for 16% -> 16%
where the time goes in v6:
time: 119 us; the launch traced here: 118 us
  starting transfers between devices  33.6 us (28%)
  Pallas kernels  32.1 us (27%)
  waiting for transfers between devices  30.9 us (26%)
  blocking collectives  10.2 us (9%)
  local copies, waits for them, and re-layouts  7.52 us (6%)
  other arithmetic  2.2 us (2%)
  between operations  1.6 us (1%)
    pallas_call x12, Pallas kernels, small_call(): pl.pallas_call(kernel, in_specs=[scalar] * scalars + [whole] * (len(opera...  23.1 us
    ppermute x14, starting transfers between devices, move(): return lax.ppermute(value, ('blk', 'tower'), found)  15.4 us
    ppermute x14, waiting for transfers between devices, move(): return lax.ppermute(value, ('blk', 'tower'), found)  12.9 us
    all_to_all x1, waiting for transfers between devices, ring_body(): packed = lax.all_to_all(copies, ('blk', 'tower'), 0, 0)  10.6 us
    all_to_all x1, blocking collectives, ring_body(): grad_hidden = lax.all_to_all(grad_cols, 'blk', 0, 0)  10.2 us
    pallas_call x1, Pallas kernels, backward_call(): pl.pallas_call(functools.partial(backward_kernel, plan), grid=(row_count...  8.94 us
    all_to_all x1, waiting for transfers between devices, ring_body(): back = lax.all_to_all(partial, ('blk', 'tower'), 0, 0)  6.14 us
    all_to_all x1, starting transfers between devices, ring_body(): back = lax.all_to_all(partial, ('blk', 'tower'), 0, 0)  6 us
  transfers between devices with their start and end apart: 18, of which 10 were waited for; matrix products, arithmetic and copies ran while one was open for 3% of the time, Pallas kernels for 16%

profile of v6, /device:TPU:0, one launch (start us, length us, event | category | flops | bytes accessed | tf_op | source)
XLA Modules:
  0.0 118.2 jit_solution(13006029775684319587)
XLA Ops:
  1.3 3.0 %collective-permute-start.1 = (bf16[128,1152]{1,0:T(8,128)(2,1)S(1)}, bf16[128,1152]{1,0:T(8,128)(2,1)}, u32[]{:S(2)}, u32[]{:S(2)}) collective-permute-start(bf16[128,1152]{1,0:T(8,128)(2,1)S(1)} %dynamic-slice_bitcast_fusion.1.one.refs_8_), channel_id=1, source_target_pairs={{0,4},{1,5},{2,6},{3,7},{8,0},{9,1},{10,2},{11,3},{16,8},{17,9},{1... | collective-permute-start | bytes 884744 | tf_op jit(solution)/shard_map/ppermute | solution.py:54
  4.5 2.0 %collective-permute-start.3 = (bf16[144,1152]{1,0:T(8,128)(2,1)S(1)}, bf16[144,1152]{1,0:T(8,128)(2,1)}, u32[]{:S(2)}, u32[]{:S(2)}) collective-permute-start(bf16[144,1152]{1,0:T(8,128)(2,1)S(1)} %dynamic-slice_bitcast_fusion.two.refs_9_), channel_id=1, source_target_pairs={{0,4},{1,5},{2,6},{3,7},{8,0},{9,1},{10,2},{11,3},{16,8},{17,9},{1... | collective-permute-start | bytes 995336 | tf_op jit(solution)/shard_map/ppermute | solution.py:54
  9.2 2.0 %shard_map.82 = (bf16[512,384]{1,0:T(8,128)(2,1)S(1)}, f32[8,8,272]{2,1,0:T(8,128)S(1)}, f32[8,1152]{1,0:T(8,128)S(1)}) custom-call(s32[8]{0:T(128)S(1)} %compare_select_fusion.2.block_of, bf16[512,1152]{1,0:T(8,128)(2,1)S(1)} %copy-done, f32[8,1]{1,0:T(8,128)S(1)} %copy.39.share, bf16[8,512]{1,0:T(8,128)(2,1)S(1)} %select_convert_fusion.member, ...), custom_call_target="tpu_custom_call" | custom-call | flops 4000000000 | bytes 16000000 | tf_op jit(solution)/shard_map/pallas_call | solution.py:334
  12.4 2.0 %collective-permute-start.5 = (bf16[128,1152]{1,0:T(8,128)(2,1)}, bf16[128,1152]{1,0:T(8,128)(2,1)S(1)}, u32[]{:S(2)}, u32[]{:S(2)}) collective-permute-start(bf16[128,1152]{1,0:T(8,128)(2,1)} %collective-permute-done.1.two.refs_11_), channel_id=1, source_target_pairs={{0,4},{1,5},{2,6},{3,7},{8,0},{9,1},{10,2},{11,3},{16,8},{17,9},{1... | collective-permute-start | bytes 884744 | tf_op jit(solution)/shard_map/ppermute | solution.py:54
  14.5 1.9 %shard_map.83 = (bf16[512,256]{1,0:T(8,128)(2,1)S(1)}, f32[8,8,272]{2,1,0:T(8,128)S(1)}) custom-call(s32[8]{0:T(128)S(1)} %compare_select_fusion.2.block_of, f32[8,8,272]{2,1,0:T(8,128)S(1)} %get-tuple-element.23.before, f32[8,1]{1,0:T(8,128)S(1)} %copy.39.share, bf16[8,512]{1,0:T(8,128)(2,1)S(1)} %select_convert_fusion.member, ...), custom_call_target="tpu_custom_call" | custom-call | flops 4000000000 | bytes 16000000 | tf_op jit(solution)/shard_map/pallas_call | solution.py:334
  17.1 2.3 %collective-permute-done.3.two.refs_13_ = bf16[144,1152]{1,0:T(8,128)(2,1)} collective-permute-done((bf16[144,1152]{1,0:T(8,128)(2,1)S(1)}, bf16[144,1152]{1,0:T(8,128)(2,1)}, u32[]{:S(2)}, u32[]{:S(2)}) %collective-permute-start.3) | collective-permute-done | bytes 331808 | tf_op jit(solution)/shard_map/ppermute | solution.py:54
  19.5 2.0 %collective-permute-start.7 = (bf16[144,1152]{1,0:T(8,128)(2,1)}, bf16[144,1152]{1,0:T(8,128)(2,1)S(1)}, u32[]{:S(2)}, u32[]{:S(2)}) collective-permute-start(bf16[144,1152]{1,0:T(8,128)(2,1)} %collective-permute-done.3.two.refs_13_), channel_id=1, source_target_pairs={{0,4},{1,5},{2,6},{3,7},{8,0},{9,1},{10,2},{11,3},{16,8},{17,9},{1... | collective-permute-start | bytes 995336 | tf_op jit(solution)/shard_map/ppermute | solution.py:54
  21.6 2.4 %shard_map.84 = (bf16[512,384]{1,0:T(8,128)(2,1)S(1)}, f32[8,8,272]{2,1,0:T(8,128)S(1)}) custom-call(s32[8]{0:T(128)S(1)} %compare_select_fusion.2.block_of, f32[8,8,272]{2,1,0:T(8,128)S(1)} %get-tuple-element.24.before, f32[8,1]{1,0:T(8,128)S(1)} %copy.39.share, bf16[8,512]{1,0:T(8,128)(2,1)S(1)} %select_convert_fusion.member, ...), custom_call_target="tpu_custom_call" | custom-call | flops 4000000000 | bytes 16000000 | tf_op jit(solution)/shard_map/pallas_call | solution.py:334
  25.7 2.0 %collective-permute-start.9 = (bf16[128,1152]{1,0:T(8,128)(2,1)S(1)}, bf16[128,1152]{1,0:T(8,128)(2,1)S(1)}, u32[]{:S(2)}, u32[]{:S(2)}) collective-permute-start(bf16[128,1152]{1,0:T(8,128)(2,1)S(1)} %collective-permute-done.5.two.refs_15_), channel_id=1, source_target_pairs={{0,4},{1,5},{2,6},{3,7},{8,0},{9,1},{10,2},{11,3},{16,8},{17,9},{1... | collective-permute-start | bytes 884744 | tf_op jit(solution)/shard_map/ppermute | solution.py:54
  30.0 2.8 %collective-permute-done.7.two.refs_17_ = bf16[144,1152]{1,0:T(8,128)(2,1)S(1)} collective-permute-done((bf16[144,1152]{1,0:T(8,128)(2,1)}, bf16[144,1152]{1,0:T(8,128)(2,1)S(1)}, u32[]{:S(2)}, u32[]{:S(2)}) %collective-permute-start.7) | collective-permute-done | bytes 331808 | tf_op jit(solution)/shard_map/ppermute | solution.py:54
  32.8 2.0 %collective-permute-start.11 = (bf16[144,1152]{1,0:T(8,128)(2,1)S(1)}, bf16[144,1152]{1,0:T(8,128)(2,1)}, u32[]{:S(2)}, u32[]{:S(2)}) collective-permute-start(bf16[144,1152]{1,0:T(8,128)(2,1)S(1)} %collective-permute-done.7.two.refs_17_), channel_id=1, source_target_pairs={{0,4},{1,5},{2,6},{3,7},{8,0},{9,1},{10,2},{11,3},{16,8},{17,9},{1... | collective-permute-start | bytes 995336 | tf_op jit(solution)/shard_map/ppermute | solution.py:54
  37.6 3.7 %collective-permute-done.8.one.refs_18_ = bf16[128,1152]{1,0:T(8,128)(2,1)} collective-permute-done((bf16[128,1152]{1,0:T(8,128)(2,1)S(1)}, bf16[128,1152]{1,0:T(8,128)(2,1)}, u32[]{:S(2)}, u32[]{:S(2)}) %collective-permute-start.8) | collective-permute-done | bytes 294944 | tf_op jit(solution)/shard_map/ppermute | solution.py:54
  41.3 1.9 %shard_map.87 = (bf16[512,256]{1,0:T(8,128)(2,1)S(1)}, f32[8,8,272]{2,1,0:T(8,128)S(1)}) custom-call(s32[8]{0:T(128)S(1)} %compare_select_fusion.2.block_of, f32[8,8,272]{2,1,0:T(8,128)S(1)} %get-tuple-element.27.before, f32[8,1]{1,0:T(8,128)S(1)} %copy.39.share, bf16[8,512]{1,0:T(8,128)(2,1)S(1)} %select_convert_fusion.member, ...), custom_call_target="tpu_custom_call" | custom-call | flops 4000000000 | bytes 16000000 | tf_op jit(solution)/shard_map/pallas_call | solution.py:334
  48.3 3.1 %shard_map.88 = (bf16[512,384]{1,0:T(8,128)(2,1)S(1)}, f32[8,8,272]{2,1,0:T(8,128)}) custom-call(s32[8]{0:T(128)S(1)} %compare_select_fusion.2.block_of, f32[8,8,272]{2,1,0:T(8,128)S(1)} %get-tuple-element.28.before, f32[8,1]{1,0:T(8,128)S(1)} %copy.39.share, bf16[8,512]{1,0:T(8,128)(2,1)S(1)} %select_convert_fusion.member, f32[512,1]{1,0:T(8,128)S(1)} %select_n.152.mask, ...), custom_call_target="tpu_custom_call" | custom-call | flops 4000000000 | bytes 16000000 | tf_op jit(solution)/shard_map/pallas_call | solution.py:334
  52.2 4.9 %all-to-all-start = ((f32[8,8,272]{2,1,0:T(8,128)}), f32[8,8,272]{2,1,0:T(8,128)S(1)}, u32[]{:S(2)}, u32[]{:S(2)}) async-start(f32[8,8,272]{2,1,0:T(8,128)} %get-tuple-element.29), calls=%async_computation | async-start | bytes 196608 | tf_op jit(solution)/shard_map/all_to_all | solution.py:424
  57.1 2.2 %shard_map.89 = f32[8,272]{1,0:T(8,128)S(1)} custom-call(f32[8,1]{1,0:T(8,128)S(1)} %copy.39.share, bf16[8,512]{1,0:T(8,128)(2,1)S(1)} %select_convert_fusion.member, bf16[512,1152]{1,0:T(8,128)(2,1)S(1)} %fusion.4.normed, bf16[128,1152]{1,0:T(8,128)(2,1)} %collective-permute-done.12.one.refs_22_, bf16[144,1152]{1,0:T(8,128)(2,1)} %collective-permute-done.13.two.refs_23_), custom_call_target="tpu_custom_call" | custom-call | flops 4000000000 | bytes 16000000 | tf_op jit(solution)/shard_map/pallas_call | solution.py:334
  59.3 4.8 %collective-permute-start.14 = (f32[8,272]{1,0:T(8,128)S(1)}, f32[8,272]{1,0:T(8,128)S(1)}, u32[]{:S(2)}, u32[]{:S(2)}) collective-permute-start(f32[8,272]{1,0:T(8,128)S(1)} %shard_map.89), channel_id=1, source_target_pairs={{0,28},{1,29},{2,30},{3,31},{8,20},{9,21},{10,22},{11,23},{16,12},... | collective-permute-start | bytes 26120 | tf_op jit(solution)/shard_map/ppermute | solution.py:430
  67.4 6.0 %all-to-all-start.1 = ((bf16[32,2,1152]{2,1,0:T(2,128)(2,1)}), bf16[32,2,1152]{2,1,0:T(2,128)(2,1)S(1)}, u32[]{:S(2)}, u32[]{:S(2)}) async-start(bf16[32,2,1152]{2,1,0:T(2,128)(2,1)} %shard_map.90.after), calls=%async_computation.1 | async-start | bytes 294912 | tf_op jit(solution)/shard_map/all_to_all | solution.py:441
  73.5 2.2 %shard_map.91.refs_0_.refs_7_ = bf16[512,384]{1,0:T(8,128)(2,1)S(1)} custom-call(f32[512,1]{1,0:T(8,128)S(1)} %copy-done.6, bf16[512,1152]{1,0:T(8,128)(2,1)S(1)} %fusion.4.normed, bf16[128,1152]{1,0:T(8,128)(2,1)} %collective-permute-done.12.one.refs_22_, bf16[144,1152]{1,0:T(8,128)(2,1)} %collective-permute-done.13.two.refs_23_, ...), custom_call_target="tpu_custom_call" | custom-call | flops 1000000000 | bytes 4000000 | tf_op jit(solution)/shard_map/pallas_call | solution.py:334
  75.7 6.1 %all-to-all-done.1.back = bf16[32,2,1152]{2,1,0:T(2,128)(2,1)S(1)} async-done(((bf16[32,2,1152]{2,1,0:T(2,128)(2,1)}), bf16[32,2,1152]{2,1,0:T(2,128)(2,1)S(1)}, u32[]{:S(2)}, u32[]{:S(2)}) %all-to-all-start.1) | async-done | bytes 147488 | tf_op jit(solution)/shard_map/all_to_all | solution.py:441
  82.7 2.6 %all-to-all-start.2 = ((bf16[32,4,1280]{2,1,0:T(4,128)(2,1)}), bf16[32,4,1280]{2,1,0:T(4,128)(2,1)S(1)}, u32[]{:S(2)}, u32[]{:S(2)}) async-start(bf16[32,4,1280]{2,1,0:T(4,128)(2,1)} %shard_map.92), calls=%async_computation.2 | async-start | bytes 655360 | tf_op jit(solution)/shard_map/all_to_all | solution.py:477
  86.7 10.6 %all-to-all-done.2 = bf16[32,4,1280]{2,1,0:T(4,128)(2,1)S(1)} async-done(((bf16[32,4,1280]{2,1,0:T(4,128)(2,1)}), bf16[32,4,1280]{2,1,0:T(4,128)(2,1)S(1)}, u32[]{:S(2)}, u32[]{:S(2)}) %all-to-all-start.2) | async-done | bytes 327712 | tf_op jit(solution)/shard_map/all_to_all | solution.py:477
  99.0 10.2 %all_to_all.20.grad_hidden = f32[8,8,272]{2,1,0:T(8,128)} all-to-all(f32[8,8,272]{2,1,0:T(8,128)S(1)} %get-tuple-element.30), channel_id=1, replica_groups=mesh['blk'=8,'tower'=4] {'blk'}, dimensions={0} | all-to-all | bytes 139264 | tf_op jit(solution)/shard_map/all_to_all | solution.py:489
  109.2 8.9 %shard_map.94 = f32[512,1152]{1,0:T(8,128)} custom-call(s32[3]{0:T(128)} %copy-done.21, s32[8]{0:T(128)} %copy-done.22, f32[8,8,272]{2,1,0:T(8,128)} %all_to_all.20.grad_hidden, f32[8,1152]{1,0:T(8,128)} %copy-done.20, f32[1,1152]{1,0:T(1,128)} %get-tuple-element.40.gain, f32[512,1]{1,0:T(8,128)} %copy-done.5, bf16[512,1152]{1,0:T(8,128)(2,1)} %layer_input.3, ...), custom_call_target="tpu_custom_call" | custom-call | flops 2566914048 | bytes 12000000 | tf_op jit(solution)/shard_map/pallas_call | solution.py:221
  (114 shorter events, 24.8 us)
Async XLA Ops:
  1.3 11.0 %collective-permute-start.1 = (bf16[128,1152]{1,0:T(8,128)(2,1)S(1)}, bf16[128,1152]{1,0:T(8,128)(2,1)}, u32[]{:S(2)}, u32[]{:S(2)}) collective-permute-start(bf16[128,1152]{1,0:T(8,128)(2,1)S(1)} %dynamic-slice_bitcast_fusion.1.one.refs_8_), channel_id=1, source_target_pairs={{0,4},{1,5},{2,6},{3,7},{8,0},{9,1},{10,2},{11,3},{16,8},{17,9},{1... | collective-permute-start | bytes 884744 | tf_op jit(solution)/shard_map/ppermute | solution.py:54
  4.4 10.0 %collective-permute-start = (bf16[128,1152]{1,0:T(8,128)(2,1)S(1)}, bf16[128,1152]{1,0:T(8,128)(2,1)}, u32[]{:S(2)}, u32[]{:S(2)}) collective-permute-start(bf16[128,1152]{1,0:T(8,128)(2,1)S(1)} %dynamic-slice_bitcast_fusion.1.one.refs_8_), channel_id=1, source_target_pairs={{0,8},{1,9},{2,10},{3,11},{8,16},{9,17},{10,18},{11,19},{16,24},{1... | collective-permute-start | bytes 884744 | tf_op jit(solution)/shard_map/ppermute | solution.py:54
  4.5 14.9 %collective-permute-start.3 = (bf16[144,1152]{1,0:T(8,128)(2,1)S(1)}, bf16[144,1152]{1,0:T(8,128)(2,1)}, u32[]{:S(2)}, u32[]{:S(2)}) collective-permute-start(bf16[144,1152]{1,0:T(8,128)(2,1)S(1)} %dynamic-slice_bitcast_fusion.two.refs_9_), channel_id=1, source_target_pairs={{0,4},{1,5},{2,6},{3,7},{8,0},{9,1},{10,2},{11,3},{16,8},{17,9},{1... | collective-permute-start | bytes 995336 | tf_op jit(solution)/shard_map/ppermute | solution.py:54
  6.5 15.0 %collective-permute-start.2 = (bf16[144,1152]{1,0:T(8,128)(2,1)S(1)}, bf16[144,1152]{1,0:T(8,128)(2,1)}, u32[]{:S(2)}, u32[]{:S(2)}) collective-permute-start(bf16[144,1152]{1,0:T(8,128)(2,1)S(1)} %dynamic-slice_bitcast_fusion.two.refs_9_), channel_id=1, source_target_pairs={{0,8},{1,9},{2,10},{3,11},{8,16},{9,17},{10,18},{11,19},{16,24},{1... | collective-permute-start | bytes 995336 | tf_op jit(solution)/shard_map/ppermute | solution.py:54
  6.9 41.4 %copy-start.5 = (f32[512,1]{1,0:T(8,128)}, f32[512,1]{1,0:T(8,128)S(1)}, u32[]{:S(2)}) copy-start(f32[512,1]{1,0:T(8,128)S(1)} %select_n.152.mask) | copy-start | bytes 6148
  7.0 58.8 %copy-start.22 = (s32[8]{0:T(128)}, s32[8]{0:T(128)S(1)}, u32[]{:S(2)}) copy-start(s32[8]{0:T(128)S(1)} %compare_select_fusion.2.block_of) | copy-start | bytes 100
  12.4 13.3 %collective-permute-start.5 = (bf16[128,1152]{1,0:T(8,128)(2,1)}, bf16[128,1152]{1,0:T(8,128)(2,1)S(1)}, u32[]{:S(2)}, u32[]{:S(2)}) collective-permute-start(bf16[128,1152]{1,0:T(8,128)(2,1)} %collective-permute-done.1.two.refs_11_), channel_id=1, source_target_pairs={{0,4},{1,5},{2,6},{3,7},{8,0},{9,1},{10,2},{11,3},{16,8},{17,9},{1... | collective-permute-start | bytes 884744 | tf_op jit(solution)/shard_map/ppermute | solution.py:54
  14.4 13.3 %collective-permute-start.4 = (bf16[128,1152]{1,0:T(8,128)(2,1)}, bf16[128,1152]{1,0:T(8,128)(2,1)S(1)}, u32[]{:S(2)}, u32[]{:S(2)}) collective-permute-start(bf16[128,1152]{1,0:T(8,128)(2,1)} %collective-permute-done.one.refs_10_), channel_id=1, source_target_pairs={{0,8},{1,9},{2,10},{3,11},{8,16},{9,17},{10,18},{11,19},{16,24},{1... | collective-permute-start | bytes 884744 | tf_op jit(solution)/shard_map/ppermute | solution.py:54
  19.5 13.3 %collective-permute-start.7 = (bf16[144,1152]{1,0:T(8,128)(2,1)}, bf16[144,1152]{1,0:T(8,128)(2,1)S(1)}, u32[]{:S(2)}, u32[]{:S(2)}) collective-permute-start(bf16[144,1152]{1,0:T(8,128)(2,1)} %collective-permute-done.3.two.refs_13_), channel_id=1, source_target_pairs={{0,4},{1,5},{2,6},{3,7},{8,0},{9,1},{10,2},{11,3},{16,8},{17,9},{1... | collective-permute-start | bytes 995336 | tf_op jit(solution)/shard_map/ppermute | solution.py:54
  21.5 13.3 %collective-permute-start.6 = (bf16[144,1152]{1,0:T(8,128)(2,1)}, bf16[144,1152]{1,0:T(8,128)(2,1)S(1)}, u32[]{:S(2)}, u32[]{:S(2)}) collective-permute-start(bf16[144,1152]{1,0:T(8,128)(2,1)} %collective-permute-done.2.one.refs_12_), channel_id=1, source_target_pairs={{0,8},{1,9},{2,10},{3,11},{8,16},{9,17},{10,18},{11,19},{16,24},{1... | collective-permute-start | bytes 995336 | tf_op jit(solution)/shard_map/ppermute | solution.py:54
  25.7 15.7 %collective-permute-start.9 = (bf16[128,1152]{1,0:T(8,128)(2,1)S(1)}, bf16[128,1152]{1,0:T(8,128)(2,1)S(1)}, u32[]{:S(2)}, u32[]{:S(2)}) collective-permute-start(bf16[128,1152]{1,0:T(8,128)(2,1)S(1)} %collective-permute-done.5.two.refs_15_), channel_id=1, source_target_pairs={{0,4},{1,5},{2,6},{3,7},{8,0},{9,1},{10,2},{11,3},{16,8},{17,9},{1... | collective-permute-start | bytes 884744 | tf_op jit(solution)/shard_map/ppermute | solution.py:54
  27.7 13.5 %collective-permute-start.8 = (bf16[128,1152]{1,0:T(8,128)(2,1)S(1)}, bf16[128,1152]{1,0:T(8,128)(2,1)}, u32[]{:S(2)}, u32[]{:S(2)}) collective-permute-start(bf16[128,1152]{1,0:T(8,128)(2,1)S(1)} %collective-permute-done.4.one.refs_14_), channel_id=1, source_target_pairs={{0,8},{1,9},{2,10},{3,11},{8,16},{9,17},{10,18},{11,19},{16,24},{1... | collective-permute-start | bytes 884744 | tf_op jit(solution)/shard_map/ppermute | solution.py:54
  32.8 12.7 %collective-permute-start.11 = (bf16[144,1152]{1,0:T(8,128)(2,1)S(1)}, bf16[144,1152]{1,0:T(8,128)(2,1)}, u32[]{:S(2)}, u32[]{:S(2)}) collective-permute-start(bf16[144,1152]{1,0:T(8,128)(2,1)S(1)} %collective-permute-done.7.two.refs_17_), channel_id=1, source_target_pairs={{0,4},{1,5},{2,6},{3,7},{8,0},{9,1},{10,2},{11,3},{16,8},{17,9},{1... | collective-permute-start | bytes 995336 | tf_op jit(solution)/shard_map/ppermute | solution.py:54
  34.8 13.4 %collective-permute-start.10 = (bf16[144,1152]{1,0:T(8,128)(2,1)S(1)}, bf16[144,1152]{1,0:T(8,128)(2,1)S(1)}, u32[]{:S(2)}, u32[]{:S(2)}) collective-permute-start(bf16[144,1152]{1,0:T(8,128)(2,1)S(1)} %collective-permute-done.6.one.refs_16_), channel_id=1, source_target_pairs={{0,8},{1,9},{2,10},{3,11},{8,16},{9,17},{10,18},{11,19},{16,24},{1... | collective-permute-start | bytes 995336 | tf_op jit(solution)/shard_map/ppermute | solution.py:54
  41.3 15.8 %collective-permute-start.12 = (bf16[128,1152]{1,0:T(8,128)(2,1)}, bf16[128,1152]{1,0:T(8,128)(2,1)}, u32[]{:S(2)}, u32[]{:S(2)}) collective-permute-start(bf16[128,1152]{1,0:T(8,128)(2,1)} %collective-permute-done.8.one.refs_18_), channel_id=1, source_target_pairs={{0,8},{1,9},{2,10},{3,11},{8,16},{9,17},{10,18},{11,19},{16,24},{1... | collective-permute-start | bytes 884744 | tf_op jit(solution)/shard_map/ppermute | solution.py:54
  45.5 11.6 %collective-permute-start.13 = (bf16[144,1152]{1,0:T(8,128)(2,1)}, bf16[144,1152]{1,0:T(8,128)(2,1)}, u32[]{:S(2)}, u32[]{:S(2)}) collective-permute-start(bf16[144,1152]{1,0:T(8,128)(2,1)} %collective-permute-done.11.two.refs_21_), channel_id=1, source_target_pairs={{0,4},{1,5},{2,6},{3,7},{8,0},{9,1},{10,2},{11,3},{16,8},{17,9},{1... | collective-permute-start | bytes 995336 | tf_op jit(solution)/shard_map/ppermute | solution.py:54
  52.2 12.3 %all-to-all-start = ((f32[8,8,272]{2,1,0:T(8,128)}), f32[8,8,272]{2,1,0:T(8,128)S(1)}, u32[]{:S(2)}, u32[]{:S(2)}) async-start(f32[8,8,272]{2,1,0:T(8,128)} %get-tuple-element.29), calls=%async_computation | async-start | bytes 196608 | tf_op jit(solution)/shard_map/all_to_all | solution.py:424
  57.1 16.4 %copy-start.6 = (f32[512,1]{1,0:T(8,128)S(1)}, f32[512,1]{1,0:T(8,128)}, u32[]{:S(2)}) copy-start(f32[512,1]{1,0:T(8,128)} %copy-done.5) | copy-start | bytes 6148
  59.3 6.5 %collective-permute-start.14 = (f32[8,272]{1,0:T(8,128)S(1)}, f32[8,272]{1,0:T(8,128)S(1)}, u32[]{:S(2)}, u32[]{:S(2)}) collective-permute-start(f32[8,272]{1,0:T(8,128)S(1)} %shard_map.89), channel_id=1, source_target_pairs={{0,28},{1,29},{2,30},{3,31},{8,20},{9,21},{10,22},{11,23},{16,12},... | collective-permute-start | bytes 26120 | tf_op jit(solution)/shard_map/ppermute | solution.py:430
  64.2 33.2 %copy-start.21 = (s32[3]{0:T(128)}, s32[3]{0:T(128)S(1)}, u32[]{:S(2)}) copy-start(s32[3]{0:T(128)S(1)} %pad_add_fusion.flags) | copy-start | bytes 40
  67.4 14.4 %all-to-all-start.1 = ((bf16[32,2,1152]{2,1,0:T(2,128)(2,1)}), bf16[32,2,1152]{2,1,0:T(2,128)(2,1)S(1)}, u32[]{:S(2)}, u32[]{:S(2)}) async-start(bf16[32,2,1152]{2,1,0:T(2,128)(2,1)} %shard_map.90.after), calls=%async_computation.1 | async-start | bytes 294912 | tf_op jit(solution)/shard_map/all_to_all | solution.py:441
  75.7 33.5 %copy-start.2 = (bf16[512,384]{1,0:T(8,128)(2,1)}, bf16[512,384]{1,0:T(8,128)(2,1)S(1)}, u32[]{:S(2)}) copy-start(bf16[512,384]{1,0:T(8,128)(2,1)S(1)} %shard_map.91.refs_0_.refs_7_) | copy-start | bytes 1179652
  82.7 14.6 %all-to-all-start.2 = ((bf16[32,4,1280]{2,1,0:T(4,128)(2,1)}), bf16[32,4,1280]{2,1,0:T(4,128)(2,1)S(1)}, u32[]{:S(2)}, u32[]{:S(2)}) async-start(bf16[32,4,1280]{2,1,0:T(4,128)(2,1)} %shard_map.92), calls=%async_computation.2 | async-start | bytes 655360 | tf_op jit(solution)/shard_map/all_to_all | solution.py:477
  99.0 10.2 %copy-start.20 = (f32[8,1152]{1,0:T(8,128)}, f32[8,1152]{1,0:T(8,128)S(1)}, u32[]{:S(2)}) copy-start(f32[8,1152]{1,0:T(8,128)S(1)} %get-tuple-element.31.own_row) | copy-start | bytes 110596
  (21 other events, 74.7 us)
